TPU v7x, 512 devices: a whole 4x8x8 slice. The times are simulated.
512 devices in a mesh: grp: 4 (over x), ep: 128 (over z, y, core).
Axes of the slice: x: 4, y: 8, z: 8, core: 2. Of those that a mesh axis runs over, the one named last changes fastest.
Arguments:
- tokens: bfloat16 [65536, 1024], P(('grp', 'ep')), may hold values from -6 to 6
- routes: int32 [65536, 1], P(('grp', 'ep')), may hold values from 0 to 127; in each aligned block of 128 rows (0 to 127, 128 to 255, ...) at most 2 rows name the same one
- gate_prob: float32 [65536], P(('grp', 'ep')), may hold values from 0.1 to 1
- coef_weight: bfloat16 [1024], replicated, may hold values from -0.1875 to 0.1875
- exp_up: bfloat16 [128, 1024, 4096], P('ep', None, 'grp'), may hold values from -0.1875 to 0.1875
- exp_down: bfloat16 [128, 4096, 1024], P('ep', 'grp'), may hold values from -0.09375 to 0.09375
- res_up: bfloat16 [1024, 4096], P('ep', 'grp'), may hold values from -0.1875 to 0.1875
- res_down: bfloat16 [4096, 1024], P('grp', 'ep'), may hold values from -0.09375 to 0.09375
Outputs:
- mixed: bfloat16 [65536, 1024], P(('grp', 'ep'))
Inputs may be any that keep to these rules, and one draw needn't show every extreme that they name: `routes`: rows are taken in aligned blocks of 128, the rows of one device in the order grp then ep. In every block at most 2 rows name the same expert, and some block reaches 2.
All inputs are finite; a program needn't handle non-finite values.
Results may differ from a plain program's by a relative error of at most 0.015.
Values may be sent and summed in bfloat16 or wider, within the bound.
No kernel may reach another device: no remote copies, remote signals or barrier semaphores. Data moves between devices by JAX's collectives and lax.ppermute only.
A program may use at most 64 MiB of HBM per device.

v0:
```python
import jax
import jax.numpy as jnp
from jax import lax
from jax.sharding import PartitionSpec as P


def gelu_hidden(inputs, weight_in):
    product = jnp.dot(inputs, weight_in, preferred_element_type=jnp.float32)
    return jax.nn.gelu(product, approximate=True).astype(jnp.bfloat16)


def slot_table(route_row, expert_count, capacity):
    expert_ids = jnp.arange(expert_count, dtype=jnp.int32)
    onehot = (route_row[:, None] == expert_ids[None, :]).astype(jnp.int32)
    earlier = jnp.cumsum(onehot, axis=0, dtype=jnp.int32) - onehot
    position = jnp.sum(earlier * onehot, axis=1, dtype=jnp.int32)
    slot_index = route_row * capacity + position
    slot_ids = jnp.arange(expert_count * capacity, dtype=jnp.int32)
    return (slot_index[:, None] == slot_ids[None, :]).astype(jnp.bfloat16)


def local(tokens, routes, gate_prob, coef_weight, exp_up, exp_down, res_up, res_down):
    row_count, model_width = tokens.shape
    group_count = lax.axis_size("grp")
    expert_count = lax.axis_size("ep")
    capacity = 2 * row_count // expert_count
    up_quarter = exp_up[0]
    down_quarter = exp_down[0]
    res_up_all, res_down_all = (
        lax.all_gather(res_up, "ep", axis=0, tiled=True),
        lax.all_gather(res_down, "ep", axis=1, tiled=True),
    )
    whole_rows, whole_routes = (
        lax.all_gather(tokens, "grp", axis=0, tiled=True),
        lax.all_gather(routes, "grp", axis=0, tiled=True),
    )
    tables = jax.vmap(lambda route_row: slot_table(route_row, expert_count, capacity))(
        whole_routes.reshape(group_count, row_count)
    )
    grouped = whole_rows.reshape(group_count, row_count, model_width)
    outgoing = jnp.einsum("gtk,gtd->gkd", tables, grouped, preferred_element_type=jnp.float32)
    outgoing = outgoing.astype(jnp.bfloat16).reshape(
        group_count, expert_count, capacity, model_width
    )
    slot_rows = lax.all_to_all(outgoing, "ep", split_axis=1, concat_axis=1, tiled=True)
    flat_rows = slot_rows.reshape(-1, model_width)
    partial_value = jnp.dot(
        gelu_hidden(flat_rows, up_quarter), down_quarter, preferred_element_type=jnp.float32
    )
    returned = lax.all_to_all(
        partial_value.astype(jnp.bfloat16).reshape(slot_rows.shape),
        "ep",
        split_axis=1,
        concat_axis=1,
        tiled=True,
    )
    partial_value = jnp.dot(
        gelu_hidden(whole_rows, res_up_all), res_down_all, preferred_element_type=jnp.float32
    )
    partial_value = lax.optimization_barrier(partial_value.astype(jnp.bfloat16))
    res_out = lax.psum_scatter(
        partial_value.astype(jnp.float32).astype(jnp.bfloat16),
        "grp",
        scatter_dimension=0,
        tiled=True,
    ).astype(jnp.float32)
    expert_sum = lax.psum_scatter(
        returned.astype(jnp.float32).astype(jnp.bfloat16), "grp", scatter_dimension=0, tiled=True
    )
    own_table = lax.dynamic_index_in_dim(tables, lax.axis_index("grp"), 0, keepdims=False)
    expert_slots = expert_sum.reshape(expert_count * capacity, model_width)
    expert_out = jnp.dot(own_table, expert_slots, preferred_element_type=jnp.float32)
    coef = jax.nn.sigmoid(jnp.dot(tokens, coef_weight, preferred_element_type=jnp.float32))
    mixed = coef[:, None] * res_out + (1.0 - coef[:, None]) * gate_prob[:, None] * expert_out
    return mixed.astype(jnp.bfloat16)


def solution(mesh):
    in_specs = (
        P(("grp", "ep"), None),
        P(("grp", "ep"), None),
        P(("grp", "ep")),
        P(),
        P("ep", None, "grp"),
        P("ep", "grp", None),
        P("ep", "grp"),
        P("grp", "ep"),
    )
    out_specs = P(("grp", "ep"), None)
    return jax.shard_map(local, mesh=mesh, in_specs=in_specs, out_specs=out_specs, check_vma=False)
```

profile of v0, /device:TPU:1, one launch (start us, length us, event | category | flops | bytes accessed | tf_op | source)
XLA Modules:
  0.0 339.2 jit_solution(1743983926027102604)
XLA Ops:
  7.4 0.0 copy-start
  7.4 0.0 all-gather.4.cloned.1.call-start
  7.4 0.7 all-gather.4.cloned.1.call-update
  8.1 8.6 %all_gather.15 = s32[512,1]{0,1:T(1,128)S(1)} all-gather(s32[128,1]{0,1:T(1,128)} %param.9), channel_id=1, replica_groups=mesh['grp'=4,'ep'=128] {'grp'}, dimensions={0}, use_global_device_ids=true | all-gather | bytes 2560 | tf_op jit(solution)/shard_map/all_gather | solution.py:35
  16.7 0.1 fusion.45
  16.9 0.3 reduce_window_sum.11
  17.1 0.2 select_reduce_fusion
  17.4 26.8 %all-gather.4.cloned.1.call-done = bf16[512,1024]{1,0:T(8,128)(2,1)} async-done(((bf16[128,1024]{1,0:T(8,128)(2,1)}), bf16[512,1024]{1,0:T(8,128)(2,1)}) %all-gather.4.cloned.1.call-update) | async-done | bytes 1048592 | tf_op jit(solution)/shard_map/all_gather | solution.py:34
  44.2 3.2 convolution_convert_fusion
  47.4 4.1 %reshape.33 = bf16[4,128,2,1024]{3,2,1,0:T(2,128)(2,1)} reshape(bf16[4,256,1024]{2,1,0:T(8,128)(2,1)} %convolution_convert_fusion) | data formatting | bytes 4194304 | tf_op jit(solution)/shard_map/reshape | solution.py:42
  51.5 5.3 %copy.12 = bf16[4,128,2,1024]{3,2,0,1:T(2,128)(2,1)} copy(bf16[4,128,2,1024]{3,2,1,0:T(2,128)(2,1)} %reshape.33) | data formatting | bytes 4194304 | tf_op jit(solution)/shard_map/reshape | solution.py:42
  56.9 15.7 %all-to-all-start = ((bf16[4,128,2,1024]{3,2,0,1:T(2,128)(2,1)}), bf16[4,128,2,1024]{3,2,0,1:T(2,128)(2,1)}, u32[]{:S(2)}, u32[]{:S(2)}) async-start(bf16[4,128,2,1024]{3,2,0,1:T(2,128)(2,1)} %copy.12), calls=%async_computation.1 | async-start | bytes 4194304 | tf_op jit(solution)/shard_map/all_to_all | solution.py:45
  72.5 0.2 all-gather.6.cloned.1.call-start
  72.7 0.3 all-gather.6.cloned.1.call-update
  73.1 50.6 %all-to-all-done = bf16[4,128,2,1024]{3,2,0,1:T(2,128)(2,1)} async-done(((bf16[4,128,2,1024]{3,2,0,1:T(2,128)(2,1)}), bf16[4,128,2,1024]{3,2,0,1:T(2,128)(2,1)}, u32[]{:S(2)}, u32[]{:S(2)}) %all-to-all-start) | async-done | bytes 2097184 | tf_op jit(solution)/shard_map/all_to_all | solution.py:45
  123.6 4.4 %copy.13 = bf16[4,128,2,1024]{3,2,1,0:T(2,128)(2,1)} copy(bf16[4,128,2,1024]{3,2,0,1:T(2,128)(2,1)} %all-to-all-done) | data formatting | bytes 4194304 | tf_op jit(solution)/shard_map/all_to_all | solution.py:45
  128.0 4.1 %reshape.34 = bf16[1024,1024]{1,0:T(8,128)(2,1)} reshape(bf16[4,128,2,1024]{3,2,1,0:T(2,128)(2,1)} %copy.13) | data formatting | bytes 4194304 | tf_op jit(solution)/shard_map/reshape | solution.py:46
  132.1 0.0 copy-done
  132.1 8.1 %fusion.25 = bf16[1024,1024]{1,0:T(8,128)(2,1)} fusion(bf16[1,1024,1024]{2,1,0:T(8,128)(2,1)S(1)} %copy-done, bf16[1024,1024]{1,0:T(8,128)(2,1)} %reshape.34, bf16[1,1024,1024]{2,1,0:T(8,128)(2,1)} %param.12), kind=kOutput, calls=%fused_computation.26 | convolution fusion | flops 4305453056 | bytes 8388608 | tf_op jit(solution)/shard_map/dot_general | solution.py:47
  140.2 4.1 %reshape.35 = bf16[4,128,2,1024]{3,2,1,0:T(2,128)(2,1)} reshape(bf16[1024,1024]{1,0:T(8,128)(2,1)} %fusion.25) | data formatting | bytes 4194304 | tf_op jit(solution)/shard_map/reshape | solution.py:51
  144.4 5.3 %copy.14 = bf16[4,128,2,1024]{3,2,0,1:T(2,128)(2,1)} copy(bf16[4,128,2,1024]{3,2,1,0:T(2,128)(2,1)} %reshape.35) | data formatting | bytes 4194304 | tf_op jit(solution)/shard_map/reshape | solution.py:51
  149.7 9.4 %all-to-all-start.1 = ((bf16[4,128,2,1024]{3,2,0,1:T(2,128)(2,1)}), bf16[4,128,2,1024]{3,2,0,1:T(2,128)(2,1)}, u32[]{:S(2)}, u32[]{:S(2)}) async-start(bf16[4,128,2,1024]{3,2,0,1:T(2,128)(2,1)} %copy.14), calls=%async_computation.2 | async-start | bytes 4194304 | tf_op jit(solution)/shard_map/all_to_all | solution.py:50
  159.1 0.0 all-gather.8.cloned.1.call-start
  159.1 0.5 all-gather.8.cloned.1.call-update
  159.6 0.0 reduce-scatter.5.cloned.1.call-start
  159.7 52.9 %all-to-all-done.1 = bf16[4,128,2,1024]{3,2,0,1:T(2,128)(2,1)} async-done(((bf16[4,128,2,1024]{3,2,0,1:T(2,128)(2,1)}), bf16[4,128,2,1024]{3,2,0,1:T(2,128)(2,1)}, u32[]{:S(2)}, u32[]{:S(2)}) %all-to-all-start.1) | async-done | bytes 2097184 | tf_op jit(solution)/shard_map/all_to_all | solution.py:50
  212.6 4.1 %copy.15 = bf16[4,128,2,1024]{3,1,2,0:T(8,128)(2,1)} copy(bf16[4,128,2,1024]{3,2,0,1:T(2,128)(2,1)} %all-to-all-done.1) | data formatting | bytes 4194304 | tf_op jit(solution)/shard_map/all_to_all | solution.py:50
  216.7 0.0 copy-start.2
  216.7 0.0 reduce-scatter.5.cloned.1.call-update
  216.7 0.0 copy-start.3
  216.7 0.0 copy-start.1
  216.7 0.0 copy-start.4
  216.7 0.3 reduce-scatter.3.cloned.1.call-start
  217.0 0.0 all-gather.6.cloned.1.call-done
  217.1 83.2 %all-gather.8.cloned.1.call-done = bf16[1024,1024]{0,1:T(8,128)(2,1)} async-done(((bf16[1024,8]{0,1:T(8,128)(2,1)}), bf16[1024,1024]{0,1:T(8,128)(2,1)}) %all-gather.8.cloned.1.call-update) | async-done | bytes 2097168 | tf_op jit(solution)/shard_map/all_gather | solution.py:31
  300.2 0.0 copy-done.2
  300.3 5.6 %convolution_convert_fusion.1 = bf16[512,1024]{1,0:T(8,128)(2,1)} fusion(bf16[1024,1024]{0,1:T(8,128)(2,1)} %all-gather.8.cloned.1.call-done, bf16[512,1024]{1,0:T(8,128)(2,1)S(1)} %copy-done.2, bf16[1024,1024]{1,0:T(8,128)(2,1)} %all-gather.6.cloned.1.call-done), kind=kOutput, calls=%fused_computation.28 | convolution fusion | flops 2152726528 | bytes 6291456 | tf_op jit(solution)/shard_map/dot_general | solution.py:57
  305.9 0.0 reduce-scatter.3.cloned.1.call-update
  305.9 0.0 copy-done.3
  305.9 0.1 iota_compare_fusion
  306.0 0.0 copy-done.1
  306.0 0.0 copy-done.4
  306.0 0.2 subtract_multiply_fusion
  306.2 0.0 reduce-scatter.5.cloned.1.call-done
  306.2 1.6 copy.16
  307.8 0.2 reshape.36
  308.0 22.1 %reduce-scatter.3.cloned.1.call-done = bf16[128,1024]{1,0:T(8,128)(2,1)} async-done(((bf16[512,1024]{1,0:T(8,128)(2,1)}), bf16[128,1024]{1,0:T(8,128)(2,1)}) %reduce-scatter.3.cloned.1.call-update) | async-done | bytes 262160 | tf_op jit(solution)/shard_map/reduce_scatter | solution.py:61
  330.1 1.9 fusion.31
  (2 shorter events, 0.0 us)
Async XLA Ops:
  7.4 124.7 %copy-start = (bf16[1,1024,1024]{2,1,0:T(8,128)(2,1)S(1)}, bf16[1,1024,1024]{2,1,0:T(8,128)(2,1)}, u32[]{:S(2)}) copy-start(bf16[1,1024,1024]{2,1,0:T(8,128)(2,1)} %param.13) | copy-start | bytes 6291460
  7.4 36.8 %all-gather.4.cloned.1.call-start = ((), (), s32[]{:S(2)}) async-start(), calls=%async_computation.4 | async-start | bytes 1310720 | tf_op jit(solution)/shard_map/all_gather | solution.py:34
  56.9 66.8 %all-to-all-start = ((bf16[4,128,2,1024]{3,2,0,1:T(2,128)(2,1)}), bf16[4,128,2,1024]{3,2,0,1:T(2,128)(2,1)}, u32[]{:S(2)}, u32[]{:S(2)}) async-start(bf16[4,128,2,1024]{3,2,0,1:T(2,128)(2,1)} %copy.12), calls=%async_computation.1 | async-start | bytes 4194304 | tf_op jit(solution)/shard_map/all_to_all | solution.py:45
  72.5 144.5 %all-gather.6.cloned.1.call-start = ((), (), s32[]{:S(2)}) async-start(), calls=%async_computation.5 | async-start | bytes 2113536 | tf_op jit(solution)/shard_map/all_gather | solution.py:30
  149.7 63.0 %all-to-all-start.1 = ((bf16[4,128,2,1024]{3,2,0,1:T(2,128)(2,1)}), bf16[4,128,2,1024]{3,2,0,1:T(2,128)(2,1)}, u32[]{:S(2)}, u32[]{:S(2)}) async-start(bf16[4,128,2,1024]{3,2,0,1:T(2,128)(2,1)} %copy.14), calls=%async_computation.2 | async-start | bytes 4194304 | tf_op jit(solution)/shard_map/all_to_all | solution.py:50
  159.1 141.2 %all-gather.8.cloned.1.call-start = ((), (), s32[]{:S(2)}) async-start(), calls=%async_computation.6 | async-start | bytes 2113536 | tf_op jit(solution)/shard_map/all_gather | solution.py:31
  159.6 146.6 %reduce-scatter.5.cloned.1.call-start = ((), (), s32[]{:S(2)}) async-start(), calls=%async_computation.8 | async-start | bytes 2621440 | tf_op jit(solution)/shard_map/reduce_scatter | solution.py:67
  216.7 83.6 %copy-start.2 = (bf16[512,1024]{1,0:T(8,128)(2,1)S(1)}, bf16[512,1024]{1,0:T(8,128)(2,1)}, u32[]{:S(2)}) copy-start(bf16[512,1024]{1,0:T(8,128)(2,1)} %all-gather.4.cloned.1.call-done) | copy-start | bytes 3145732
  216.7 89.2 %copy-start.3 = (bf16[1024]{0:T(1024)(128)(2,1)S(1)}, bf16[1024]{0:T(1024)(128)(2,1)}, u32[]{:S(2)}) copy-start(bf16[1024]{0:T(1024)(128)(2,1)} %param.11) | copy-start | bytes 6148
  216.7 89.3 %copy-start.1 = (bf16[128,1024]{1,0:T(8,128)(2,1)S(1)}, bf16[128,1024]{1,0:T(8,128)(2,1)}, u32[]{:S(2)}) copy-start(bf16[128,1024]{1,0:T(8,128)(2,1)} %param.8) | copy-start | bytes 786436
  216.7 89.3 %copy-start.4 = (f32[128]{0:T(128)S(1)}, f32[128]{0:T(128)}, u32[]{:S(2)}) copy-start(f32[128]{0:T(128)} %param.10) | copy-start | bytes 1540
  216.7 113.4 %reduce-scatter.3.cloned.1.call-start = ((), (), s32[]{:S(2)}) async-start(), calls=%async_computation.7 | async-start | bytes 1310720 | tf_op jit(solution)/shard_map/reduce_scatter | solution.py:61
Sparse Core Ops, SparseCore 0:
  10.3 33.8 all-gather.3
  216.8 30.2 reduce-scatter.4
  306.0 24.0 reduce-scatter.2
Sparse Core Ops, SparseCore 1:
  76.6 133.8 all-gather.5
  213.9 86.3 all-gather.7
where the time goes:
time: 340 us; the launch traced here: 339 us
  waiting for transfers between devices  237 us (70%)
  local copies, waits for them, and re-layouts  33.2 us (10%)
  starting transfers between devices  25.6 us (8%)
  matrix products  19.1 us (6%)
  between operations  14.7 us (4%)
  blocking collectives  8.65 us (3%)
    all_gather x1, waiting for transfers between devices, local(): lax.all_gather(res_down, 'ep', axis=1, tiled=True)  83.2 us
    all_to_all x1, waiting for transfers between devices, local(): lax.all_to_all(partial_value.astype(jnp.bfloat16).reshape(slot_rows.shape...  52.9 us
    all_to_all x1, waiting for transfers between devices, local(): lax.all_to_all(outgoing, 'ep', split_axis=1, concat_axis=1, tiled=True)  50.6 us
    all_gather x1, waiting for transfers between devices, local(): lax.all_gather(tokens, 'grp', axis=0, tiled=True)  26.8 us
    reduce_scatter x1, waiting for transfers between devices, local(): lax.psum_scatter(partial_value.astype(jnp.float32).astype(jnp.bfloat16),...  22.1 us
    all_to_all x1, starting transfers between devices, local(): lax.all_to_all(outgoing, 'ep', split_axis=1, concat_axis=1, tiled=True)  15.7 us
    reshape x2, local copies, waits for them, and re-layouts, local(): outgoing.astype(jnp.bfloat16)  9.42 us
    reshape x2, local copies, waits for them, and re-layouts, local(): partial_value.astype(jnp.bfloat16).reshape(slot_rows.shape)  9.41 us
  transfers between devices with their start and end apart: 7, of which 5 were waited for; matrix products, arithmetic and copies ran while one was open for 11% of the time, Pallas kernels for 0%

commit v1 on v0

v1 whole, which is shorter than its diff:
```python
import jax
import jax.numpy as jnp
from jax import lax
from jax.sharding import PartitionSpec as P


def two_products(rows, weight_in, weight_out, out_dims):
    product = jnp.dot(rows, weight_in, preferred_element_type=jnp.float32)
    hidden = jax.nn.gelu(product, approximate=True).astype(jnp.bfloat16)
    part = lax.dot_general(
        hidden, weight_out, (((1,), (out_dims,)), ((), ())), preferred_element_type=jnp.float32
    )
    return part.astype(jnp.bfloat16)


def slot_of(route_row, capacity):
    place = jnp.arange(route_row.shape[0], dtype=jnp.int32)
    same = (route_row[:, None] == route_row[None, :]) & (place[None, :] < place[:, None])
    return route_row * capacity + jnp.sum(same.astype(jnp.int32), axis=1)


def shifted(value, step, size):
    return lax.ppermute(value, "grp", [(i, (i + step) % size) for i in range(size)])


def local(tokens, routes, gate_prob, coef_weight, exp_up, exp_down, res_up, res_down):
    row_count, model_width = tokens.shape
    groups = lax.axis_size("grp")
    experts = lax.axis_size("ep")
    capacity = 2 * row_count // experts
    slots = experts * capacity

    res_pair = jnp.concatenate([res_up, res_down.T], axis=1)
    res_all = lax.all_gather(res_pair, "ep", axis=0, tiled=True)
    res_up_all = res_all[:, : res_up.shape[1]]
    res_down_all = res_all[:, res_up.shape[1] :]
    whole_rows = lax.all_gather(tokens, "grp", axis=0, tiled=True)

    slot_index = slot_of(routes[:, 0], capacity)
    table = (slot_index[:, None] == jnp.arange(slots, dtype=jnp.int32)[None, :]).astype(jnp.bfloat16)
    outgoing = lax.dot_general(
        table, tokens, (((0,), (0,)), ((), ())), preferred_element_type=jnp.float32
    ).astype(jnp.bfloat16)
    arrived = lax.all_to_all(
        outgoing.reshape(experts, capacity, model_width), "ep", split_axis=0, concat_axis=0, tiled=True
    ).reshape(slots, model_width)

    steps = [1, groups - 1, 2]
    from_others = [shifted(arrived, step, groups) for step in steps]
    own = lax.optimization_barrier(two_products(arrived, exp_up[0], exp_down[0], 0))
    back = [
        shifted(two_products(rows, exp_up[0], exp_down[0], 0), groups - step, groups)
        for rows, step in zip(from_others, steps)
    ]
    total = own.astype(jnp.float32)
    for part in back:
        total = total + part.astype(jnp.float32)
    returned = lax.all_to_all(
        total.astype(jnp.bfloat16).reshape(experts, capacity, model_width),
        "ep",
        split_axis=0,
        concat_axis=0,
        tiled=True,
    ).reshape(slots, model_width)

    part_res = two_products(whole_rows, res_up_all, res_down_all, 1)
    res_out = lax.psum_scatter(part_res, "grp", scatter_dimension=0, tiled=True).astype(jnp.float32)

    expert_out = jnp.dot(table, returned, preferred_element_type=jnp.float32)
    coef = jax.nn.sigmoid(jnp.dot(tokens, coef_weight, preferred_element_type=jnp.float32))
    mixed = coef[:, None] * res_out + (1.0 - coef[:, None]) * gate_prob[:, None] * expert_out
    return mixed.astype(jnp.bfloat16)


def solution(mesh):
    in_specs = (
        P(("grp", "ep"), None),
        P(("grp", "ep"), None),
        P(("grp", "ep")),
        P(),
        P("ep", None, "grp"),
        P("ep", "grp", None),
        P("ep", "grp"),
        P("grp", "ep"),
    )
    out_specs = P(("grp", "ep"), None)
    return jax.shard_map(local, mesh=mesh, in_specs=in_specs, out_specs=out_specs, check_vma=False)
```

time: 340 us -> 209 us (0.61)
  waiting for transfers between devices: 237 us -> 91.7 us
  blocking collectives: 8.65 us -> 38.8 us
  local copies, waits for them, and re-layouts: 33.2 us -> 3.21 us
  matrix products: 19.1 us -> 25.4 us
  starting transfers between devices: 25.6 us -> 31.6 us
  other arithmetic: 0.72 us -> 4.66 us
    all_to_all x2 -> x1, waiting for transfers between devices: 103 us -> 20.4 us  [local(): lax.all_to_all(total.astype(jnp.bfloat16).reshape(experts, capacity, mode...]
    all_gather x3 -> x2, waiting for transfers between devices: 110 us -> 45.4 us  [the longest x1 45.3 us: local(): res_all = lax.all_gather(res_pair, 'ep', axis=0, tiled=True)]
    all_to_all x0 -> x1, blocking collectives: none -> 38.8 us  [local(): lax.all_to_all(outgoing.reshape(experts, capacity, model_width), 'ep', sp...]
    ppermute x0 -> x6, waiting for transfers between devices: none -> 25.3 us  [shifted(): lax.ppermute(value, 'grp', [(i, (i + step) % size) for i in range(size)])]
    reduce_scatter x2 -> x1, waiting for transfers between devices: 22.1 us -> 0.02 us  [local(): lax.psum_scatter(part_res, 'grp', scatter_dimension=0, tiled=True)]
    ppermute x0 -> x6, starting transfers between devices: none -> 21.9 us  [shifted(): lax.ppermute(value, 'grp', [(i, (i + step) % size) for i in range(size)])]
    reshape x6 -> x4, local copies, waits for them, and re-layouts: 23.1 us -> 2.39 us  [the longest x1 1 us: local(): arrived = lax.all_to_all(outgoing.reshape(experts, capacity, model_width)...]
    all_to_all x2 -> x1, starting transfers between devices: 25 us -> 9.58 us  [local(): lax.all_to_all(total.astype(jnp.bfloat16).reshape(experts, capacity, mode...]
  transfers between devices with their start and end apart: 7 -> 10, of which waited for: 5 -> 5; matrix products, arithmetic and copies ran while one was open for 11% -> 15% of each run, Pallas kernels for 0% -> 0%
where the time goes in v1:
time: 209 us
  waiting for transfers between devices  91.7 us (44%)
  blocking collectives  38.8 us (19%)
  starting transfers between devices  31.6 us (15%)
  matrix products  25.4 us (12%)
  between operations  13.3 us (6%)
  other arithmetic  4.66 us (2%)
  local copies, waits for them, and re-layouts  3.21 us (2%)
    all_gather x1, waiting for transfers between devices, local(): res_all = lax.all_gather(res_pair, 'ep', axis=0, tiled=True)  45.3 us
    all_to_all x1, blocking collectives, local(): lax.all_to_all(outgoing.reshape(experts, capacity, model_width), 'ep', sp...  38.8 us
    ppermute x6, waiting for transfers between devices, shifted(): lax.ppermute(value, 'grp', [(i, (i + step) % size) for i in range(size)])  25.3 us
    dot_general x5, matrix products, two_products(): lax.dot_general(hidden, weight_out, (((1,), (out_dims,)), ((), ())), pref...  21.9 us
    ppermute x6, starting transfers between devices, shifted(): lax.ppermute(value, 'grp', [(i, (i + step) % size) for i in range(size)])  21.9 us
    all_to_all x1, waiting for transfers between devices, local(): lax.all_to_all(total.astype(jnp.bfloat16).reshape(experts, capacity, mode...  20.4 us
    all_to_all x1, starting transfers between devices, local(): lax.all_to_all(total.astype(jnp.bfloat16).reshape(experts, capacity, mode...  9.58 us
  transfers between devices with their start and end apart: 10, of which 5 were waited for; matrix products, arithmetic and copies ran while one was open for 15% of the time, Pallas kernels for 0%

profile of v1, /device:TPU:1, one launch (start us, length us, event | category | flops | bytes accessed | tf_op | source)
XLA Modules:
  0.0 208.6 jit_solution(16023660863359351768)
XLA Ops:
  6.5 0.0 copy-start
  6.5 0.0 all-gather.5.cloned.1.call-start
  6.5 0.7 all-gather.5.cloned.1.call-update
  7.3 0.0 all-gather.3.cloned.1.call-start
  7.3 1.4 pad_maximum_fusion
  8.7 0.0 all-gather.3.cloned.1.call-update
  8.7 0.0 reduce-scatter.2.cloned.1.call-start
  8.7 0.9 convert_reduce_fusion
  9.6 0.7 fusion.132
  10.3 1.3 convolution_convert_fusion
  11.7 0.2 reshape.18
  11.9 38.8 %all_to_all.10 = bf16[128,2,1024]{2,1,0:T(2,128)(2,1)S(1)} all-to-all(bf16[128,2,1024]{2,1,0:T(2,128)(2,1)S(1)} %reshape.18), channel_id=1, replica_groups=mesh['grp'=4,'ep'=128] {'ep'}, dimensions={0} | all-to-all | bytes 1048576 | tf_op jit(solution)/shard_map/all_to_all | solution.py:44
  50.7 1.0 reshape.19
  51.7 4.6 %collective-permute-start.4 = (bf16[256,1024]{1,0:T(8,128)(2,1)}, bf16[256,1024]{1,0:T(8,128)(2,1)S(1)}, u32[]{:S(2)}, u32[]{:S(2)}) collective-permute-start(bf16[256,1024]{1,0:T(8,128)(2,1)} %reshape.19), channel_id=1, source_target_pairs={{0,256},{128,384},{256,0},{384,128},{1,257},{129,385},{257,1},{385... | collective-permute-start | bytes 1572872 | tf_op jit(solution)/shard_map/ppermute | solution.py:23
  56.3 2.8 %collective-permute-start.2 = (bf16[256,1024]{1,0:T(8,128)(2,1)}, bf16[256,1024]{1,0:T(8,128)(2,1)S(1)}, u32[]{:S(2)}, u32[]{:S(2)}) collective-permute-start(bf16[256,1024]{1,0:T(8,128)(2,1)} %reshape.19), channel_id=1, source_target_pairs={{0,384},{128,0},{256,128},{384,256},{1,385},{129,1},{257,129},{385... | collective-permute-start | bytes 1572872 | tf_op jit(solution)/shard_map/ppermute | solution.py:23
  59.1 2.5 %collective-permute-start = (bf16[256,1024]{1,0:T(8,128)(2,1)}, bf16[256,1024]{1,0:T(8,128)(2,1)}, u32[]{:S(2)}, u32[]{:S(2)}) collective-permute-start(bf16[256,1024]{1,0:T(8,128)(2,1)} %reshape.19), channel_id=1, source_target_pairs={{0,128},{128,256},{256,384},{384,0},{1,129},{129,257},{257,385},{3... | collective-permute-start | bytes 1572872 | tf_op jit(solution)/shard_map/ppermute | solution.py:23
  61.6 7.6 %collective-permute-done.4 = bf16[256,1024]{1,0:T(8,128)(2,1)S(1)} collective-permute-done((bf16[256,1024]{1,0:T(8,128)(2,1)}, bf16[256,1024]{1,0:T(8,128)(2,1)S(1)}, u32[]{:S(2)}, u32[]{:S(2)}) %collective-permute-start.4) | collective-permute-done | bytes 524320 | tf_op jit(solution)/shard_map/ppermute | solution.py:23
  69.2 0.0 copy-done
  69.2 3.9 %fusion.42 = bf16[256,1024]{1,0:T(8,128)(2,1)} fusion(bf16[1,1024,1024]{2,1,0:T(8,128)(2,1)S(1)} %copy-done, bf16[256,1024]{1,0:T(8,128)(2,1)S(1)} %collective-permute-done.4, bf16[1,1024,1024]{2,1,0:T(8,128)(2,1)} %param.12), kind=kOutput, calls=%fused_computation.37 | convolution fusion | flops 1076363264 | bytes 5242880 | tf_op jit(solution)/shard_map/dot_general | solution.py:10
  73.1 4.7 %collective-permute-start.5 = (bf16[256,1024]{1,0:T(8,128)(2,1)}, bf16[256,1024]{1,0:T(8,128)(2,1)S(1)}, u32[]{:S(2)}, u32[]{:S(2)}) collective-permute-start(bf16[256,1024]{1,0:T(8,128)(2,1)} %fusion.42), channel_id=1, source_target_pairs={{0,256},{128,384},{256,0},{384,128},{1,257},{129,385},{257,1},{385... | collective-permute-start | bytes 1572872 | tf_op jit(solution)/shard_map/ppermute | solution.py:23
  77.7 2.9 %collective-permute-done.2 = bf16[256,1024]{1,0:T(8,128)(2,1)S(1)} collective-permute-done((bf16[256,1024]{1,0:T(8,128)(2,1)}, bf16[256,1024]{1,0:T(8,128)(2,1)S(1)}, u32[]{:S(2)}, u32[]{:S(2)}) %collective-permute-start.2) | collective-permute-done | bytes 524320 | tf_op jit(solution)/shard_map/ppermute | solution.py:23
  80.6 3.9 %fusion.39 = bf16[256,1024]{1,0:T(8,128)(2,1)} fusion(bf16[1,1024,1024]{2,1,0:T(8,128)(2,1)S(1)} %copy-done, bf16[256,1024]{1,0:T(8,128)(2,1)S(1)} %collective-permute-done.2, bf16[1,1024,1024]{2,1,0:T(8,128)(2,1)} %param.12), kind=kOutput, calls=%fused_computation.36 | convolution fusion | flops 1076363264 | bytes 5242880 | tf_op jit(solution)/shard_map/dot_general | solution.py:10
  84.5 3.0 %collective-permute-start.3 = (bf16[256,1024]{1,0:T(8,128)(2,1)}, bf16[256,1024]{1,0:T(8,128)(2,1)S(1)}, u32[]{:S(2)}, u32[]{:S(2)}) collective-permute-start(bf16[256,1024]{1,0:T(8,128)(2,1)} %fusion.39), channel_id=1, source_target_pairs={{0,128},{128,256},{256,384},{384,0},{1,129},{129,257},{257,385},{3... | collective-permute-start | bytes 1572872 | tf_op jit(solution)/shard_map/ppermute | solution.py:23
  87.5 0.0 all-gather.5.cloned.1.call-done
  87.6 45.3 %all-gather.3.cloned.1.call-done = bf16[1024,2048]{1,0:T(8,128)(2,1)} async-done(((bf16[8,2048]{1,0:T(8,128)(2,1)}), bf16[1024,2048]{1,0:T(8,128)(2,1)}) %all-gather.3.cloned.1.call-update) | async-done | bytes 4194320 | tf_op jit(solution)/shard_map/all_gather | solution.py:34
  132.9 6.1 %fusion.30 = bf16[512,1024]{1,0:T(8,128)(2,1)} fusion(bf16[1024,2048]{1,0:T(8,128)(2,1)} %all-gather.3.cloned.1.call-done, bf16[512,1024]{1,0:T(8,128)(2,1)} %all-gather.5.cloned.1.call-done), kind=kOutput, calls=%fused_computation.33 | convolution fusion | flops 2152726528 | bytes 6291456 | tf_op jit(solution)/shard_map/dot_general | solution.py:10
  139.0 0.0 reduce-scatter.2.cloned.1.call-update
  139.0 0.0 collective-permute-done
  139.0 4.1 %fusion.36 = bf16[256,1024]{1,0:T(8,128)(2,1)} fusion(bf16[1,1024,1024]{2,1,0:T(8,128)(2,1)S(1)} %copy-done, bf16[256,1024]{1,0:T(8,128)(2,1)} %collective-permute-done, bf16[1,1024,1024]{2,1,0:T(8,128)(2,1)} %param.12), kind=kOutput, calls=%fused_computation.35 | convolution fusion | flops 1076363264 | bytes 5242880 | tf_op jit(solution)/shard_map/dot_general | solution.py:10
  143.1 4.3 %collective-permute-start.1 = (bf16[256,1024]{1,0:T(8,128)(2,1)}, bf16[256,1024]{1,0:T(8,128)(2,1)}, u32[]{:S(2)}, u32[]{:S(2)}) collective-permute-start(bf16[256,1024]{1,0:T(8,128)(2,1)} %fusion.36), channel_id=1, source_target_pairs={{0,384},{128,0},{256,128},{384,256},{1,385},{129,1},{257,129},{385... | collective-permute-start | bytes 1572872 | tf_op jit(solution)/shard_map/ppermute | solution.py:23
  147.4 4.0 %fusion.33 = bf16[256,1024]{1,0:T(8,128)(2,1)} fusion(bf16[1,1024,1024]{2,1,0:T(8,128)(2,1)S(1)} %copy-done, bf16[256,1024]{1,0:T(8,128)(2,1)} %reshape.19, bf16[1,1024,1024]{2,1,0:T(8,128)(2,1)} %param.12), kind=kOutput, calls=%fused_computation.34 | convolution fusion | flops 1076363264 | bytes 5242880 | tf_op jit(solution)/shard_map/dot_general | solution.py:10
  151.4 0.0 copy-start.3
  151.4 0.0 collective-permute-done.5
  151.4 0.0 collective-permute-done.3
  151.4 0.0 copy-start.2
  151.5 0.8 copy-done.2
  152.3 14.8 %collective-permute-done.1 = bf16[256,1024]{1,0:T(8,128)(2,1)} collective-permute-done((bf16[256,1024]{1,0:T(8,128)(2,1)}, bf16[256,1024]{1,0:T(8,128)(2,1)}, u32[]{:S(2)}, u32[]{:S(2)}) %collective-permute-start.1) | collective-permute-done | bytes 524320 | tf_op jit(solution)/shard_map/ppermute | solution.py:23
  167.0 1.7 add_convert_fusion
  168.8 1.0 reshape.20
  169.8 9.6 %all-to-all-start.1 = ((bf16[128,2,1024]{2,1,0:T(2,128)(2,1)}), bf16[128,2,1024]{2,1,0:T(2,128)(2,1)S(1)}, u32[]{:S(2)}, u32[]{:S(2)}) async-start(bf16[128,2,1024]{2,1,0:T(2,128)(2,1)} %reshape.20), calls=%async_computation.2 | async-start | bytes 1048576 | tf_op jit(solution)/shard_map/all_to_all | solution.py:58
  179.4 0.0 copy-done.3
  179.4 0.0 copy-done.1
  179.4 0.0 copy-done.4
  179.4 0.2 subtract_multiply_fusion
  179.6 20.4 %all-to-all-done.1 = bf16[128,2,1024]{2,1,0:T(2,128)(2,1)S(1)} async-done(((bf16[128,2,1024]{2,1,0:T(2,128)(2,1)}), bf16[128,2,1024]{2,1,0:T(2,128)(2,1)S(1)}, u32[]{:S(2)}, u32[]{:S(2)}) %all-to-all-start.1) | async-done | bytes 524320 | tf_op jit(solution)/shard_map/all_to_all | solution.py:58
  199.9 0.2 reshape.21
  200.1 0.0 reduce-scatter.2.cloned.1.call-done
  200.2 1.9 fusion.46
  (3 shorter events, 0.0 us)
Async XLA Ops:
  6.5 62.7 %copy-start = (bf16[1,1024,1024]{2,1,0:T(8,128)(2,1)S(1)}, bf16[1,1024,1024]{2,1,0:T(8,128)(2,1)}, u32[]{:S(2)}) copy-start(bf16[1,1024,1024]{2,1,0:T(8,128)(2,1)} %param.13) | copy-start | bytes 6291460
  6.5 81.0 %all-gather.5.cloned.1.call-start = ((), (), s32[]{:S(2)}) async-start(), calls=%async_computation.4 | async-start | bytes 1310720 | tf_op jit(solution)/shard_map/all_gather | solution.py:37
  7.3 125.6 %all-gather.3.cloned.1.call-start = ((), (), s32[]{:S(2)}) async-start(), calls=%async_computation.3 | async-start | bytes 4227072 | tf_op jit(solution)/shard_map/all_gather | solution.py:34
  8.7 191.5 %reduce-scatter.2.cloned.1.call-start = ((), (), s32[]{:S(2)}) async-start(), calls=%async_computation.5 | async-start | bytes 1310720 | tf_op jit(solution)/shard_map/reduce_scatter | solution.py:67
  51.7 17.5 %collective-permute-start.4 = (bf16[256,1024]{1,0:T(8,128)(2,1)}, bf16[256,1024]{1,0:T(8,128)(2,1)S(1)}, u32[]{:S(2)}, u32[]{:S(2)}) collective-permute-start(bf16[256,1024]{1,0:T(8,128)(2,1)} %reshape.19), channel_id=1, source_target_pairs={{0,256},{128,384},{256,0},{384,128},{1,257},{129,385},{257,1},{385... | collective-permute-start | bytes 1572872 | tf_op jit(solution)/shard_map/ppermute | solution.py:23
  56.3 24.3 %collective-permute-start.2 = (bf16[256,1024]{1,0:T(8,128)(2,1)}, bf16[256,1024]{1,0:T(8,128)(2,1)S(1)}, u32[]{:S(2)}, u32[]{:S(2)}) collective-permute-start(bf16[256,1024]{1,0:T(8,128)(2,1)} %reshape.19), channel_id=1, source_target_pairs={{0,384},{128,0},{256,128},{384,256},{1,385},{129,1},{257,129},{385... | collective-permute-start | bytes 1572872 | tf_op jit(solution)/shard_map/ppermute | solution.py:23
  59.1 79.9 %collective-permute-start = (bf16[256,1024]{1,0:T(8,128)(2,1)}, bf16[256,1024]{1,0:T(8,128)(2,1)}, u32[]{:S(2)}, u32[]{:S(2)}) collective-permute-start(bf16[256,1024]{1,0:T(8,128)(2,1)} %reshape.19), channel_id=1, source_target_pairs={{0,128},{128,256},{256,384},{384,0},{1,129},{129,257},{257,385},{3... | collective-permute-start | bytes 1572872 | tf_op jit(solution)/shard_map/ppermute | solution.py:23
  73.1 78.4 %collective-permute-start.5 = (bf16[256,1024]{1,0:T(8,128)(2,1)}, bf16[256,1024]{1,0:T(8,128)(2,1)S(1)}, u32[]{:S(2)}, u32[]{:S(2)}) collective-permute-start(bf16[256,1024]{1,0:T(8,128)(2,1)} %fusion.42), channel_id=1, source_target_pairs={{0,256},{128,384},{256,0},{384,128},{1,257},{129,385},{257,1},{385... | collective-permute-start | bytes 1572872 | tf_op jit(solution)/shard_map/ppermute | solution.py:23
  84.5 66.9 %collective-permute-start.3 = (bf16[256,1024]{1,0:T(8,128)(2,1)}, bf16[256,1024]{1,0:T(8,128)(2,1)S(1)}, u32[]{:S(2)}, u32[]{:S(2)}) collective-permute-start(bf16[256,1024]{1,0:T(8,128)(2,1)} %fusion.39), channel_id=1, source_target_pairs={{0,128},{128,256},{256,384},{384,0},{1,129},{129,257},{257,385},{3... | collective-permute-start | bytes 1572872 | tf_op jit(solution)/shard_map/ppermute | solution.py:23
  143.1 24.0 %collective-permute-start.1 = (bf16[256,1024]{1,0:T(8,128)(2,1)}, bf16[256,1024]{1,0:T(8,128)(2,1)}, u32[]{:S(2)}, u32[]{:S(2)}) collective-permute-start(bf16[256,1024]{1,0:T(8,128)(2,1)} %fusion.36), channel_id=1, source_target_pairs={{0,384},{128,0},{256,128},{384,256},{1,385},{129,1},{257,129},{385... | collective-permute-start | bytes 1572872 | tf_op jit(solution)/shard_map/ppermute | solution.py:23
  151.4 27.9 %copy-start.3 = (bf16[1024]{0:T(1024)(128)(2,1)S(1)}, bf16[1024]{0:T(1024)(128)(2,1)}, u32[]{:S(2)}) copy-start(bf16[1024]{0:T(1024)(128)(2,1)} %param.11) | copy-start | bytes 6148
  151.4 28.0 %copy-start.1 = (bf16[128,1024]{1,0:T(8,128)(2,1)S(1)}, bf16[128,1024]{1,0:T(8,128)(2,1)}, u32[]{:S(2)}) copy-start(bf16[128,1024]{1,0:T(8,128)(2,1)} %param.8) | copy-start | bytes 786436
  151.4 28.0 %copy-start.4 = (f32[128]{0:T(128)S(1)}, f32[128]{0:T(128)}, u32[]{:S(2)}) copy-start(f32[128]{0:T(128)} %param.10) | copy-start | bytes 1540
  151.4 0.8 copy-start.2
  169.8 30.2 %all-to-all-start.1 = ((bf16[128,2,1024]{2,1,0:T(2,128)(2,1)}), bf16[128,2,1024]{2,1,0:T(2,128)(2,1)S(1)}, u32[]{:S(2)}, u32[]{:S(2)}) async-start(bf16[128,2,1024]{2,1,0:T(2,128)(2,1)} %reshape.20), calls=%async_computation.2 | async-start | bytes 1048576 | tf_op jit(solution)/shard_map/all_to_all | solution.py:58
Sparse Core Ops, SparseCore 0:
  9.5 33.8 all-gather.4
  46.5 86.3 all-gather.2
  139.1 29.3 reduce-scatter.1

commit v2 on v1

v2 whole, which is shorter than its diff:
```python
import jax
import jax.numpy as jnp
from jax import lax
from jax.sharding import PartitionSpec as P


def gelu_product(rows, weight_in):
    product = jnp.dot(rows, weight_in, preferred_element_type=jnp.float32)
    return jax.nn.gelu(product, approximate=True).astype(jnp.bfloat16)


def two_products(rows, weight_in, weight_out, out_dim):
    part = lax.dot_general(
        gelu_product(rows, weight_in),
        weight_out,
        (((1,), (out_dim,)), ((), ())),
        preferred_element_type=jnp.float32,
    )
    return part.astype(jnp.bfloat16)


def slot_of(route_row, capacity):
    place = jnp.arange(route_row.shape[0], dtype=jnp.int32)
    same = (route_row[:, None] == route_row[None, :]) & (place[None, :] < place[:, None])
    return route_row * capacity + jnp.sum(same.astype(jnp.int32), axis=1)


def shifted(value, step):
    size = lax.axis_size("grp")
    return lax.ppermute(value, "grp", [(i, (i + step) % size) for i in range(size)])


def exchanged(rows, capacity):
    experts = lax.axis_size("ep")
    cut = rows.reshape(experts, capacity, rows.shape[1])
    return lax.all_to_all(cut, "ep", split_axis=0, concat_axis=0, tiled=True).reshape(rows.shape)


def after(value, earlier):
    return lax.optimization_barrier((value, earlier))[0]


def summed(own, others):
    total = own.astype(jnp.float32)
    for part in others:
        total = total + part.astype(jnp.float32)
    return total


def local(tokens, routes, gate_prob, coef_weight, exp_up, exp_down, res_up, res_down):
    row_count, model_width = tokens.shape
    groups = lax.axis_size("grp")
    experts = lax.axis_size("ep")
    capacity = 2 * row_count // experts
    slots = experts * capacity
    steps = [1, groups - 1, 2]

    res_pair = jnp.concatenate([res_up, res_down.T], axis=1)
    res_all = lax.all_gather(res_pair, "ep", axis=0, tiled=True)
    res_up_all = res_all[:, : res_up.shape[1]]
    res_down_all = res_all[:, res_up.shape[1] :]

    slot_index = slot_of(routes[:, 0], capacity)
    table = (slot_index[:, None] == jnp.arange(slots, dtype=jnp.int32)[None, :]).astype(jnp.bfloat16)
    outgoing = lax.dot_general(
        table, tokens, (((0,), (0,)), ((), ())), preferred_element_type=jnp.float32
    ).astype(jnp.bfloat16)
    arrived = exchanged(outgoing, capacity)
    other_tokens = [shifted(tokens, step) for step in steps]
    arrived = after(arrived, other_tokens)

    from_others = [shifted(arrived, step) for step in steps]
    own = lax.optimization_barrier(two_products(arrived, exp_up[0], exp_down[0], 0))
    parts = [two_products(rows, exp_up[0], exp_down[0], 0) for rows in from_others]
    back = [shifted(part, groups - step) for part, step in zip(parts, steps)]
    total = summed(own, back).astype(jnp.bfloat16)
    returned = exchanged(total, capacity)

    whole_rows = jnp.concatenate([tokens] + other_tokens, axis=0)
    part_res = two_products(after(whole_rows, total), res_up_all, res_down_all, 1)
    pieces = [part_res[i * row_count : (i + 1) * row_count] for i in range(groups)]
    res_back = [shifted(piece, groups - step) for piece, step in zip(pieces[1:], steps)]
    res_out = summed(pieces[0], res_back)

    expert_out = jnp.dot(table, returned, preferred_element_type=jnp.float32)
    coef = jax.nn.sigmoid(jnp.dot(tokens, coef_weight, preferred_element_type=jnp.float32))
    mixed = coef[:, None] * res_out + (1.0 - coef[:, None]) * gate_prob[:, None] * expert_out
    return mixed.astype(jnp.bfloat16)


def solution(mesh):
    in_specs = (
        P(("grp", "ep"), None),
        P(("grp", "ep"), None),
        P(("grp", "ep")),
        P(),
        P("ep", None, "grp"),
        P("ep", "grp", None),
        P("ep", "grp"),
        P("grp", "ep"),
    )
    out_specs = P(("grp", "ep"), None)
    return jax.shard_map(local, mesh=mesh, in_specs=in_specs, out_specs=out_specs, check_vma=False)
```

time: 209 us -> 157 us (0.75)
  waiting for transfers between devices: 91.7 us -> 32.4 us
  starting transfers between devices: 31.6 us -> 71.4 us
  blocking collectives: 38.8 us -> 0 us
  local copies, waits for them, and re-layouts: 3.21 us -> 6.02 us
  other arithmetic: 4.66 us -> 6.95 us
    all_gather x1, waiting for transfers between devices: 45.3 us -> 0.02 us  [local(): res_all = lax.all_gather(res_pair, 'ep', axis=0, tiled=True)]
    all_to_all x1 -> x0, blocking collectives: 38.8 us -> none  [local(): lax.all_to_all(outgoing.reshape(experts, capacity, model_width), 'ep', sp...]
    all_to_all x1 -> x2, starting transfers between devices: 9.58 us -> 34.1 us  [exchanged(): lax.all_to_all(cut, 'ep', split_axis=0, concat_axis=0, tiled=True)]
    ppermute x6 -> x12, starting transfers between devices: 21.9 us -> 37.3 us  [shifted(): lax.ppermute(value, 'grp', [(i, (i + step) % size) for i in range(size)])]
    ppermute x6 -> x12, waiting for transfers between devices: 25.3 us -> 17.4 us  [shifted(): lax.ppermute(value, 'grp', [(i, (i + step) % size) for i in range(size)])]
    all_to_all x1 -> x2, waiting for transfers between devices: 20.4 us -> 15 us  [exchanged(): lax.all_to_all(cut, 'ep', split_axis=0, concat_axis=0, tiled=True)]
    concatenate x0 -> x1, other arithmetic: none -> 2.18 us  [local(): whole_rows = jnp.concatenate([tokens] + other_tokens, axis=0)]
  transfers between devices with their start and end apart: 10 -> 15, of which waited for: 5 -> 6; matrix products, arithmetic and copies ran while one was open for 15% -> 22% of each run, Pallas kernels for 0% -> 0%
where the time goes in v2:
time: 157 us; the launch traced here: 156 us
  starting transfers between devices  71.4 us (45%)
  waiting for transfers between devices  32.4 us (21%)
  matrix products  25.8 us (16%)
  between operations  13.6 us (9%)
  other arithmetic  6.95 us (4%)
  local copies, waits for them, and re-layouts  6.02 us (4%)
    ppermute x12, starting transfers between devices, shifted(): lax.ppermute(value, 'grp', [(i, (i + step) % size) for i in range(size)])  37.3 us
    all_to_all x2, starting transfers between devices, exchanged(): lax.all_to_all(cut, 'ep', split_axis=0, concat_axis=0, tiled=True)  34.1 us
    dot_general x5, matrix products, two_products(): lax.dot_general(gelu_product(rows, weight_in), weight_out, (((1,), (out_d...  22 us
    ppermute x12, waiting for transfers between devices, shifted(): lax.ppermute(value, 'grp', [(i, (i + step) % size) for i in range(size)])  17.4 us
    all_to_all x2, waiting for transfers between devices, exchanged(): lax.all_to_all(cut, 'ep', split_axis=0, concat_axis=0, tiled=True)  15 us
  transfers between devices with their start and end apart: 15, of which 6 were waited for; matrix products, arithmetic and copies ran while one was open for 22% of the time, Pallas kernels for 0%

profile of v2, /device:TPU:1, one launch (start us, length us, event | category | flops | bytes accessed | tf_op | source)
XLA Modules:
  0.0 156.2 jit_solution(9269922019665609175)
XLA Ops:
  6.5 1.5 pad_maximum_fusion.1
  8.0 0.0 all-gather.2.cloned.1.call-update
  8.1 0.9 convert_reduce_fusion
  9.0 0.7 fusion.130
  9.6 1.3 convolution_convert_fusion
  11.0 1.0 reshape.18
  12.0 18.4 %all-to-all-start = ((bf16[128,2,1024]{2,1,0:T(2,128)(2,1)}), bf16[128,2,1024]{2,1,0:T(2,128)(2,1)S(1)}, u32[]{:S(2)}, u32[]{:S(2)}) async-start(bf16[128,2,1024]{2,1,0:T(2,128)(2,1)} %reshape.18), calls=%async_computation | async-start | bytes 1048576 | tf_op jit(solution)/shard_map/all_to_all | solution.py:36
  30.4 3.1 %collective-permute-start = (bf16[128,1024]{1,0:T(8,128)(2,1)S(1)}, bf16[128,1024]{1,0:T(8,128)(2,1)S(1)}, u32[]{:S(2)}, u32[]{:S(2)}) collective-permute-start(bf16[128,1024]{1,0:T(8,128)(2,1)S(1)} %copy-done.1), channel_id=1, source_target_pairs={{0,128},{128,256},{256,384},{384,0},{1,129},{129,257},{257,385},{3... | collective-permute-start | bytes 786440 | tf_op jit(solution)/shard_map/ppermute | solution.py:30
  33.6 3.4 %collective-permute-start.1 = (bf16[128,1024]{1,0:T(8,128)(2,1)S(1)}, bf16[128,1024]{1,0:T(8,128)(2,1)S(1)}, u32[]{:S(2)}, u32[]{:S(2)}) collective-permute-start(bf16[128,1024]{1,0:T(8,128)(2,1)S(1)} %copy-done.1), channel_id=1, source_target_pairs={{0,384},{128,0},{256,128},{384,256},{1,385},{129,1},{257,129},{385... | collective-permute-start | bytes 786440 | tf_op jit(solution)/shard_map/ppermute | solution.py:30
  36.9 3.4 %collective-permute-start.2 = (bf16[128,1024]{1,0:T(8,128)(2,1)S(1)}, bf16[128,1024]{1,0:T(8,128)(2,1)}, u32[]{:S(2)}, u32[]{:S(2)}) collective-permute-start(bf16[128,1024]{1,0:T(8,128)(2,1)S(1)} %copy-done.1), channel_id=1, source_target_pairs={{0,256},{128,384},{256,0},{384,128},{1,257},{129,385},{257,1},{385... | collective-permute-start | bytes 786440 | tf_op jit(solution)/shard_map/ppermute | solution.py:30
  40.4 11.0 %all-to-all-done = bf16[128,2,1024]{2,1,0:T(2,128)(2,1)S(1)} async-done(((bf16[128,2,1024]{2,1,0:T(2,128)(2,1)}), bf16[128,2,1024]{2,1,0:T(2,128)(2,1)S(1)}, u32[]{:S(2)}, u32[]{:S(2)}) %all-to-all-start) | async-done | bytes 524320 | tf_op jit(solution)/shard_map/all_to_all | solution.py:36
  51.4 1.0 reshape.19
  52.4 0.0 collective-permute-done
  52.4 0.0 collective-permute-done.1
  52.4 0.0 copy-start.4
  52.4 0.0 collective-permute-done.2
  52.4 3.1 %collective-permute-start.3 = (bf16[256,1024]{1,0:T(8,128)(2,1)}, bf16[256,1024]{1,0:T(8,128)(2,1)S(1)}, u32[]{:S(2)}, u32[]{:S(2)}) collective-permute-start(bf16[256,1024]{1,0:T(8,128)(2,1)} %reshape.19), channel_id=1, source_target_pairs={{0,128},{128,256},{256,384},{384,0},{1,129},{129,257},{257,385},{3... | collective-permute-start | bytes 1572872 | tf_op jit(solution)/shard_map/ppermute | solution.py:30
  55.5 3.4 %collective-permute-start.5 = (bf16[256,1024]{1,0:T(8,128)(2,1)}, bf16[256,1024]{1,0:T(8,128)(2,1)}, u32[]{:S(2)}, u32[]{:S(2)}) collective-permute-start(bf16[256,1024]{1,0:T(8,128)(2,1)} %reshape.19), channel_id=1, source_target_pairs={{0,384},{128,0},{256,128},{384,256},{1,385},{129,1},{257,129},{385... | collective-permute-start | bytes 1572872 | tf_op jit(solution)/shard_map/ppermute | solution.py:30
  58.9 3.4 %collective-permute-start.7 = (bf16[256,1024]{1,0:T(8,128)(2,1)}, bf16[256,1024]{1,0:T(8,128)(2,1)}, u32[]{:S(2)}, u32[]{:S(2)}) collective-permute-start(bf16[256,1024]{1,0:T(8,128)(2,1)} %reshape.19), channel_id=1, source_target_pairs={{0,256},{128,384},{256,0},{384,128},{1,257},{129,385},{257,1},{385... | collective-permute-start | bytes 1572872 | tf_op jit(solution)/shard_map/ppermute | solution.py:30
  62.4 7.1 %collective-permute-done.3 = bf16[256,1024]{1,0:T(8,128)(2,1)S(1)} collective-permute-done((bf16[256,1024]{1,0:T(8,128)(2,1)}, bf16[256,1024]{1,0:T(8,128)(2,1)S(1)}, u32[]{:S(2)}, u32[]{:S(2)}) %collective-permute-start.3) | collective-permute-done | bytes 524320 | tf_op jit(solution)/shard_map/ppermute | solution.py:30
  69.5 3.9 %fusion.34 = bf16[256,1024]{1,0:T(8,128)(2,1)} fusion(bf16[1,1024,1024]{2,1,0:T(8,128)(2,1)S(1)} %copy-done, bf16[256,1024]{1,0:T(8,128)(2,1)S(1)} %collective-permute-done.3, bf16[1,1024,1024]{2,1,0:T(8,128)(2,1)} %param.12), kind=kOutput, calls=%fused_computation.35 | convolution fusion | flops 1076363264 | bytes 5242880 | tf_op jit(solution)/shard_map/dot_general | solution.py:13
  73.4 3.2 %collective-permute-start.4 = (bf16[256,1024]{1,0:T(8,128)(2,1)}, bf16[256,1024]{1,0:T(8,128)(2,1)S(1)}, u32[]{:S(2)}, u32[]{:S(2)}) collective-permute-start(bf16[256,1024]{1,0:T(8,128)(2,1)} %fusion.34), channel_id=1, source_target_pairs={{0,384},{128,0},{256,128},{384,256},{1,385},{129,1},{257,129},{385... | collective-permute-start | bytes 1572872 | tf_op jit(solution)/shard_map/ppermute | solution.py:30
  76.6 0.0 collective-permute-done.5
  76.6 4.1 %fusion.37 = bf16[256,1024]{1,0:T(8,128)(2,1)} fusion(bf16[1,1024,1024]{2,1,0:T(8,128)(2,1)S(1)} %copy-done, bf16[256,1024]{1,0:T(8,128)(2,1)} %collective-permute-done.5, bf16[1,1024,1024]{2,1,0:T(8,128)(2,1)} %param.12), kind=kOutput, calls=%fused_computation.36 | convolution fusion | flops 1076363264 | bytes 5242880 | tf_op jit(solution)/shard_map/dot_general | solution.py:13
  80.7 2.0 %collective-permute-start.6 = (bf16[256,1024]{1,0:T(8,128)(2,1)}, bf16[256,1024]{1,0:T(8,128)(2,1)S(1)}, u32[]{:S(2)}, u32[]{:S(2)}) collective-permute-start(bf16[256,1024]{1,0:T(8,128)(2,1)} %fusion.37), channel_id=1, source_target_pairs={{0,128},{128,256},{256,384},{384,0},{1,129},{129,257},{257,385},{3... | collective-permute-start | bytes 1572872 | tf_op jit(solution)/shard_map/ppermute | solution.py:30
  82.7 4.1 %fusion.40 = bf16[256,1024]{1,0:T(8,128)(2,1)} fusion(bf16[1,1024,1024]{2,1,0:T(8,128)(2,1)S(1)} %copy-done, bf16[256,1024]{1,0:T(8,128)(2,1)} %collective-permute-done.7, bf16[1,1024,1024]{2,1,0:T(8,128)(2,1)} %param.12), kind=kOutput, calls=%fused_computation.37 | convolution fusion | flops 1076363264 | bytes 5242880 | tf_op jit(solution)/shard_map/dot_general | solution.py:13
  86.8 3.8 %collective-permute-start.8 = (bf16[256,1024]{1,0:T(8,128)(2,1)}, bf16[256,1024]{1,0:T(8,128)(2,1)}, u32[]{:S(2)}, u32[]{:S(2)}) collective-permute-start(bf16[256,1024]{1,0:T(8,128)(2,1)} %fusion.40), channel_id=1, source_target_pairs={{0,256},{128,384},{256,0},{384,128},{1,257},{129,385},{257,1},{385... | collective-permute-start | bytes 1572872 | tf_op jit(solution)/shard_map/ppermute | solution.py:30
  90.6 2.2 %pad_maximum_fusion = bf16[512,1024]{1,0:T(8,128)(2,1)} fusion(bf16[128,1024]{1,0:T(8,128)(2,1)} %collective-permute-done.2, bf16[128,1024]{1,0:T(8,128)(2,1)} %copy-done.4, bf16[128,1024]{1,0:T(8,128)(2,1)} %copy-done.3, bf16[128,1024]{1,0:T(8,128)(2,1)S(1)} %copy-done.1), kind=kLoop, calls=%fused_computation.77 | loop fusion | flops 4194304 | bytes 2097152 | tf_op jit(solution)/shard_map/concatenate | solution.py:79
  92.7 4.1 %fusion.31 = bf16[256,1024]{1,0:T(8,128)(2,1)} fusion(bf16[1,1024,1024]{2,1,0:T(8,128)(2,1)S(1)} %copy-done, bf16[256,1024]{1,0:T(8,128)(2,1)} %reshape.19, bf16[1,1024,1024]{2,1,0:T(8,128)(2,1)} %param.12), kind=kOutput, calls=%fused_computation.34 | convolution fusion | flops 1076363264 | bytes 5242880 | tf_op jit(solution)/shard_map/dot_general | solution.py:13
  96.9 0.8 copy-done.2
  97.7 4.4 %collective-permute-done.8 = bf16[256,1024]{1,0:T(8,128)(2,1)} collective-permute-done((bf16[256,1024]{1,0:T(8,128)(2,1)}, bf16[256,1024]{1,0:T(8,128)(2,1)}, u32[]{:S(2)}, u32[]{:S(2)}) %collective-permute-start.8) | collective-permute-done | bytes 524320 | tf_op jit(solution)/shard_map/ppermute | solution.py:30
  102.0 1.7 %add_convert_fusion = bf16[256,1024]{1,0:T(8,128)(2,1)S(1)} fusion(bf16[256,1024]{1,0:T(8,128)(2,1)} %collective-permute-done.8, bf16[256,1024]{1,0:T(8,128)(2,1)} %copy-done.2, bf16[256,1024]{1,0:T(8,128)(2,1)S(1)} %collective-permute-done.4, bf16[256,1024]{1,0:T(8,128)(2,1)} %fusion.31), kind=kLoop, calls=%fused_computation.82 | loop fusion | flops 2097152 | bytes 2621440 | tf_op jit(solution)/shard_map/convert_element_type | solution.py:76
  103.8 1.0 reshape.20
  104.8 15.6 %all-to-all-start.1 = ((bf16[128,2,1024]{2,1,0:T(2,128)(2,1)}), bf16[128,2,1024]{2,1,0:T(2,128)(2,1)S(1)}, u32[]{:S(2)}, u32[]{:S(2)}) async-start(bf16[128,2,1024]{2,1,0:T(2,128)(2,1)} %reshape.20), calls=%async_computation.1 | async-start | bytes 1048576 | tf_op jit(solution)/shard_map/all_to_all | solution.py:36
  120.4 0.0 copy-start.5
  120.4 0.0 copy-start.6
  120.4 0.0 all-gather.2.cloned.1.call-done
  120.5 5.9 %fusion.28 = bf16[512,1024]{1,0:T(8,128)(2,1)} fusion(bf16[1024,2048]{1,0:T(8,128)(2,1)} %all-gather.2.cloned.1.call-done, bf16[512,1024]{1,0:T(8,128)(2,1)} %pad_maximum_fusion), kind=kOutput, calls=%fused_computation.33 | convolution fusion | flops 2152726528 | bytes 6291456 | tf_op jit(solution)/shard_map/dot_general | solution.py:13
  126.4 2.0 %fusion.151 = (bf16[128,1024]{1,0:T(8,128)(2,1)}, bf16[128,1024]{1,0:T(8,128)(2,1)}, bf16[128,1024]{1,0:T(8,128)(2,1)}) fusion(bf16[512,1024]{1,0:T(8,128)(2,1)} %fusion.28), kind=kLoop, calls=%fused_computation.130 | loop fusion | bytes 1572864 | tf_op jit(solution)/shard_map/slice | solution.py:81
  128.4 1.9 %collective-permute-start.10 = (bf16[128,1024]{1,0:T(8,128)(2,1)}, bf16[128,1024]{1,0:T(8,128)(2,1)}, u32[]{:S(2)}, u32[]{:S(2)}) collective-permute-start(bf16[128,1024]{1,0:T(8,128)(2,1)} %get-tuple-element.11), channel_id=1, source_target_pairs={{0,128},{128,256},{256,384},{384,0},{1,129},{129,257},{257,385},{3... | collective-permute-start | bytes 786440 | tf_op jit(solution)/shard_map/ppermute | solution.py:30
  130.3 3.6 %collective-permute-start.11 = (bf16[128,1024]{1,0:T(8,128)(2,1)}, bf16[128,1024]{1,0:T(8,128)(2,1)}, u32[]{:S(2)}, u32[]{:S(2)}) collective-permute-start(bf16[128,1024]{1,0:T(8,128)(2,1)} %get-tuple-element.10), channel_id=1, source_target_pairs={{0,256},{128,384},{256,0},{384,128},{1,257},{129,385},{257,1},{385... | collective-permute-start | bytes 786440 | tf_op jit(solution)/shard_map/ppermute | solution.py:30
  133.9 2.9 %collective-permute-start.9 = (bf16[128,1024]{1,0:T(8,128)(2,1)}, bf16[128,1024]{1,0:T(8,128)(2,1)}, u32[]{:S(2)}, u32[]{:S(2)}) collective-permute-start(bf16[128,1024]{1,0:T(8,128)(2,1)} %get-tuple-element.9), channel_id=1, source_target_pairs={{0,384},{128,0},{256,128},{384,256},{1,385},{129,1},{257,129},{385... | collective-permute-start | bytes 786440 | tf_op jit(solution)/shard_map/ppermute | solution.py:30
  136.8 0.2 subtract_multiply_fusion
  137.0 4.0 %all-to-all-done.1 = bf16[128,2,1024]{2,1,0:T(2,128)(2,1)S(1)} async-done(((bf16[128,2,1024]{2,1,0:T(2,128)(2,1)}), bf16[128,2,1024]{2,1,0:T(2,128)(2,1)S(1)}, u32[]{:S(2)}, u32[]{:S(2)}) %all-to-all-start.1) | async-done | bytes 524320 | tf_op jit(solution)/shard_map/all_to_all | solution.py:36
  141.0 0.2 reshape.21
  141.2 2.0 %collective-permute-done.11 = bf16[128,1024]{1,0:T(8,128)(2,1)} collective-permute-done((bf16[128,1024]{1,0:T(8,128)(2,1)}, bf16[128,1024]{1,0:T(8,128)(2,1)}, u32[]{:S(2)}, u32[]{:S(2)}) %collective-permute-start.11) | collective-permute-done | bytes 262176 | tf_op jit(solution)/shard_map/ppermute | solution.py:30
  143.2 3.9 %collective-permute-done.9 = bf16[128,1024]{1,0:T(8,128)(2,1)} collective-permute-done((bf16[128,1024]{1,0:T(8,128)(2,1)}, bf16[128,1024]{1,0:T(8,128)(2,1)}, u32[]{:S(2)}, u32[]{:S(2)}) %collective-permute-start.9) | collective-permute-done | bytes 262176 | tf_op jit(solution)/shard_map/ppermute | solution.py:30
  147.1 2.2 %add_convert_fusion.1 = bf16[128,1024]{1,0:T(8,128)(2,1)} fusion(bf16[128,1024]{1,0:T(8,128)(2,1)} %collective-permute-done.11, bf16[128,1024]{1,0:T(8,128)(2,1)} %collective-permute-done.10, bf16[128,1024]{1,0:T(8,128)(2,1)} %collective-permute-done.9, bf16[512,1024]{1,0:T(8,128)(2,1)} %fusion.28, bf16[256,1024]{1,0:T(8,128)(2,1)S(1)} %reshape.21, ...), kind=kOutput, calls=%fused_computation.83 | convolution fusion | flops 68583424 | bytes 1836544 | tf_op jit(solution)/shard_map/dot_general | solution.py:85
  (16 shorter events, 0.0 us)
Async XLA Ops:
  6.5 63.0 %copy-start = (bf16[1,1024,1024]{2,1,0:T(8,128)(2,1)S(1)}, bf16[1,1024,1024]{2,1,0:T(8,128)(2,1)}, u32[]{:S(2)}) copy-start(bf16[1,1024,1024]{2,1,0:T(8,128)(2,1)} %param.13) | copy-start | bytes 6291460
  6.5 23.9 %copy-start.1 = (bf16[128,1024]{1,0:T(8,128)(2,1)S(1)}, bf16[128,1024]{1,0:T(8,128)(2,1)}, u32[]{:S(2)}) copy-start(bf16[128,1024]{1,0:T(8,128)(2,1)} %param.8) | copy-start | bytes 786436
  6.5 113.9 %all-gather.2.cloned.1.call-start = ((), (), s32[]{:S(2)}) async-start(), calls=%async_computation.2 | async-start | bytes 4227072 | tf_op jit(solution)/shard_map/all_gather | solution.py:59
  12.0 39.4 %all-to-all-start = ((bf16[128,2,1024]{2,1,0:T(2,128)(2,1)}), bf16[128,2,1024]{2,1,0:T(2,128)(2,1)S(1)}, u32[]{:S(2)}, u32[]{:S(2)}) async-start(bf16[128,2,1024]{2,1,0:T(2,128)(2,1)} %reshape.18), calls=%async_computation | async-start | bytes 1048576 | tf_op jit(solution)/shard_map/all_to_all | solution.py:36
  30.4 22.0 %collective-permute-start = (bf16[128,1024]{1,0:T(8,128)(2,1)S(1)}, bf16[128,1024]{1,0:T(8,128)(2,1)S(1)}, u32[]{:S(2)}, u32[]{:S(2)}) collective-permute-start(bf16[128,1024]{1,0:T(8,128)(2,1)S(1)} %copy-done.1), channel_id=1, source_target_pairs={{0,128},{128,256},{256,384},{384,0},{1,129},{129,257},{257,385},{3... | collective-permute-start | bytes 786440 | tf_op jit(solution)/shard_map/ppermute | solution.py:30
  33.6 18.8 %collective-permute-start.1 = (bf16[128,1024]{1,0:T(8,128)(2,1)S(1)}, bf16[128,1024]{1,0:T(8,128)(2,1)S(1)}, u32[]{:S(2)}, u32[]{:S(2)}) collective-permute-start(bf16[128,1024]{1,0:T(8,128)(2,1)S(1)} %copy-done.1), channel_id=1, source_target_pairs={{0,384},{128,0},{256,128},{384,256},{1,385},{129,1},{257,129},{385... | collective-permute-start | bytes 786440 | tf_op jit(solution)/shard_map/ppermute | solution.py:30
  36.9 15.5 %collective-permute-start.2 = (bf16[128,1024]{1,0:T(8,128)(2,1)S(1)}, bf16[128,1024]{1,0:T(8,128)(2,1)}, u32[]{:S(2)}, u32[]{:S(2)}) collective-permute-start(bf16[128,1024]{1,0:T(8,128)(2,1)S(1)} %copy-done.1), channel_id=1, source_target_pairs={{0,256},{128,384},{256,0},{384,128},{1,257},{129,385},{257,1},{385... | collective-permute-start | bytes 786440 | tf_op jit(solution)/shard_map/ppermute | solution.py:30
  52.4 21.0 %copy-start.3 = (bf16[128,1024]{1,0:T(8,128)(2,1)}, bf16[128,1024]{1,0:T(8,128)(2,1)S(1)}, u32[]{:S(2)}) copy-start(bf16[128,1024]{1,0:T(8,128)(2,1)S(1)} %collective-permute-done) | copy-start | bytes 786436
  52.4 21.0 %copy-start.4 = (bf16[128,1024]{1,0:T(8,128)(2,1)}, bf16[128,1024]{1,0:T(8,128)(2,1)S(1)}, u32[]{:S(2)}) copy-start(bf16[128,1024]{1,0:T(8,128)(2,1)S(1)} %collective-permute-done.1) | copy-start | bytes 786436
  52.4 17.1 %collective-permute-start.3 = (bf16[256,1024]{1,0:T(8,128)(2,1)}, bf16[256,1024]{1,0:T(8,128)(2,1)S(1)}, u32[]{:S(2)}, u32[]{:S(2)}) collective-permute-start(bf16[256,1024]{1,0:T(8,128)(2,1)} %reshape.19), channel_id=1, source_target_pairs={{0,128},{128,256},{256,384},{384,0},{1,129},{129,257},{257,385},{3... | collective-permute-start | bytes 1572872 | tf_op jit(solution)/shard_map/ppermute | solution.py:30
  55.5 21.1 %collective-permute-start.5 = (bf16[256,1024]{1,0:T(8,128)(2,1)}, bf16[256,1024]{1,0:T(8,128)(2,1)}, u32[]{:S(2)}, u32[]{:S(2)}) collective-permute-start(bf16[256,1024]{1,0:T(8,128)(2,1)} %reshape.19), channel_id=1, source_target_pairs={{0,384},{128,0},{256,128},{384,256},{1,385},{129,1},{257,129},{385... | collective-permute-start | bytes 1572872 | tf_op jit(solution)/shard_map/ppermute | solution.py:30
  58.9 23.8 %collective-permute-start.7 = (bf16[256,1024]{1,0:T(8,128)(2,1)}, bf16[256,1024]{1,0:T(8,128)(2,1)}, u32[]{:S(2)}, u32[]{:S(2)}) collective-permute-start(bf16[256,1024]{1,0:T(8,128)(2,1)} %reshape.19), channel_id=1, source_target_pairs={{0,256},{128,384},{256,0},{384,128},{1,257},{129,385},{257,1},{385... | collective-permute-start | bytes 1572872 | tf_op jit(solution)/shard_map/ppermute | solution.py:30
  73.4 23.5 %collective-permute-start.4 = (bf16[256,1024]{1,0:T(8,128)(2,1)}, bf16[256,1024]{1,0:T(8,128)(2,1)S(1)}, u32[]{:S(2)}, u32[]{:S(2)}) collective-permute-start(bf16[256,1024]{1,0:T(8,128)(2,1)} %fusion.34), channel_id=1, source_target_pairs={{0,384},{128,0},{256,128},{384,256},{1,385},{129,1},{257,129},{385... | collective-permute-start | bytes 1572872 | tf_op jit(solution)/shard_map/ppermute | solution.py:30
  80.7 16.2 %collective-permute-start.6 = (bf16[256,1024]{1,0:T(8,128)(2,1)}, bf16[256,1024]{1,0:T(8,128)(2,1)S(1)}, u32[]{:S(2)}, u32[]{:S(2)}) collective-permute-start(bf16[256,1024]{1,0:T(8,128)(2,1)} %fusion.37), channel_id=1, source_target_pairs={{0,128},{128,256},{256,384},{384,0},{1,129},{129,257},{257,385},{3... | collective-permute-start | bytes 1572872 | tf_op jit(solution)/shard_map/ppermute | solution.py:30
  86.8 15.3 %collective-permute-start.8 = (bf16[256,1024]{1,0:T(8,128)(2,1)}, bf16[256,1024]{1,0:T(8,128)(2,1)}, u32[]{:S(2)}, u32[]{:S(2)}) collective-permute-start(bf16[256,1024]{1,0:T(8,128)(2,1)} %fusion.40), channel_id=1, source_target_pairs={{0,256},{128,384},{256,0},{384,128},{1,257},{129,385},{257,1},{385... | collective-permute-start | bytes 1572872 | tf_op jit(solution)/shard_map/ppermute | solution.py:30
  96.9 0.8 copy-start.2
  104.8 36.2 %all-to-all-start.1 = ((bf16[128,2,1024]{2,1,0:T(2,128)(2,1)}), bf16[128,2,1024]{2,1,0:T(2,128)(2,1)S(1)}, u32[]{:S(2)}, u32[]{:S(2)}) async-start(bf16[128,2,1024]{2,1,0:T(2,128)(2,1)} %reshape.20), calls=%async_computation.1 | async-start | bytes 1048576 | tf_op jit(solution)/shard_map/all_to_all | solution.py:36
  120.4 16.4 %copy-start.5 = (bf16[1024]{0:T(1024)(128)(2,1)S(1)}, bf16[1024]{0:T(1024)(128)(2,1)}, u32[]{:S(2)}) copy-start(bf16[1024]{0:T(1024)(128)(2,1)} %param.11) | copy-start | bytes 6148
  120.4 16.4 %copy-start.6 = (f32[128]{0:T(128)S(1)}, f32[128]{0:T(128)}, u32[]{:S(2)}) copy-start(f32[128]{0:T(128)} %param.10) | copy-start | bytes 1540
  128.4 12.8 %collective-permute-start.10 = (bf16[128,1024]{1,0:T(8,128)(2,1)}, bf16[128,1024]{1,0:T(8,128)(2,1)}, u32[]{:S(2)}, u32[]{:S(2)}) collective-permute-start(bf16[128,1024]{1,0:T(8,128)(2,1)} %get-tuple-element.11), channel_id=1, source_target_pairs={{0,128},{128,256},{256,384},{384,0},{1,129},{129,257},{257,385},{3... | collective-permute-start | bytes 786440 | tf_op jit(solution)/shard_map/ppermute | solution.py:30
  130.3 12.9 %collective-permute-start.11 = (bf16[128,1024]{1,0:T(8,128)(2,1)}, bf16[128,1024]{1,0:T(8,128)(2,1)}, u32[]{:S(2)}, u32[]{:S(2)}) collective-permute-start(bf16[128,1024]{1,0:T(8,128)(2,1)} %get-tuple-element.10), channel_id=1, source_target_pairs={{0,256},{128,384},{256,0},{384,128},{1,257},{129,385},{257,1},{385... | collective-permute-start | bytes 786440 | tf_op jit(solution)/shard_map/ppermute | solution.py:30
  133.9 13.2 %collective-permute-start.9 = (bf16[128,1024]{1,0:T(8,128)(2,1)}, bf16[128,1024]{1,0:T(8,128)(2,1)}, u32[]{:S(2)}, u32[]{:S(2)}) collective-permute-start(bf16[128,1024]{1,0:T(8,128)(2,1)} %get-tuple-element.9), channel_id=1, source_target_pairs={{0,384},{128,0},{256,128},{384,256},{1,385},{129,1},{257,129},{385... | collective-permute-start | bytes 786440 | tf_op jit(solution)/shard_map/ppermute | solution.py:30
Sparse Core Ops, SparseCore 0:
  10.5 95.8 all-gather.1

commit v3 on v1

v3 whole, which is shorter than its diff:
```python
import functools

import jax
import jax.numpy as jnp
from jax import lax
from jax.experimental import pallas as pl
from jax.experimental.pallas import tpu as pltpu
from jax.sharding import PartitionSpec as P

SMEM = pl.BlockSpec(memory_space=pltpu.SMEM)
PARAMS = pltpu.CompilerParams(vmem_limit_bytes=48 * 1024 * 1024)
WHOLE = pltpu.CompilerParams(vmem_limit_bytes=60 * 1024 * 1024)


def cost(rows, model, hidden):
    return pl.CostEstimate(
        flops=4 * rows * model * hidden,
        bytes_accessed=4 * model * (hidden + rows),
        transcendentals=rows * hidden,
    )


def slot_table(route_row, capacity, slots):
    count = route_row.shape[1]
    route = jnp.broadcast_to(route_row, (count, count))
    earlier = lax.broadcasted_iota(jnp.int32, (count, count), 0) < lax.broadcasted_iota(jnp.int32, (count, count), 1)
    place = jnp.sum(jnp.where((route == jnp.transpose(route)) & earlier, 1, 0), axis=0, keepdims=True)
    slot = jnp.broadcast_to(route_row * capacity + place, (slots, count))
    return jnp.where(lax.broadcasted_iota(jnp.int32, (slots, count), 0) == slot, 1.0, 0.0).astype(jnp.bfloat16)


def dispatch_kernel(routes, tokens, out):
    experts, capacity, model = out.shape
    table = slot_table(routes[...], capacity, experts * capacity)
    rows = jnp.dot(table, tokens[...], preferred_element_type=jnp.float32).astype(jnp.bfloat16)
    out[...] = rows.reshape(experts, capacity, model)


def unpack_kernel(slots, out):
    out[...] = slots[...].reshape(out.shape)


def products(rows, weight_in, weight_out, out_dim):
    product = jnp.dot(rows, weight_in, preferred_element_type=jnp.float32)
    hidden = jax.nn.gelu(product, approximate=True).astype(jnp.bfloat16)
    part = lax.dot_general(
        hidden, weight_out, (((1,), (out_dim,)), ((), ())), preferred_element_type=jnp.float32
    )
    return part.astype(jnp.bfloat16)


def expert_kernel(rows, weight_in, weight_out, out):
    out[...] = products(rows[...], weight_in[0], weight_out[0], 0)


def expert_pair_kernel(left, right, weight_in, weight_out, out_left, out_right, stack):
    count = left.shape[0]
    stack[:count, :] = left[...]
    stack[count:, :] = right[...]
    part = products(stack[...], weight_in[0], weight_out[0], 0)
    out_left[...] = part[:count, :]
    out_right[...] = part[count:, :]


def gather_kernel(me, left, right, far, own, out):
    count = own.shape[0]
    groups = out.shape[0] // count
    for rows, step in ((left, 1), (right, 3), (far, 2), (own, 0)):
        group = lax.rem(me[0] + groups - step, groups)
        out[pl.ds(pl.multiple_of(group * count, count), count), :] = rows[...]


def residual_kernel(rows, pair, out):
    hidden = pair.shape[1] // 2
    out[...] = products(rows[...], pair[:, :hidden], pair[:, hidden:], 1)


def sum_kernel(own, left, right, far, out):
    total = own[...].astype(jnp.float32) + left[...].astype(jnp.float32)
    total = total + right[...].astype(jnp.float32) + far[...].astype(jnp.float32)
    out[...] = total.astype(jnp.bfloat16).reshape(out.shape)


def scale_kernel(res, tokens, weight, gate, out):
    model = res.shape[1]
    logit = jnp.sum(tokens[...].astype(jnp.float32) * weight[...].astype(jnp.float32), axis=1, keepdims=True)
    coef = 1.0 / (1.0 + jnp.exp(-logit))
    gates = jnp.transpose(jnp.broadcast_to(gate[...], (128, gate.shape[1])))
    out[:, :model] = coef * res[...].astype(jnp.float32)
    out[:, model:] = (1.0 - coef) * gates


def mix_kernel(routes, slots, scaled, out):
    experts, capacity, model = slots.shape
    table = slot_table(routes[...], capacity, experts * capacity)
    rows = slots[...].reshape(experts * capacity, model)
    expert_out = lax.dot_general(table, rows, (((0,), (0,)), ((), ())), preferred_element_type=jnp.float32)
    out[...] = (scaled[:, :model] + scaled[:, model : model + 1] * expert_out).astype(jnp.bfloat16)


def block(shape):
    return pl.BlockSpec(shape, lambda i: (0,) * len(shape))


def call(kernel, ins, shape, estimate=None, scratch=(), count=1, params=PARAMS, dtype=jnp.bfloat16):
    whole = jax.ShapeDtypeStruct(shape, dtype)
    return pl.pallas_call(
        kernel,
        grid=(1,),
        in_specs=[SMEM if value.ndim == 1 else block(value.shape) for value in ins],
        out_specs=block(shape) if count == 1 else [block(shape)] * count,
        out_shape=whole if count == 1 else [whole] * count,
        scratch_shapes=scratch,
        compiler_params=params,
        cost_estimate=estimate,
    )(*ins)


def shifted(value, step):
    size = lax.axis_size("grp")
    return lax.ppermute(value, "grp", [(i, (i + step) % size) for i in range(size)])


def across(value, axis):
    return lax.all_to_all(value, axis, split_axis=0, concat_axis=0, tiled=True)


def after(value, earlier):
    return lax.optimization_barrier((value, earlier))[0]


def local(tokens, routes, gate_prob, coef_weight, exp_up, exp_down, res_up, res_down):
    row_count, model = tokens.shape
    groups, experts = lax.axis_size("grp"), lax.axis_size("ep")
    capacity = 2 * row_count // experts
    slots = experts * capacity
    hidden = exp_up.shape[2]
    route_row = routes.reshape(1, row_count)

    res_pair = jnp.concatenate([res_up, res_down.T], axis=1)
    res_all = lax.all_gather(res_pair, "ep", axis=0, tiled=True)

    outgoing = call(dispatch_kernel, (route_row, tokens), (experts, capacity, model), params=WHOLE)
    arrived = across(outgoing, "ep")
    me = lax.axis_index("grp").astype(jnp.int32).reshape(1)
    other_tokens = [shifted(tokens, step) for step in (1, 3, 2)]
    whole_rows = call(gather_kernel, (me, *other_tokens, tokens), (groups * row_count, model))
    arrived = after(arrived, whole_rows)
    arrived = call(unpack_kernel, (arrived,), (slots, model))
    left, right, far = [shifted(arrived, step) for step in (1, 3, 2)]
    shape, weights = arrived.shape, (exp_up, exp_down)
    own = call(expert_kernel, (arrived, *weights), shape, cost(slots, model, hidden))
    left, right = call(
        expert_pair_kernel,
        (after(left, own), right, *weights),
        shape,
        cost(2 * slots, model, hidden),
        scratch=[pltpu.VMEM((2 * slots, model), jnp.bfloat16)],
        count=2,
    )
    part = call(expert_kernel, (after(far, left), *weights), shape, cost(slots, model, hidden))
    left, right, far = shifted(left, 3), shifted(right, 1), shifted(part, 2)

    total = call(sum_kernel, (own, left, right, far), (experts, capacity, model))
    res_part = call(
        residual_kernel,
        (after(whole_rows, total), res_all),
        whole_rows.shape,
        cost(groups * row_count, model, hidden),
    )
    res_out = lax.psum_scatter(res_part, "grp", scatter_dimension=0, tiled=True)
    total = after(total, res_part)
    returned = across(total, "ep")
    scaled = call(
        scale_kernel,
        (res_out, tokens, coef_weight.reshape(1, model), gate_prob.reshape(1, row_count)),
        (row_count, model + 128),
        dtype=jnp.float32,
    )
    return call(mix_kernel, (route_row, after(returned, scaled), scaled), (row_count, model))


def solution(mesh):
    in_specs = (
        P(("grp", "ep"), None),
        P(("grp", "ep"), None),
        P(("grp", "ep")),
        P(),
        P("ep", None, "grp"),
        P("ep", "grp", None),
        P("ep", "grp"),
        P("grp", "ep"),
    )
    out_specs = P(("grp", "ep"), None)
    return jax.shard_map(local, mesh=mesh, in_specs=in_specs, out_specs=out_specs, check_vma=False)
```

time: 209 us -> 156 us (0.75)
  waiting for transfers between devices: 91.7 us -> 51 us
  blocking collectives: 38.8 us -> 0 us
  starting transfers between devices: 31.6 us -> 67.8 us
  matrix products: 25.4 us -> 0 us
  Pallas kernels: 0 us -> 18.1 us
  other arithmetic: 4.66 us -> 1.39 us
    all_gather x1, waiting for transfers between devices: 45.3 us -> 1.22 us  [local(): res_all = lax.all_gather(res_pair, 'ep', axis=0, tiled=True)]
    all_to_all x1 -> x0, blocking collectives: 38.8 us -> none  [local(): lax.all_to_all(outgoing.reshape(experts, capacity, model_width), 'ep', sp...]
    all_to_all x1 -> x2, starting transfers between devices: 9.58 us -> 35 us  [across(): return lax.all_to_all(value, axis, split_axis=0, concat_axis=0, tiled=True)]
    dot_general x8 -> x0, matrix products: 25.4 us -> none  [the longest x5 21.9 us: two_products(): lax.dot_general(hidden, weight_out, (((1,), (out_dims,)), ((), ())), pref...]
    pallas_call x0 -> x10, Pallas kernels: none -> 18.1 us  [call(): pl.pallas_call(kernel, grid=(1,), in_specs=[SMEM if value.ndim == 1 else...]
    reduce_scatter x1, waiting for transfers between devices: 0.02 us -> 13.2 us  [local(): res_out = lax.psum_scatter(res_part, 'grp', scatter_dimension=0, tiled=True)]
    all_to_all x1 -> x2, waiting for transfers between devices: 20.4 us -> 8.58 us  [across(): return lax.all_to_all(value, axis, split_axis=0, concat_axis=0, tiled=True)]
    ppermute x6 -> x9, starting transfers between devices: 21.9 us -> 32.7 us  [shifted(): lax.ppermute(value, 'grp', [(i, (i + step) % size) for i in range(size)])]
  transfers between devices with their start and end apart: 10 -> 13, of which waited for: 5 -> 12; matrix products, arithmetic and copies ran while one was open for 15% -> 0% of each run, Pallas kernels for 0% -> 7%
where the time goes in v3:
time: 156 us; the launch traced here: 155 us
  starting transfers between devices  67.8 us (43%)
  waiting for transfers between devices  51 us (33%)
  Pallas kernels  18.1 us (12%)
  between operations  13.6 us (9%)
  local copies, waits for them, and re-layouts  3.56 us (2%)
    all_to_all x2, starting transfers between devices, across(): return lax.all_to_all(value, axis, split_axis=0, concat_axis=0, tiled=True)  35 us
    ppermute x9, starting transfers between devices, shifted(): lax.ppermute(value, 'grp', [(i, (i + step) % size) for i in range(size)])  32.7 us
    ppermute x9, waiting for transfers between devices, shifted(): lax.ppermute(value, 'grp', [(i, (i + step) % size) for i in range(size)])  28 us
    pallas_call x10, Pallas kernels, call(): pl.pallas_call(kernel, grid=(1,), in_specs=[SMEM if value.ndim == 1 else...  18.1 us
    reduce_scatter x1, waiting for transfers between devices, local(): res_out = lax.psum_scatter(res_part, 'grp', scatter_dimension=0, tiled=True)  13.2 us
    all_to_all x2, waiting for transfers between devices, across(): return lax.all_to_all(value, axis, split_axis=0, concat_axis=0, tiled=True)  8.58 us
    unnamed x20, local copies, waits for them, and re-layouts  3.56 us
  transfers between devices with their start and end apart: 13, of which 12 were waited for; matrix products, arithmetic and copies ran while one was open for 0% of the time, Pallas kernels for 7%

profile of v3, /device:TPU:1, one launch (start us, length us, event | category | flops | bytes accessed | tf_op | source)
XLA Modules:
  0.0 155.4 jit_solution(11373056119245937124)
XLA Ops:
  6.5 0.0 all-gather.2.cloned.1.call-start
  6.5 1.4 pad_maximum_fusion
  7.9 0.0 all-gather.2.cloned.1.call-update
  8.0 2.2 %shard_map.82 = bf16[128,2,1024]{2,1,0:T(2,128)(2,1)} custom-call(s32[1,128]{1,0:T(1,128)} %bitcast.4, bf16[128,1024]{1,0:T(8,128)(2,1)} %tokens.3), custom_call_target="tpu_custom_call" | custom-call | tf_op jit(solution)/shard_map/pallas_call | solution.py:107
  10.1 18.6 %all-to-all-start = ((bf16[128,2,1024]{2,1,0:T(2,128)(2,1)}), bf16[128,2,1024]{2,1,0:T(2,128)(2,1)S(1)}, u32[]{:S(2)}, u32[]{:S(2)}) async-start(bf16[128,2,1024]{2,1,0:T(2,128)(2,1)} %shard_map.82), calls=%async_computation | async-start | bytes 1048576 | tf_op jit(solution)/shard_map/all_to_all | solution.py:125
  28.7 0.0 reduce-scatter.2.cloned.1.call-start
  28.7 3.1 %collective-permute-start = (bf16[128,1024]{1,0:T(8,128)(2,1)}, bf16[128,1024]{1,0:T(8,128)(2,1)S(1)}, u32[]{:S(2)}, u32[]{:S(2)}) collective-permute-start(bf16[128,1024]{1,0:T(8,128)(2,1)} %tokens.3), channel_id=1, source_target_pairs={{0,128},{128,256},{256,384},{384,0},{1,129},{129,257},{257,385},{3... | collective-permute-start | bytes 786440 | tf_op jit(solution)/shard_map/ppermute | solution.py:121
  31.9 3.4 %collective-permute-start.1 = (bf16[128,1024]{1,0:T(8,128)(2,1)}, bf16[128,1024]{1,0:T(8,128)(2,1)S(1)}, u32[]{:S(2)}, u32[]{:S(2)}) collective-permute-start(bf16[128,1024]{1,0:T(8,128)(2,1)} %tokens.3), channel_id=1, source_target_pairs={{0,384},{128,0},{256,128},{384,256},{1,385},{129,1},{257,129},{385... | collective-permute-start | bytes 786440 | tf_op jit(solution)/shard_map/ppermute | solution.py:121
  35.2 3.4 %collective-permute-start.2 = (bf16[128,1024]{1,0:T(8,128)(2,1)}, bf16[128,1024]{1,0:T(8,128)(2,1)}, u32[]{:S(2)}, u32[]{:S(2)}) collective-permute-start(bf16[128,1024]{1,0:T(8,128)(2,1)} %tokens.3), channel_id=1, source_target_pairs={{0,256},{128,384},{256,0},{384,128},{1,257},{129,385},{257,1},{385... | collective-permute-start | bytes 786440 | tf_op jit(solution)/shard_map/ppermute | solution.py:121
  38.7 0.3 collective-permute-done.left
  39.0 1.7 %collective-permute-done.1.right = bf16[128,1024]{1,0:T(8,128)(2,1)S(1)} collective-permute-done((bf16[128,1024]{1,0:T(8,128)(2,1)}, bf16[128,1024]{1,0:T(8,128)(2,1)S(1)}, u32[]{:S(2)}, u32[]{:S(2)}) %collective-permute-start.1) | collective-permute-done | bytes 262176 | tf_op jit(solution)/shard_map/ppermute | solution.py:121
  40.7 4.6 %collective-permute-done.2.far = bf16[128,1024]{1,0:T(8,128)(2,1)} collective-permute-done((bf16[128,1024]{1,0:T(8,128)(2,1)}, bf16[128,1024]{1,0:T(8,128)(2,1)}, u32[]{:S(2)}, u32[]{:S(2)}) %collective-permute-start.2) | collective-permute-done | bytes 262176 | tf_op jit(solution)/shard_map/ppermute | solution.py:121
  45.3 0.0 copy-done.3
  45.3 1.0 shard_map.83.rows
  46.3 0.0 copy-start.4
  46.3 1.0 copy-done.4
  47.3 2.3 %all-to-all-done.slots = bf16[128,2,1024]{2,1,0:T(2,128)(2,1)S(1)} async-done(((bf16[128,2,1024]{2,1,0:T(2,128)(2,1)}), bf16[128,2,1024]{2,1,0:T(2,128)(2,1)S(1)}, u32[]{:S(2)}, u32[]{:S(2)}) %all-to-all-start) | async-done | bytes 524320 | tf_op jit(solution)/shard_map/all_to_all | solution.py:125
  49.6 0.1 shard_map.84.rows
  49.7 3.1 %collective-permute-start.3 = (bf16[256,1024]{1,0:T(8,128)(2,1)S(1)}, bf16[256,1024]{1,0:T(8,128)(2,1)S(1)}, u32[]{:S(2)}, u32[]{:S(2)}) collective-permute-start(bf16[256,1024]{1,0:T(8,128)(2,1)S(1)} %shard_map.84.rows), channel_id=1, source_target_pairs={{0,128},{128,256},{256,384},{384,0},{1,129},{129,257},{257,385},{3... | collective-permute-start | bytes 1572872 | tf_op jit(solution)/shard_map/ppermute | solution.py:121
  52.8 3.4 %collective-permute-start.4 = (bf16[256,1024]{1,0:T(8,128)(2,1)S(1)}, bf16[256,1024]{1,0:T(8,128)(2,1)S(1)}, u32[]{:S(2)}, u32[]{:S(2)}) collective-permute-start(bf16[256,1024]{1,0:T(8,128)(2,1)S(1)} %shard_map.84.rows), channel_id=1, source_target_pairs={{0,384},{128,0},{256,128},{384,256},{1,385},{129,1},{257,129},{385... | collective-permute-start | bytes 1572872 | tf_op jit(solution)/shard_map/ppermute | solution.py:121
  56.2 3.4 %collective-permute-start.7 = (bf16[256,1024]{1,0:T(8,128)(2,1)S(1)}, bf16[256,1024]{1,0:T(8,128)(2,1)S(1)}, u32[]{:S(2)}, u32[]{:S(2)}) collective-permute-start(bf16[256,1024]{1,0:T(8,128)(2,1)S(1)} %shard_map.84.rows), channel_id=1, source_target_pairs={{0,256},{128,384},{256,0},{384,128},{1,257},{129,385},{257,1},{385... | collective-permute-start | bytes 1572872 | tf_op jit(solution)/shard_map/ppermute | solution.py:121
  59.7 0.0 copy-start.1
  59.7 1.6 %copy-done.1 = bf16[1,1024,1024]{2,1,0:T(8,128)(2,1)S(1)} copy-done((bf16[1,1024,1024]{2,1,0:T(8,128)(2,1)S(1)}, bf16[1,1024,1024]{2,1,0:T(8,128)(2,1)}, u32[]{:S(2)}) %copy-start.1) | copy-done | bytes 2097176
  61.3 1.5 shard_map.85.own
  62.7 0.0 copy-start.2
  62.8 3.2 %collective-permute-done.3.left = bf16[256,1024]{1,0:T(8,128)(2,1)S(1)} collective-permute-done((bf16[256,1024]{1,0:T(8,128)(2,1)S(1)}, bf16[256,1024]{1,0:T(8,128)(2,1)S(1)}, u32[]{:S(2)}, u32[]{:S(2)}) %collective-permute-start.3) | collective-permute-done | bytes 524320 | tf_op jit(solution)/shard_map/ppermute | solution.py:121
  65.9 1.7 %collective-permute-done.4.right = bf16[256,1024]{1,0:T(8,128)(2,1)S(1)} collective-permute-done((bf16[256,1024]{1,0:T(8,128)(2,1)S(1)}, bf16[256,1024]{1,0:T(8,128)(2,1)S(1)}, u32[]{:S(2)}, u32[]{:S(2)}) %collective-permute-start.4) | collective-permute-done | bytes 524320 | tf_op jit(solution)/shard_map/ppermute | solution.py:121
  67.6 3.9 %shard_map.86 = (bf16[256,1024]{1,0:T(8,128)(2,1)S(1)}, bf16[256,1024]{1,0:T(8,128)(2,1)S(1)}) custom-call(bf16[256,1024]{1,0:T(8,128)(2,1)S(1)} %collective-permute-done.3.left, bf16[256,1024]{1,0:T(8,128)(2,1)S(1)} %collective-permute-done.4.right, bf16[1,1024,1024]{2,1,0:T(8,128)(2,1)S(1)} %copy-done, bf16[1,1024,1024]{2,1,0:T(8,128)(2,1)} %weight_out.5), custom_call_target="tpu_custom_call" | custom-call | flops 2147483648 | bytes 6291456 | tf_op jit(solution)/shard_map/pallas_call | solution.py:107
  71.6 5.8 %collective-permute-start.5 = (bf16[256,1024]{1,0:T(8,128)(2,1)S(1)}, bf16[256,1024]{1,0:T(8,128)(2,1)S(1)}, u32[]{:S(2)}, u32[]{:S(2)}) collective-permute-start(bf16[256,1024]{1,0:T(8,128)(2,1)S(1)} %get-tuple-element.15), channel_id=1, source_target_pairs={{0,384},{128,0},{256,128},{384,256},{1,385},{129,1},{257,129},{385... | collective-permute-start | bytes 1572872 | tf_op jit(solution)/shard_map/ppermute | solution.py:121
  77.4 0.1 collective-permute-done.7.rows
  77.6 1.5 shard_map.87
  79.0 0.0 copy-start.5
  79.0 2.1 %collective-permute-start.8 = (bf16[256,1024]{1,0:T(8,128)(2,1)S(1)}, bf16[256,1024]{1,0:T(8,128)(2,1)S(1)}, u32[]{:S(2)}, u32[]{:S(2)}) collective-permute-start(bf16[256,1024]{1,0:T(8,128)(2,1)S(1)} %shard_map.87), channel_id=1, source_target_pairs={{0,256},{128,384},{256,0},{384,128},{1,257},{129,385},{257,1},{385... | collective-permute-start | bytes 1572872 | tf_op jit(solution)/shard_map/ppermute | solution.py:121
  81.1 5.0 %collective-permute-start.6 = (bf16[256,1024]{1,0:T(8,128)(2,1)S(1)}, bf16[256,1024]{1,0:T(8,128)(2,1)S(1)}, u32[]{:S(2)}, u32[]{:S(2)}) collective-permute-start(bf16[256,1024]{1,0:T(8,128)(2,1)S(1)} %get-tuple-element.16), channel_id=1, source_target_pairs={{0,128},{128,256},{256,384},{384,0},{1,129},{129,257},{257,385},{3... | collective-permute-start | bytes 1572872 | tf_op jit(solution)/shard_map/ppermute | solution.py:121
  86.1 4.6 %collective-permute-done.8.far = bf16[256,1024]{1,0:T(8,128)(2,1)S(1)} collective-permute-done((bf16[256,1024]{1,0:T(8,128)(2,1)S(1)}, bf16[256,1024]{1,0:T(8,128)(2,1)S(1)}, u32[]{:S(2)}, u32[]{:S(2)}) %collective-permute-start.8) | collective-permute-done | bytes 524320 | tf_op jit(solution)/shard_map/ppermute | solution.py:121
  90.7 0.0 collective-permute-done.5.left
  90.7 11.8 %collective-permute-done.6.right = bf16[256,1024]{1,0:T(8,128)(2,1)S(1)} collective-permute-done((bf16[256,1024]{1,0:T(8,128)(2,1)S(1)}, bf16[256,1024]{1,0:T(8,128)(2,1)S(1)}, u32[]{:S(2)}, u32[]{:S(2)}) %collective-permute-start.6) | collective-permute-done | bytes 524320 | tf_op jit(solution)/shard_map/ppermute | solution.py:121
  102.5 1.1 shard_map.88
  103.6 1.2 all-gather.2.cloned.1.call-done.pair
  104.8 5.6 %shard_map.89 = bf16[512,1024]{1,0:T(8,128)(2,1)} custom-call(bf16[512,1024]{1,0:T(8,128)(2,1)S(1)} %copy-done.5, bf16[1024,2048]{1,0:T(8,128)(2,1)} %all-gather.2.cloned.1.call-done.pair), custom_call_target="tpu_custom_call" | custom-call | flops 2147483648 | bytes 6291456 | tf_op jit(solution)/shard_map/pallas_call | solution.py:107
  110.4 0.0 reduce-scatter.2.cloned.1.call-update
  110.4 16.5 %all-to-all-start.1 = ((bf16[128,2,1024]{2,1,0:T(2,128)(2,1)}), bf16[128,2,1024]{2,1,0:T(2,128)(2,1)S(1)}, u32[]{:S(2)}, u32[]{:S(2)}) async-start(bf16[128,2,1024]{2,1,0:T(2,128)(2,1)} %shard_map.88), calls=%async_computation.1 | async-start | bytes 1048576 | tf_op jit(solution)/shard_map/all_to_all | solution.py:125
  126.9 13.2 %reduce-scatter.2.cloned.1.call-done.res = bf16[128,1024]{1,0:T(8,128)(2,1)} async-done(((bf16[512,1024]{1,0:T(8,128)(2,1)}), bf16[128,1024]{1,0:T(8,128)(2,1)}) %reduce-scatter.2.cloned.1.call-update) | async-done | bytes 262160 | tf_op jit(solution)/shard_map/reduce_scatter | solution.py:171
  140.1 0.0 copy-done.8
  140.1 0.9 copy-done.6
  141.1 0.2 shard_map.90.scaled
  141.2 6.3 %all-to-all-done.1.slots = bf16[128,2,1024]{2,1,0:T(2,128)(2,1)S(1)} async-done(((bf16[128,2,1024]{2,1,0:T(2,128)(2,1)}), bf16[128,2,1024]{2,1,0:T(2,128)(2,1)S(1)}, u32[]{:S(2)}, u32[]{:S(2)}) %all-to-all-start.1) | async-done | bytes 524320 | tf_op jit(solution)/shard_map/all_to_all | solution.py:125
  147.5 1.1 shard_map.91
  (12 shorter events, 0.0 us)
Async XLA Ops:
  6.5 38.8 %copy-start.3 = (bf16[128,1024]{1,0:T(8,128)(2,1)S(1)}, bf16[128,1024]{1,0:T(8,128)(2,1)}, u32[]{:S(2)}) copy-start(bf16[128,1024]{1,0:T(8,128)(2,1)} %tokens.3) | copy-start | bytes 786436
  6.5 98.3 %all-gather.2.cloned.1.call-start = ((), (), s32[]{:S(2)}) async-start(), calls=%async_computation.3 | async-start | bytes 4227072 | tf_op jit(solution)/shard_map/all_gather | solution.py:141
  10.1 49.5 %copy-start = (bf16[1,1024,1024]{2,1,0:T(8,128)(2,1)S(1)}, bf16[1,1024,1024]{2,1,0:T(8,128)(2,1)}, u32[]{:S(2)}) copy-start(bf16[1,1024,1024]{2,1,0:T(8,128)(2,1)} %weight_in.5) | copy-start | bytes 6291460
  10.1 39.5 %all-to-all-start = ((bf16[128,2,1024]{2,1,0:T(2,128)(2,1)}), bf16[128,2,1024]{2,1,0:T(2,128)(2,1)S(1)}, u32[]{:S(2)}, u32[]{:S(2)}) async-start(bf16[128,2,1024]{2,1,0:T(2,128)(2,1)} %shard_map.82), calls=%async_computation | async-start | bytes 1048576 | tf_op jit(solution)/shard_map/all_to_all | solution.py:125
  28.7 111.4 %reduce-scatter.2.cloned.1.call-start = ((), (), s32[]{:S(2)}) async-start(), calls=%async_computation.4 | async-start | bytes 1310720 | tf_op jit(solution)/shard_map/reduce_scatter | solution.py:171
  28.7 10.2 %collective-permute-start = (bf16[128,1024]{1,0:T(8,128)(2,1)}, bf16[128,1024]{1,0:T(8,128)(2,1)S(1)}, u32[]{:S(2)}, u32[]{:S(2)}) collective-permute-start(bf16[128,1024]{1,0:T(8,128)(2,1)} %tokens.3), channel_id=1, source_target_pairs={{0,128},{128,256},{256,384},{384,0},{1,129},{129,257},{257,385},{3... | collective-permute-start | bytes 786440 | tf_op jit(solution)/shard_map/ppermute | solution.py:121
  31.9 8.8 %collective-permute-start.1 = (bf16[128,1024]{1,0:T(8,128)(2,1)}, bf16[128,1024]{1,0:T(8,128)(2,1)S(1)}, u32[]{:S(2)}, u32[]{:S(2)}) collective-permute-start(bf16[128,1024]{1,0:T(8,128)(2,1)} %tokens.3), channel_id=1, source_target_pairs={{0,384},{128,0},{256,128},{384,256},{1,385},{129,1},{257,129},{385... | collective-permute-start | bytes 786440 | tf_op jit(solution)/shard_map/ppermute | solution.py:121
  35.2 10.1 %collective-permute-start.2 = (bf16[128,1024]{1,0:T(8,128)(2,1)}, bf16[128,1024]{1,0:T(8,128)(2,1)}, u32[]{:S(2)}, u32[]{:S(2)}) collective-permute-start(bf16[128,1024]{1,0:T(8,128)(2,1)} %tokens.3), channel_id=1, source_target_pairs={{0,256},{128,384},{256,0},{384,128},{1,257},{129,385},{257,1},{385... | collective-permute-start | bytes 786440 | tf_op jit(solution)/shard_map/ppermute | solution.py:121
  46.3 1.0 copy-start.4
  49.7 16.2 %collective-permute-start.3 = (bf16[256,1024]{1,0:T(8,128)(2,1)S(1)}, bf16[256,1024]{1,0:T(8,128)(2,1)S(1)}, u32[]{:S(2)}, u32[]{:S(2)}) collective-permute-start(bf16[256,1024]{1,0:T(8,128)(2,1)S(1)} %shard_map.84.rows), channel_id=1, source_target_pairs={{0,128},{128,256},{256,384},{384,0},{1,129},{129,257},{257,385},{3... | collective-permute-start | bytes 1572872 | tf_op jit(solution)/shard_map/ppermute | solution.py:121
  52.8 14.8 %collective-permute-start.4 = (bf16[256,1024]{1,0:T(8,128)(2,1)S(1)}, bf16[256,1024]{1,0:T(8,128)(2,1)S(1)}, u32[]{:S(2)}, u32[]{:S(2)}) collective-permute-start(bf16[256,1024]{1,0:T(8,128)(2,1)S(1)} %shard_map.84.rows), channel_id=1, source_target_pairs={{0,384},{128,0},{256,128},{384,256},{1,385},{129,1},{257,129},{385... | collective-permute-start | bytes 1572872 | tf_op jit(solution)/shard_map/ppermute | solution.py:121
  56.2 21.3 %collective-permute-start.7 = (bf16[256,1024]{1,0:T(8,128)(2,1)S(1)}, bf16[256,1024]{1,0:T(8,128)(2,1)S(1)}, u32[]{:S(2)}, u32[]{:S(2)}) collective-permute-start(bf16[256,1024]{1,0:T(8,128)(2,1)S(1)} %shard_map.84.rows), channel_id=1, source_target_pairs={{0,256},{128,384},{256,0},{384,128},{1,257},{129,385},{257,1},{385... | collective-permute-start | bytes 1572872 | tf_op jit(solution)/shard_map/ppermute | solution.py:121
  59.7 1.6 %copy-start.1 = (bf16[1,1024,1024]{2,1,0:T(8,128)(2,1)S(1)}, bf16[1,1024,1024]{2,1,0:T(8,128)(2,1)}, u32[]{:S(2)}) copy-start(bf16[1,1024,1024]{2,1,0:T(8,128)(2,1)} %weight_out.5) | copy-start | bytes 6291460
  62.7 14.8 %copy-start.2 = (bf16[1,1024,1024]{2,1,0:T(8,128)(2,1)S(1)}, bf16[1,1024,1024]{2,1,0:T(8,128)(2,1)}, u32[]{:S(2)}) copy-start(bf16[1,1024,1024]{2,1,0:T(8,128)(2,1)} %weight_out.5) | copy-start | bytes 6291460
  71.6 19.1 %collective-permute-start.5 = (bf16[256,1024]{1,0:T(8,128)(2,1)S(1)}, bf16[256,1024]{1,0:T(8,128)(2,1)S(1)}, u32[]{:S(2)}, u32[]{:S(2)}) collective-permute-start(bf16[256,1024]{1,0:T(8,128)(2,1)S(1)} %get-tuple-element.15), channel_id=1, source_target_pairs={{0,384},{128,0},{256,128},{384,256},{1,385},{129,1},{257,129},{385... | collective-permute-start | bytes 1572872 | tf_op jit(solution)/shard_map/ppermute | solution.py:121
  79.0 25.8 %copy-start.5 = (bf16[512,1024]{1,0:T(8,128)(2,1)S(1)}, bf16[512,1024]{1,0:T(8,128)(2,1)}, u32[]{:S(2)}) copy-start(bf16[512,1024]{1,0:T(8,128)(2,1)} %copy-done.4) | copy-start | bytes 3145732
  79.0 11.7 %collective-permute-start.8 = (bf16[256,1024]{1,0:T(8,128)(2,1)S(1)}, bf16[256,1024]{1,0:T(8,128)(2,1)S(1)}, u32[]{:S(2)}, u32[]{:S(2)}) collective-permute-start(bf16[256,1024]{1,0:T(8,128)(2,1)S(1)} %shard_map.87), channel_id=1, source_target_pairs={{0,256},{128,384},{256,0},{384,128},{1,257},{129,385},{257,1},{385... | collective-permute-start | bytes 1572872 | tf_op jit(solution)/shard_map/ppermute | solution.py:121
  81.1 21.4 %collective-permute-start.6 = (bf16[256,1024]{1,0:T(8,128)(2,1)S(1)}, bf16[256,1024]{1,0:T(8,128)(2,1)S(1)}, u32[]{:S(2)}, u32[]{:S(2)}) collective-permute-start(bf16[256,1024]{1,0:T(8,128)(2,1)S(1)} %get-tuple-element.16), channel_id=1, source_target_pairs={{0,128},{128,256},{256,384},{384,0},{1,129},{129,257},{257,385},{3... | collective-permute-start | bytes 1572872 | tf_op jit(solution)/shard_map/ppermute | solution.py:121
  110.4 16.5 %copy-start.9 = (bf16[1024]{0:T(1024)(128)(2,1)S(1)}, bf16[1024]{0:T(1024)(128)(2,1)}, u32[]{:S(2)}) copy-start(bf16[1024]{0:T(1024)(128)(2,1)} %param.11) | copy-start | bytes 6148
  110.4 29.7 %copy-start.8 = (f32[128]{0:T(128)S(1)}, f32[128]{0:T(128)}, u32[]{:S(2)}) copy-start(f32[128]{0:T(128)} %param.10) | copy-start | bytes 1540
  110.4 37.1 %copy-start.7 = (s32[128,1]{0,1:T(1,128)S(1)}, s32[128,1]{0,1:T(1,128)}, u32[]{:S(2)}) copy-start(s32[128,1]{0,1:T(1,128)} %param.9) | copy-start | bytes 1540
  110.4 37.0 %all-to-all-start.1 = ((bf16[128,2,1024]{2,1,0:T(2,128)(2,1)}), bf16[128,2,1024]{2,1,0:T(2,128)(2,1)S(1)}, u32[]{:S(2)}, u32[]{:S(2)}) async-start(bf16[128,2,1024]{2,1,0:T(2,128)(2,1)} %shard_map.88), calls=%async_computation.1 | async-start | bytes 1048576 | tf_op jit(solution)/shard_map/all_to_all | solution.py:125
  140.1 1.0 copy-start.6
Sparse Core Ops, SparseCore 0:
  10.5 94.3 all-gather.1
  110.6 29.4 reduce-scatter.1

commit v4 on v3

--- a/solution.py
+++ b/solution.py
@@ -53,6 +53,13 @@
     out[...] = products(rows[...], weight_in[0], weight_out[0], 0)
 
 
+def expert_halves_kernel(upper, lower, weight_in, weight_out, out, stack):
+    count = upper.shape[0]
+    stack[:count, :] = upper[...]
+    stack[count:, :] = lower[...]
+    out[...] = products(stack[...], weight_in[0], weight_out[0], 0)
+
+
 def expert_pair_kernel(left, right, weight_in, weight_out, out_left, out_right, stack):
     count = left.shape[0]
     stack[:count, :] = left[...]
@@ -62,17 +69,18 @@
     out_right[...] = part[count:, :]
 
 
-def gather_kernel(me, left, right, far, own, out):
+def gather_kernel(left, right, far, own, out):
     count = own.shape[0]
-    groups = out.shape[0] // count
-    for rows, step in ((left, 1), (right, 3), (far, 2), (own, 0)):
-        group = lax.rem(me[0] + groups - step, groups)
-        out[pl.ds(pl.multiple_of(group * count, count), count), :] = rows[...]
-
-
-def residual_kernel(rows, pair, out):
+    for place, rows in enumerate((left, right, far, own)):
+        out[place * count : (place + 1) * count, :] = rows[...]
+
+
+def residual_kernel(rows, pair, *outs):
     hidden = pair.shape[1] // 2
-    out[...] = products(rows[...], pair[:, :hidden], pair[:, hidden:], 1)
+    part = products(rows[...], pair[:, :hidden], pair[:, hidden:], 1)
+    count = part.shape[0] // len(outs)
+    for place, out in enumerate(outs):
+        out[...] = part[place * count : (place + 1) * count, :]
 
 
 def sum_kernel(own, left, right, far, out):
@@ -81,12 +89,14 @@
     out[...] = total.astype(jnp.bfloat16).reshape(out.shape)
 
 
-def scale_kernel(res, tokens, weight, gate, out):
-    model = res.shape[1]
+def scale_kernel(left, right, far, own, tokens, weight, gate, out):
+    model = own.shape[1]
+    res = left[...].astype(jnp.float32) + right[...].astype(jnp.float32)
+    res = res + far[...].astype(jnp.float32) + own[...].astype(jnp.float32)
     logit = jnp.sum(tokens[...].astype(jnp.float32) * weight[...].astype(jnp.float32), axis=1, keepdims=True)
     coef = 1.0 / (1.0 + jnp.exp(-logit))
     gates = jnp.transpose(jnp.broadcast_to(gate[...], (128, gate.shape[1])))
-    out[:, :model] = coef * res[...].astype(jnp.float32)
+    out[:, :model] = coef * res
     out[:, model:] = (1.0 - coef) * gates
 
 
@@ -142,38 +152,47 @@
 
     outgoing = call(dispatch_kernel, (route_row, tokens), (experts, capacity, model), params=WHOLE)
     arrived = across(outgoing, "ep")
-    me = lax.axis_index("grp").astype(jnp.int32).reshape(1)
     other_tokens = [shifted(tokens, step) for step in (1, 3, 2)]
-    whole_rows = call(gather_kernel, (me, *other_tokens, tokens), (groups * row_count, model))
-    arrived = after(arrived, whole_rows)
+    arrived = after(arrived, other_tokens)
     arrived = call(unpack_kernel, (arrived,), (slots, model))
-    left, right, far = [shifted(arrived, step) for step in (1, 3, 2)]
-    shape, weights = arrived.shape, (exp_up, exp_down)
-    own = call(expert_kernel, (arrived, *weights), shape, cost(slots, model, hidden))
-    left, right = call(
+    left, right = shifted(arrived, 1), shifted(arrived, 3)
+    half, shape, weights = slots // 2, arrived.shape, (exp_up, exp_down)
+    whole_rows = call(gather_kernel, (*other_tokens, tokens), (groups * row_count, model))
+    own = call(expert_kernel, (after(arrived, whole_rows), *weights), shape, cost(slots, model, hidden))
+    left, right = after((left, right), own)
+    upper, lower = shifted(left[:half], 1), shifted(right[half:], 3)
+    near_left, near_right = call(
         expert_pair_kernel,
-        (after(left, own), right, *weights),
+        (left, right, *weights),
         shape,
         cost(2 * slots, model, hidden),
         scratch=[pltpu.VMEM((2 * slots, model), jnp.bfloat16)],
         count=2,
     )
-    part = call(expert_kernel, (after(far, left), *weights), shape, cost(slots, model, hidden))
-    left, right, far = shifted(left, 3), shifted(right, 1), shifted(part, 2)
-
-    total = call(sum_kernel, (own, left, right, far), (experts, capacity, model))
-    res_part = call(
+    far = call(
+        expert_halves_kernel,
+        (after(upper, near_left), lower, *weights),
+        shape,
+        cost(slots, model, hidden),
+        scratch=[pltpu.VMEM(shape, jnp.bfloat16)],
+    )
+    left, right, far_back = shifted(near_left, 3), shifted(near_right, 1), shifted(far, 2)
+
+    res_parts = call(
         residual_kernel,
-        (after(whole_rows, total), res_all),
-        whole_rows.shape,
+        (after(whole_rows, far), res_all),
+        (row_count, model),
         cost(groups * row_count, model, hidden),
-    )
-    res_out = lax.psum_scatter(res_part, "grp", scatter_dimension=0, tiled=True)
-    total = after(total, res_part)
+        count=groups,
+        params=WHOLE,
+    )
+    total = call(sum_kernel, (own, left, after(right, res_parts), far_back), (experts, capacity, model))
+    res_parts = after(res_parts, total)
+    res_parts = [shifted(part, step) for part, step in zip(res_parts, (3, 1, 2))] + [res_parts[3]]
     returned = across(total, "ep")
     scaled = call(
         scale_kernel,
-        (res_out, tokens, coef_weight.reshape(1, model), gate_prob.reshape(1, row_count)),
+        (*res_parts, tokens, coef_weight.reshape(1, model), gate_prob.reshape(1, row_count)),
         (row_count, model + 128),
         dtype=jnp.float32,
     )

time: 156 us -> 153 us (0.981)
  waiting for transfers between devices: 51 us -> 42.7 us
  starting transfers between devices: 67.8 us -> 69.9 us
  Pallas kernels: 18.1 us -> 20.2 us
    reduce_scatter x1 -> x0, waiting for transfers between devices: 13.2 us -> none  [local(): res_out = lax.psum_scatter(res_part, 'grp', scatter_dimension=0, tiled=True)]
    all_gather x1, waiting for transfers between devices: 1.22 us -> 14.1 us  [local(): res_all = lax.all_gather(res_pair, 'ep', axis=0, tiled=True)]
    ppermute x9 -> x13, starting transfers between devices: 32.7 us -> 40.6 us  [shifted(): lax.ppermute(value, 'grp', [(i, (i + step) % size) for i in range(size)])]
    ppermute x9 -> x13, waiting for transfers between devices: 28 us -> 22.3 us  [shifted(): lax.ppermute(value, 'grp', [(i, (i + step) % size) for i in range(size)])]
    all_to_all x2, starting transfers between devices: 35 us -> 29.3 us  [across(): return lax.all_to_all(value, axis, split_axis=0, concat_axis=0, tiled=True)]
    all_to_all x2, waiting for transfers between devices: 8.58 us -> 6.25 us  [across(): return lax.all_to_all(value, axis, split_axis=0, concat_axis=0, tiled=True)]
    pallas_call x10, Pallas kernels: 18.1 us -> 20.2 us  [call(): pl.pallas_call(kernel, grid=(1,), in_specs=[SMEM if value.ndim == 1 else...]
    unnamed x20 -> x22, local copies, waits for them, and re-layouts: 3.56 us -> 4.27 us
  transfers between devices with their start and end apart: 13 -> 16, of which waited for: 12 -> 11; matrix products, arithmetic and copies ran while one was open for 0% -> 0% of each run, Pallas kernels for 7% -> 11%
where the time goes in v4:
time: 153 us; the launch traced here: 152 us
  starting transfers between devices  69.9 us (46%)
  waiting for transfers between devices  42.7 us (28%)
  Pallas kernels  20.2 us (13%)
  between operations  13.7 us (9%)
  local copies, waits for them, and re-layouts  4.31 us (3%)
    ppermute x13, starting transfers between devices, shifted(): lax.ppermute(value, 'grp', [(i, (i + step) % size) for i in range(size)])  40.6 us
    all_to_all x2, starting transfers between devices, across(): return lax.all_to_all(value, axis, split_axis=0, concat_axis=0, tiled=True)  29.3 us
    ppermute x13, waiting for transfers between devices, shifted(): lax.ppermute(value, 'grp', [(i, (i + step) % size) for i in range(size)])  22.3 us
    pallas_call x10, Pallas kernels, call(): pl.pallas_call(kernel, grid=(1,), in_specs=[SMEM if value.ndim == 1 else...  20.2 us
    all_gather x1, waiting for transfers between devices, local(): res_all = lax.all_gather(res_pair, 'ep', axis=0, tiled=True)  14.1 us
    all_to_all x2, waiting for transfers between devices, across(): return lax.all_to_all(value, axis, split_axis=0, concat_axis=0, tiled=True)  6.25 us
    unnamed x22, local copies, waits for them, and re-layouts  4.27 us
  transfers between devices with their start and end apart: 16, of which 11 were waited for; matrix products, arithmetic and copies ran while one was open for 0% of the time, Pallas kernels for 11%

profile of v4, /device:TPU:1, one launch (start us, length us, event | category | flops | bytes accessed | tf_op | source)
XLA Modules:
  0.0 152.2 jit_solution(15745877626537182188)
XLA Ops:
  6.5 1.4 pad_maximum_fusion
  7.9 0.0 all-gather.2.cloned.1.call-update
  8.0 2.2 %shard_map.82 = bf16[128,2,1024]{2,1,0:T(2,128)(2,1)} custom-call(s32[1,128]{1,0:T(1,128)} %bitcast.3, bf16[128,1024]{1,0:T(8,128)(2,1)} %tokens.3), custom_call_target="tpu_custom_call" | custom-call | tf_op jit(solution)/shard_map/pallas_call | solution.py:117
  10.1 18.6 %all-to-all-start = ((bf16[128,2,1024]{2,1,0:T(2,128)(2,1)}), bf16[128,2,1024]{2,1,0:T(2,128)(2,1)S(1)}, u32[]{:S(2)}, u32[]{:S(2)}) async-start(bf16[128,2,1024]{2,1,0:T(2,128)(2,1)} %shard_map.82), calls=%async_computation | async-start | bytes 1048576 | tf_op jit(solution)/shard_map/all_to_all | solution.py:135
  28.7 3.1 %collective-permute-start = (bf16[128,1024]{1,0:T(8,128)(2,1)}, bf16[128,1024]{1,0:T(8,128)(2,1)S(1)}, u32[]{:S(2)}, u32[]{:S(2)}) collective-permute-start(bf16[128,1024]{1,0:T(8,128)(2,1)} %tokens.3), channel_id=1, source_target_pairs={{0,128},{128,256},{256,384},{384,0},{1,129},{129,257},{257,385},{3... | collective-permute-start | bytes 786440 | tf_op jit(solution)/shard_map/ppermute | solution.py:131
  31.8 3.4 %collective-permute-start.1 = (bf16[128,1024]{1,0:T(8,128)(2,1)}, bf16[128,1024]{1,0:T(8,128)(2,1)S(1)}, u32[]{:S(2)}, u32[]{:S(2)}) collective-permute-start(bf16[128,1024]{1,0:T(8,128)(2,1)} %tokens.3), channel_id=1, source_target_pairs={{0,384},{128,0},{256,128},{384,256},{1,385},{129,1},{257,129},{385... | collective-permute-start | bytes 786440 | tf_op jit(solution)/shard_map/ppermute | solution.py:131
  35.2 3.4 %collective-permute-start.2 = (bf16[128,1024]{1,0:T(8,128)(2,1)}, bf16[128,1024]{1,0:T(8,128)(2,1)S(1)}, u32[]{:S(2)}, u32[]{:S(2)}) collective-permute-start(bf16[128,1024]{1,0:T(8,128)(2,1)} %tokens.3), channel_id=1, source_target_pairs={{0,256},{128,384},{256,0},{384,128},{1,257},{129,385},{257,1},{385... | collective-permute-start | bytes 786440 | tf_op jit(solution)/shard_map/ppermute | solution.py:131
  38.6 0.3 collective-permute-done.left
  38.9 1.7 %collective-permute-done.1.right = bf16[128,1024]{1,0:T(8,128)(2,1)S(1)} collective-permute-done((bf16[128,1024]{1,0:T(8,128)(2,1)}, bf16[128,1024]{1,0:T(8,128)(2,1)S(1)}, u32[]{:S(2)}, u32[]{:S(2)}) %collective-permute-start.1) | collective-permute-done | bytes 262176 | tf_op jit(solution)/shard_map/ppermute | solution.py:131
  40.7 4.5 %collective-permute-done.2.far = bf16[128,1024]{1,0:T(8,128)(2,1)S(1)} collective-permute-done((bf16[128,1024]{1,0:T(8,128)(2,1)}, bf16[128,1024]{1,0:T(8,128)(2,1)S(1)}, u32[]{:S(2)}, u32[]{:S(2)}) %collective-permute-start.2) | collective-permute-done | bytes 262176 | tf_op jit(solution)/shard_map/ppermute | solution.py:131
  45.2 0.7 copy-done.6
  45.9 3.8 %all-to-all-done.slots = bf16[128,2,1024]{2,1,0:T(2,128)(2,1)S(1)} async-done(((bf16[128,2,1024]{2,1,0:T(2,128)(2,1)}), bf16[128,2,1024]{2,1,0:T(2,128)(2,1)S(1)}, u32[]{:S(2)}, u32[]{:S(2)}) %all-to-all-start) | async-done | bytes 524320 | tf_op jit(solution)/shard_map/all_to_all | solution.py:135
  49.6 0.1 shard_map.83.rows
  49.7 3.1 %collective-permute-start.3 = (bf16[256,1024]{1,0:T(8,128)(2,1)S(1)}, bf16[256,1024]{1,0:T(8,128)(2,1)S(1)}, u32[]{:S(2)}, u32[]{:S(2)}) collective-permute-start(bf16[256,1024]{1,0:T(8,128)(2,1)S(1)} %shard_map.83.rows), channel_id=1, source_target_pairs={{0,128},{128,256},{256,384},{384,0},{1,129},{129,257},{257,385},{3... | collective-permute-start | bytes 1572872 | tf_op jit(solution)/shard_map/ppermute | solution.py:131
  52.8 3.4 %collective-permute-start.4 = (bf16[256,1024]{1,0:T(8,128)(2,1)S(1)}, bf16[256,1024]{1,0:T(8,128)(2,1)S(1)}, u32[]{:S(2)}, u32[]{:S(2)}) collective-permute-start(bf16[256,1024]{1,0:T(8,128)(2,1)S(1)} %shard_map.83.rows), channel_id=1, source_target_pairs={{0,384},{128,0},{256,128},{384,256},{1,385},{129,1},{257,129},{385... | collective-permute-start | bytes 1572872 | tf_op jit(solution)/shard_map/ppermute | solution.py:131
  56.2 0.0 copy-start.7
  56.2 0.9 copy-done.7
  57.2 0.1 shard_map.84.rows
  57.3 1.0 copy-done.4
  58.3 1.6 %copy-done.1 = bf16[1,1024,1024]{2,1,0:T(8,128)(2,1)S(1)} copy-done((bf16[1,1024,1024]{2,1,0:T(8,128)(2,1)S(1)}, bf16[1,1024,1024]{2,1,0:T(8,128)(2,1)}, u32[]{:S(2)}) %copy-start.1) | copy-done | bytes 2097176
  59.9 1.5 shard_map.85.own
  61.3 5.4 %collective-permute-done.3.left = bf16[256,1024]{1,0:T(8,128)(2,1)S(1)} collective-permute-done((bf16[256,1024]{1,0:T(8,128)(2,1)S(1)}, bf16[256,1024]{1,0:T(8,128)(2,1)S(1)}, u32[]{:S(2)}, u32[]{:S(2)}) %collective-permute-start.3) | collective-permute-done | bytes 524320 | tf_op jit(solution)/shard_map/ppermute | solution.py:131
  66.7 1.3 collective-permute-done.4.right
  68.0 3.5 %collective-permute-start.7 = (bf16[128,1024]{1,0:T(8,128)(2,1)S(1)}, bf16[128,1024]{1,0:T(8,128)(2,1)S(1)}, u32[]{:S(2)}, u32[]{:S(2)}) collective-permute-start(bf16[128,1024]{1,0:T(8,128)(2,1)S(1)} %slice.6), channel_id=1, source_target_pairs={{0,128},{128,256},{256,384},{384,0},{1,129},{129,257},{257,385},{3... | collective-permute-start | bytes 786440 | tf_op jit(solution)/shard_map/ppermute | solution.py:131
  71.6 0.0 copy-start.2
  71.6 3.5 %collective-permute-start.8 = (bf16[128,1024]{1,0:T(8,128)(2,1)S(1)}, bf16[128,1024]{1,0:T(8,128)(2,1)S(1)}, u32[]{:S(2)}, u32[]{:S(2)}) collective-permute-start(bf16[128,1024]{1,0:T(8,128)(2,1)S(1)} %slice.7), channel_id=1, source_target_pairs={{0,384},{128,0},{256,128},{384,256},{1,385},{129,1},{257,129},{385... | collective-permute-start | bytes 786440 | tf_op jit(solution)/shard_map/ppermute | solution.py:131
  75.1 4.9 %shard_map.86 = (bf16[256,1024]{1,0:T(8,128)(2,1)}, bf16[256,1024]{1,0:T(8,128)(2,1)}) custom-call(bf16[256,1024]{1,0:T(8,128)(2,1)S(1)} %collective-permute-done.3.left, bf16[256,1024]{1,0:T(8,128)(2,1)S(1)} %collective-permute-done.4.right, bf16[1,1024,1024]{2,1,0:T(8,128)(2,1)S(1)} %copy-done, bf16[1,1024,1024]{2,1,0:T(8,128)(2,1)} %weight_out.5), custom_call_target="tpu_custom_call" | custom-call | flops 2147483648 | bytes 6291456 | tf_op jit(solution)/shard_map/pallas_call | solution.py:117
  80.0 3.4 %collective-permute-start.5 = (bf16[256,1024]{1,0:T(8,128)(2,1)}, bf16[256,1024]{1,0:T(8,128)(2,1)S(1)}, u32[]{:S(2)}, u32[]{:S(2)}) collective-permute-start(bf16[256,1024]{1,0:T(8,128)(2,1)} %get-tuple-element.27), channel_id=1, source_target_pairs={{0,384},{128,0},{256,128},{384,256},{1,385},{129,1},{257,129},{385... | collective-permute-start | bytes 1572872 | tf_op jit(solution)/shard_map/ppermute | solution.py:131
  83.3 1.9 %collective-permute-start.6 = (bf16[256,1024]{1,0:T(8,128)(2,1)}, bf16[256,1024]{1,0:T(8,128)(2,1)}, u32[]{:S(2)}, u32[]{:S(2)}) collective-permute-start(bf16[256,1024]{1,0:T(8,128)(2,1)} %get-tuple-element.28), channel_id=1, source_target_pairs={{0,128},{128,256},{256,384},{384,0},{1,129},{129,257},{257,385},{3... | collective-permute-start | bytes 1572872 | tf_op jit(solution)/shard_map/ppermute | solution.py:131
  85.3 0.0 collective-permute-done.7.upper
  85.3 0.0 collective-permute-done.8.lower
  85.3 2.3 %shard_map.87 = bf16[256,1024]{1,0:T(8,128)(2,1)} custom-call(bf16[128,1024]{1,0:T(8,128)(2,1)S(1)} %collective-permute-done.7.upper, bf16[128,1024]{1,0:T(8,128)(2,1)S(1)} %collective-permute-done.8.lower, bf16[1,1024,1024]{2,1,0:T(8,128)(2,1)S(1)} %copy-done, bf16[1,1024,1024]{2,1,0:T(8,128)(2,1)S(1)} %copy-done.2), custom_call_target="tpu_custom_call" | custom-call | flops 1073741824 | bytes 5242880 | tf_op jit(solution)/shard_map/pallas_call | solution.py:117
  87.6 3.2 %collective-permute-start.9 = (bf16[256,1024]{1,0:T(8,128)(2,1)}, bf16[256,1024]{1,0:T(8,128)(2,1)S(1)}, u32[]{:S(2)}, u32[]{:S(2)}) collective-permute-start(bf16[256,1024]{1,0:T(8,128)(2,1)} %shard_map.87), channel_id=1, source_target_pairs={{0,256},{128,384},{256,0},{384,128},{1,257},{129,385},{257,1},{385... | collective-permute-start | bytes 1572872 | tf_op jit(solution)/shard_map/ppermute | solution.py:131
  90.7 14.1 %all-gather.2.cloned.1.call-done.pair = bf16[1024,2048]{1,0:T(8,128)(2,1)} async-done(((bf16[8,2048]{1,0:T(8,128)(2,1)}), bf16[1024,2048]{1,0:T(8,128)(2,1)}) %all-gather.2.cloned.1.call-update) | async-done | bytes 4194320 | tf_op jit(solution)/shard_map/all_gather | solution.py:151
  104.9 5.8 %shard_map.88 = (bf16[128,1024]{1,0:T(8,128)(2,1)}, bf16[128,1024]{1,0:T(8,128)(2,1)}, bf16[128,1024]{1,0:T(8,128)(2,1)}, bf16[128,1024]{1,0:T(8,128)(2,1)}) custom-call(bf16[512,1024]{1,0:T(8,128)(2,1)} %copy-done.4, bf16[1024,2048]{1,0:T(8,128)(2,1)} %all-gather.2.cloned.1.call-done.pair), custom_call_target="tpu_custom_call" | custom-call | flops 2147483648 | bytes 6291456 | tf_op jit(solution)/shard_map/pallas_call | solution.py:117
  110.7 0.0 collective-permute-done.6.right
  110.7 0.0 collective-permute-done.9.far
  110.7 2.2 %shard_map.89 = bf16[128,2,1024]{2,1,0:T(2,128)(2,1)} custom-call(bf16[256,1024]{1,0:T(8,128)(2,1)S(1)} %shard_map.85.own, bf16[256,1024]{1,0:T(8,128)(2,1)S(1)} %collective-permute-done.5.left, bf16[256,1024]{1,0:T(8,128)(2,1)} %collective-permute-done.6.right, bf16[256,1024]{1,0:T(8,128)(2,1)S(1)} %collective-permute-done.9.far), custom_call_target="tpu_custom_call" | custom-call | tf_op jit(solution)/shard_map/pallas_call | solution.py:117
  112.9 10.7 %all-to-all-start.1 = ((bf16[128,2,1024]{2,1,0:T(2,128)(2,1)}), bf16[128,2,1024]{2,1,0:T(2,128)(2,1)S(1)}, u32[]{:S(2)}, u32[]{:S(2)}) async-start(bf16[128,2,1024]{2,1,0:T(2,128)(2,1)} %shard_map.89), calls=%async_computation.1 | async-start | bytes 1048576 | tf_op jit(solution)/shard_map/all_to_all | solution.py:135
  123.6 3.0 %collective-permute-start.10 = (bf16[128,1024]{1,0:T(8,128)(2,1)}, bf16[128,1024]{1,0:T(8,128)(2,1)S(1)}, u32[]{:S(2)}, u32[]{:S(2)}) collective-permute-start(bf16[128,1024]{1,0:T(8,128)(2,1)} %get-tuple-element.36), channel_id=1, source_target_pairs={{0,384},{128,0},{256,128},{384,256},{1,385},{129,1},{257,129},{385... | collective-permute-start | bytes 786440 | tf_op jit(solution)/shard_map/ppermute | solution.py:131
  126.7 2.2 %collective-permute-start.11 = (bf16[128,1024]{1,0:T(8,128)(2,1)}, bf16[128,1024]{1,0:T(8,128)(2,1)S(1)}, u32[]{:S(2)}, u32[]{:S(2)}) collective-permute-start(bf16[128,1024]{1,0:T(8,128)(2,1)} %get-tuple-element.37), channel_id=1, source_target_pairs={{0,128},{128,256},{256,384},{384,0},{1,129},{129,257},{257,385},{3... | collective-permute-start | bytes 786440 | tf_op jit(solution)/shard_map/ppermute | solution.py:131
  128.9 3.5 %collective-permute-start.12 = (bf16[128,1024]{1,0:T(8,128)(2,1)}, bf16[128,1024]{1,0:T(8,128)(2,1)S(1)}, u32[]{:S(2)}, u32[]{:S(2)}) collective-permute-start(bf16[128,1024]{1,0:T(8,128)(2,1)} %get-tuple-element.38), channel_id=1, source_target_pairs={{0,256},{128,384},{256,0},{384,128},{1,257},{129,385},{257,1},{385... | collective-permute-start | bytes 786440 | tf_op jit(solution)/shard_map/ppermute | solution.py:131
  132.5 0.2 collective-permute-done.10.left
  132.7 4.7 %collective-permute-done.11.right = bf16[128,1024]{1,0:T(8,128)(2,1)S(1)} collective-permute-done((bf16[128,1024]{1,0:T(8,128)(2,1)}, bf16[128,1024]{1,0:T(8,128)(2,1)S(1)}, u32[]{:S(2)}, u32[]{:S(2)}) %collective-permute-start.11) | collective-permute-done | bytes 262176 | tf_op jit(solution)/shard_map/ppermute | solution.py:131
  137.4 4.2 %collective-permute-done.12.far = bf16[128,1024]{1,0:T(8,128)(2,1)S(1)} collective-permute-done((bf16[128,1024]{1,0:T(8,128)(2,1)}, bf16[128,1024]{1,0:T(8,128)(2,1)S(1)}, u32[]{:S(2)}, u32[]{:S(2)}) %collective-permute-start.12) | collective-permute-done | bytes 262176 | tf_op jit(solution)/shard_map/ppermute | solution.py:131
  141.5 0.2 shard_map.90.scaled
  141.8 2.5 %all-to-all-done.1.slots = bf16[128,2,1024]{2,1,0:T(2,128)(2,1)S(1)} async-done(((bf16[128,2,1024]{2,1,0:T(2,128)(2,1)}), bf16[128,2,1024]{2,1,0:T(2,128)(2,1)S(1)}, u32[]{:S(2)}, u32[]{:S(2)}) %all-to-all-start.1) | async-done | bytes 524320 | tf_op jit(solution)/shard_map/all_to_all | solution.py:135
  144.2 1.1 shard_map.91
  (21 shorter events, 0.1 us)
Async XLA Ops:
  6.5 49.7 %copy-start.3 = (bf16[128,1024]{1,0:T(8,128)(2,1)S(1)}, bf16[128,1024]{1,0:T(8,128)(2,1)}, u32[]{:S(2)}) copy-start(bf16[128,1024]{1,0:T(8,128)(2,1)} %tokens.3) | copy-start | bytes 786436
  6.5 98.3 %all-gather.2.cloned.1.call-start = ((), (), s32[]{:S(2)}) async-start(), calls=%async_computation.2 | async-start | bytes 4227072 | tf_op jit(solution)/shard_map/all_gather | solution.py:151
  10.1 48.1 %copy-start = (bf16[1,1024,1024]{2,1,0:T(8,128)(2,1)S(1)}, bf16[1,1024,1024]{2,1,0:T(8,128)(2,1)}, u32[]{:S(2)}) copy-start(bf16[1,1024,1024]{2,1,0:T(8,128)(2,1)} %weight_in.5) | copy-start | bytes 6291460
  10.1 39.5 %all-to-all-start = ((bf16[128,2,1024]{2,1,0:T(2,128)(2,1)}), bf16[128,2,1024]{2,1,0:T(2,128)(2,1)S(1)}, u32[]{:S(2)}, u32[]{:S(2)}) async-start(bf16[128,2,1024]{2,1,0:T(2,128)(2,1)} %shard_map.82), calls=%async_computation | async-start | bytes 1048576 | tf_op jit(solution)/shard_map/all_to_all | solution.py:135
  28.7 10.2 %collective-permute-start = (bf16[128,1024]{1,0:T(8,128)(2,1)}, bf16[128,1024]{1,0:T(8,128)(2,1)S(1)}, u32[]{:S(2)}, u32[]{:S(2)}) collective-permute-start(bf16[128,1024]{1,0:T(8,128)(2,1)} %tokens.3), channel_id=1, source_target_pairs={{0,128},{128,256},{256,384},{384,0},{1,129},{129,257},{257,385},{3... | collective-permute-start | bytes 786440 | tf_op jit(solution)/shard_map/ppermute | solution.py:131
  31.8 8.8 %collective-permute-start.1 = (bf16[128,1024]{1,0:T(8,128)(2,1)}, bf16[128,1024]{1,0:T(8,128)(2,1)S(1)}, u32[]{:S(2)}, u32[]{:S(2)}) collective-permute-start(bf16[128,1024]{1,0:T(8,128)(2,1)} %tokens.3), channel_id=1, source_target_pairs={{0,384},{128,0},{256,128},{384,256},{1,385},{129,1},{257,129},{385... | collective-permute-start | bytes 786440 | tf_op jit(solution)/shard_map/ppermute | solution.py:131
  35.2 10.0 %collective-permute-start.2 = (bf16[128,1024]{1,0:T(8,128)(2,1)}, bf16[128,1024]{1,0:T(8,128)(2,1)S(1)}, u32[]{:S(2)}, u32[]{:S(2)}) collective-permute-start(bf16[128,1024]{1,0:T(8,128)(2,1)} %tokens.3), channel_id=1, source_target_pairs={{0,256},{128,384},{256,0},{384,128},{1,257},{129,385},{257,1},{385... | collective-permute-start | bytes 786440 | tf_op jit(solution)/shard_map/ppermute | solution.py:131
  45.2 0.7 copy-start.6
  49.7 17.0 %collective-permute-start.3 = (bf16[256,1024]{1,0:T(8,128)(2,1)S(1)}, bf16[256,1024]{1,0:T(8,128)(2,1)S(1)}, u32[]{:S(2)}, u32[]{:S(2)}) collective-permute-start(bf16[256,1024]{1,0:T(8,128)(2,1)S(1)} %shard_map.83.rows), channel_id=1, source_target_pairs={{0,128},{128,256},{256,384},{384,0},{1,129},{129,257},{257,385},{3... | collective-permute-start | bytes 1572872 | tf_op jit(solution)/shard_map/ppermute | solution.py:131
  52.8 15.2 %collective-permute-start.4 = (bf16[256,1024]{1,0:T(8,128)(2,1)S(1)}, bf16[256,1024]{1,0:T(8,128)(2,1)S(1)}, u32[]{:S(2)}, u32[]{:S(2)}) collective-permute-start(bf16[256,1024]{1,0:T(8,128)(2,1)S(1)} %shard_map.83.rows), channel_id=1, source_target_pairs={{0,384},{128,0},{256,128},{384,256},{1,385},{129,1},{257,129},{385... | collective-permute-start | bytes 1572872 | tf_op jit(solution)/shard_map/ppermute | solution.py:131
  56.2 1.0 copy-start.7
  57.2 1.0 copy-start.4
  58.3 1.6 %copy-start.1 = (bf16[1,1024,1024]{2,1,0:T(8,128)(2,1)S(1)}, bf16[1,1024,1024]{2,1,0:T(8,128)(2,1)}, u32[]{:S(2)}) copy-start(bf16[1,1024,1024]{2,1,0:T(8,128)(2,1)} %weight_out.5) | copy-start | bytes 6291460
  68.0 17.2 %collective-permute-start.7 = (bf16[128,1024]{1,0:T(8,128)(2,1)S(1)}, bf16[128,1024]{1,0:T(8,128)(2,1)S(1)}, u32[]{:S(2)}, u32[]{:S(2)}) collective-permute-start(bf16[128,1024]{1,0:T(8,128)(2,1)S(1)} %slice.6), channel_id=1, source_target_pairs={{0,128},{128,256},{256,384},{384,0},{1,129},{129,257},{257,385},{3... | collective-permute-start | bytes 786440 | tf_op jit(solution)/shard_map/ppermute | solution.py:131
  71.6 13.7 %copy-start.2 = (bf16[1,1024,1024]{2,1,0:T(8,128)(2,1)S(1)}, bf16[1,1024,1024]{2,1,0:T(8,128)(2,1)}, u32[]{:S(2)}) copy-start(bf16[1,1024,1024]{2,1,0:T(8,128)(2,1)} %weight_out.5) | copy-start | bytes 6291460
  71.6 13.7 %collective-permute-start.8 = (bf16[128,1024]{1,0:T(8,128)(2,1)S(1)}, bf16[128,1024]{1,0:T(8,128)(2,1)S(1)}, u32[]{:S(2)}, u32[]{:S(2)}) collective-permute-start(bf16[128,1024]{1,0:T(8,128)(2,1)S(1)} %slice.7), channel_id=1, source_target_pairs={{0,384},{128,0},{256,128},{384,256},{1,385},{129,1},{257,129},{385... | collective-permute-start | bytes 786440 | tf_op jit(solution)/shard_map/ppermute | solution.py:131
  80.0 30.7 %collective-permute-start.5 = (bf16[256,1024]{1,0:T(8,128)(2,1)}, bf16[256,1024]{1,0:T(8,128)(2,1)S(1)}, u32[]{:S(2)}, u32[]{:S(2)}) collective-permute-start(bf16[256,1024]{1,0:T(8,128)(2,1)} %get-tuple-element.27), channel_id=1, source_target_pairs={{0,384},{128,0},{256,128},{384,256},{1,385},{129,1},{257,129},{385... | collective-permute-start | bytes 1572872 | tf_op jit(solution)/shard_map/ppermute | solution.py:131
  83.3 27.3 %collective-permute-start.6 = (bf16[256,1024]{1,0:T(8,128)(2,1)}, bf16[256,1024]{1,0:T(8,128)(2,1)}, u32[]{:S(2)}, u32[]{:S(2)}) collective-permute-start(bf16[256,1024]{1,0:T(8,128)(2,1)} %get-tuple-element.28), channel_id=1, source_target_pairs={{0,128},{128,256},{256,384},{384,0},{1,129},{129,257},{257,385},{3... | collective-permute-start | bytes 1572872 | tf_op jit(solution)/shard_map/ppermute | solution.py:131
  87.6 23.1 %collective-permute-start.9 = (bf16[256,1024]{1,0:T(8,128)(2,1)}, bf16[256,1024]{1,0:T(8,128)(2,1)S(1)}, u32[]{:S(2)}, u32[]{:S(2)}) collective-permute-start(bf16[256,1024]{1,0:T(8,128)(2,1)} %shard_map.87), channel_id=1, source_target_pairs={{0,256},{128,384},{256,0},{384,128},{1,257},{129,385},{257,1},{385... | collective-permute-start | bytes 1572872 | tf_op jit(solution)/shard_map/ppermute | solution.py:131
  110.7 21.8 %copy-start.10 = (bf16[1024]{0:T(1024)(128)(2,1)S(1)}, bf16[1024]{0:T(1024)(128)(2,1)}, u32[]{:S(2)}) copy-start(bf16[1024]{0:T(1024)(128)(2,1)} %param.11) | copy-start | bytes 6148
  110.7 30.9 %copy-start.5 = (bf16[128,1024]{1,0:T(8,128)(2,1)S(1)}, bf16[128,1024]{1,0:T(8,128)(2,1)}, u32[]{:S(2)}) copy-start(bf16[128,1024]{1,0:T(8,128)(2,1)} %get-tuple-element.39.own) | copy-start | bytes 786436
  110.7 30.9 %copy-start.9 = (f32[128]{0:T(128)S(1)}, f32[128]{0:T(128)}, u32[]{:S(2)}) copy-start(f32[128]{0:T(128)} %param.10) | copy-start | bytes 1540
  112.9 31.3 %copy-start.8 = (s32[128,1]{0,1:T(1,128)S(1)}, s32[128,1]{0,1:T(1,128)}, u32[]{:S(2)}) copy-start(s32[128,1]{0,1:T(1,128)} %param.9) | copy-start | bytes 1540
  112.9 31.3 %all-to-all-start.1 = ((bf16[128,2,1024]{2,1,0:T(2,128)(2,1)}), bf16[128,2,1024]{2,1,0:T(2,128)(2,1)S(1)}, u32[]{:S(2)}, u32[]{:S(2)}) async-start(bf16[128,2,1024]{2,1,0:T(2,128)(2,1)} %shard_map.89), calls=%async_computation.1 | async-start | bytes 1048576 | tf_op jit(solution)/shard_map/all_to_all | solution.py:135
  123.6 9.0 %collective-permute-start.10 = (bf16[128,1024]{1,0:T(8,128)(2,1)}, bf16[128,1024]{1,0:T(8,128)(2,1)S(1)}, u32[]{:S(2)}, u32[]{:S(2)}) collective-permute-start(bf16[128,1024]{1,0:T(8,128)(2,1)} %get-tuple-element.36), channel_id=1, source_target_pairs={{0,384},{128,0},{256,128},{384,256},{1,385},{129,1},{257,129},{385... | collective-permute-start | bytes 786440 | tf_op jit(solution)/shard_map/ppermute | solution.py:131
  126.7 10.7 %collective-permute-start.11 = (bf16[128,1024]{1,0:T(8,128)(2,1)}, bf16[128,1024]{1,0:T(8,128)(2,1)S(1)}, u32[]{:S(2)}, u32[]{:S(2)}) collective-permute-start(bf16[128,1024]{1,0:T(8,128)(2,1)} %get-tuple-element.37), channel_id=1, source_target_pairs={{0,128},{128,256},{256,384},{384,0},{1,129},{129,257},{257,385},{3... | collective-permute-start | bytes 786440 | tf_op jit(solution)/shard_map/ppermute | solution.py:131
  128.9 12.6 %collective-permute-start.12 = (bf16[128,1024]{1,0:T(8,128)(2,1)}, bf16[128,1024]{1,0:T(8,128)(2,1)S(1)}, u32[]{:S(2)}, u32[]{:S(2)}) collective-permute-start(bf16[128,1024]{1,0:T(8,128)(2,1)} %get-tuple-element.38), channel_id=1, source_target_pairs={{0,256},{128,384},{256,0},{384,128},{1,257},{129,385},{257,1},{385... | collective-permute-start | bytes 786440 | tf_op jit(solution)/shard_map/ppermute | solution.py:131
Sparse Core Ops, SparseCore 0:
  10.5 94.3 all-gather.1

commit v5 on v4

--- a/solution.py
+++ b/solution.py
@@ -75,12 +75,14 @@
         out[place * count : (place + 1) * count, :] = rows[...]
 
 
-def residual_kernel(rows, pair, *outs):
+def residual_kernel(me, rows, pair, out):
     hidden = pair.shape[1] // 2
     part = products(rows[...], pair[:, :hidden], pair[:, hidden:], 1)
-    count = part.shape[0] // len(outs)
-    for place, out in enumerate(outs):
-        out[...] = part[place * count : (place + 1) * count, :]
+    steps = (1, 3, 2, 0)
+    count = part.shape[0] // len(steps)
+    for place, step in enumerate(steps):
+        group = lax.rem(me[0] + len(steps) - step, len(steps))
+        out[pl.ds(pl.multiple_of(group * count, count), count), :] = part[place * count : (place + 1) * count, :]
 
 
 def sum_kernel(own, left, right, far, out):
@@ -89,14 +91,12 @@
     out[...] = total.astype(jnp.bfloat16).reshape(out.shape)
 
 
-def scale_kernel(left, right, far, own, tokens, weight, gate, out):
-    model = own.shape[1]
-    res = left[...].astype(jnp.float32) + right[...].astype(jnp.float32)
-    res = res + far[...].astype(jnp.float32) + own[...].astype(jnp.float32)
+def scale_kernel(res, tokens, weight, gate, out):
+    model = res.shape[1]
     logit = jnp.sum(tokens[...].astype(jnp.float32) * weight[...].astype(jnp.float32), axis=1, keepdims=True)
     coef = 1.0 / (1.0 + jnp.exp(-logit))
     gates = jnp.transpose(jnp.broadcast_to(gate[...], (128, gate.shape[1])))
-    out[:, :model] = coef * res
+    out[:, :model] = coef * res[...].astype(jnp.float32)
     out[:, model:] = (1.0 - coef) * gates
 
 
@@ -178,21 +178,25 @@
     )
     left, right, far_back = shifted(near_left, 3), shifted(near_right, 1), shifted(far, 2)
 
-    res_parts = call(
+    me = lax.axis_index("grp").astype(jnp.int32).reshape(1)
+    res_part = call(
         residual_kernel,
-        (after(whole_rows, far), res_all),
-        (row_count, model),
+        (me, after(whole_rows, far), res_all),
+        whole_rows.shape,
         cost(groups * row_count, model, hidden),
-        count=groups,
         params=WHOLE,
     )
-    total = call(sum_kernel, (own, left, after(right, res_parts), far_back), (experts, capacity, model))
-    res_parts = after(res_parts, total)
-    res_parts = [shifted(part, step) for part, step in zip(res_parts, (3, 1, 2))] + [res_parts[3]]
+    res_out = lax.psum_scatter(res_part, "grp", scatter_dimension=0, tiled=True)
+    total = call(
+        sum_kernel,
+        (own, left, after(right, res_part), far_back),
+        (experts, capacity, model),
+        cost(64 * slots, model, hidden),
+    )
     returned = across(total, "ep")
     scaled = call(
         scale_kernel,
-        (*res_parts, tokens, coef_weight.reshape(1, model), gate_prob.reshape(1, row_count)),
+        (res_out, tokens, coef_weight.reshape(1, model), gate_prob.reshape(1, row_count)),
         (row_count, model + 128),
         dtype=jnp.float32,
     )

time: 153 us -> 153 us (level)
  starting transfers between devices: 69.9 us -> 61.2 us
  waiting for transfers between devices: 42.7 us -> 51.2 us
    reduce_scatter x0 -> x1, waiting for transfers between devices: none -> 10.9 us  [local(): res_out = lax.psum_scatter(res_part, 'grp', scatter_dimension=0, tiled=True)]
    ppermute x13 -> x10, waiting for transfers between devices: 22.3 us -> 13.2 us  [shifted(): lax.ppermute(value, 'grp', [(i, (i + step) % size) for i in range(size)])]
    ppermute x13 -> x10, starting transfers between devices: 40.6 us -> 31.9 us  [shifted(): lax.ppermute(value, 'grp', [(i, (i + step) % size) for i in range(size)])]
    all_to_all x2, waiting for transfers between devices: 6.25 us -> 12.2 us  [across(): return lax.all_to_all(value, axis, split_axis=0, concat_axis=0, tiled=True)]
  transfers between devices with their start and end apart: 16 -> 14, of which waited for: 11 -> 9; matrix products, arithmetic and copies ran while one was open for 0% -> 0% of each run, Pallas kernels for 11% -> 12%
where the time goes in v5:
time: 153 us; the launch traced here: 152 us
  starting transfers between devices  61.2 us (40%)
  waiting for transfers between devices  51.2 us (33%)
  Pallas kernels  19.7 us (13%)
  between operations  13.7 us (9%)
  local copies, waits for them, and re-layouts  5.24 us (3%)
    ppermute x10, starting transfers between devices, shifted(): lax.ppermute(value, 'grp', [(i, (i + step) % size) for i in range(size)])  31.9 us
    all_to_all x2, starting transfers between devices, across(): return lax.all_to_all(value, axis, split_axis=0, concat_axis=0, tiled=True)  29.2 us
    pallas_call x10, Pallas kernels, call(): pl.pallas_call(kernel, grid=(1,), in_specs=[SMEM if value.ndim == 1 else...  19.7 us
    all_gather x1, waiting for transfers between devices, local(): res_all = lax.all_gather(res_pair, 'ep', axis=0, tiled=True)  14.8 us
    ppermute x10, waiting for transfers between devices, shifted(): lax.ppermute(value, 'grp', [(i, (i + step) % size) for i in range(size)])  13.2 us
    all_to_all x2, waiting for transfers between devices, across(): return lax.all_to_all(value, axis, split_axis=0, concat_axis=0, tiled=True)  12.2 us
    reduce_scatter x1, waiting for transfers between devices, local(): res_out = lax.psum_scatter(res_part, 'grp', scatter_dimension=0, tiled=True)  10.9 us
    unnamed x22, local copies, waits for them, and re-layouts  5.19 us
  transfers between devices with their start and end apart: 14, of which 9 were waited for; matrix products, arithmetic and copies ran while one was open for 0% of the time, Pallas kernels for 12%

profile of v5, /device:TPU:1, one launch (start us, length us, event | category | flops | bytes accessed | tf_op | source)
XLA Modules:
  0.0 152.4 jit_solution(16407293930912357492)
XLA Ops:
  6.5 1.4 pad_maximum_fusion
  7.9 0.0 all-gather.2.cloned.1.call-update
  7.9 2.2 %shard_map.82 = bf16[128,2,1024]{2,1,0:T(2,128)(2,1)} custom-call(s32[1,128]{1,0:T(1,128)} %bitcast.4, bf16[128,1024]{1,0:T(8,128)(2,1)} %tokens.3), custom_call_target="tpu_custom_call" | custom-call | tf_op jit(solution)/shard_map/pallas_call | solution.py:117
  10.1 18.5 %all-to-all-start = ((bf16[128,2,1024]{2,1,0:T(2,128)(2,1)}), bf16[128,2,1024]{2,1,0:T(2,128)(2,1)S(1)}, u32[]{:S(2)}, u32[]{:S(2)}) async-start(bf16[128,2,1024]{2,1,0:T(2,128)(2,1)} %shard_map.82), calls=%async_computation | async-start | bytes 1048576 | tf_op jit(solution)/shard_map/all_to_all | solution.py:135
  28.7 0.0 reduce-scatter.2.cloned.1.call-start
  28.7 3.1 %collective-permute-start = (bf16[128,1024]{1,0:T(8,128)(2,1)}, bf16[128,1024]{1,0:T(8,128)(2,1)S(1)}, u32[]{:S(2)}, u32[]{:S(2)}) collective-permute-start(bf16[128,1024]{1,0:T(8,128)(2,1)} %tokens.3), channel_id=1, source_target_pairs={{0,128},{128,256},{256,384},{384,0},{1,129},{129,257},{257,385},{3... | collective-permute-start | bytes 786440 | tf_op jit(solution)/shard_map/ppermute | solution.py:131
  31.8 3.4 %collective-permute-start.1 = (bf16[128,1024]{1,0:T(8,128)(2,1)}, bf16[128,1024]{1,0:T(8,128)(2,1)S(1)}, u32[]{:S(2)}, u32[]{:S(2)}) collective-permute-start(bf16[128,1024]{1,0:T(8,128)(2,1)} %tokens.3), channel_id=1, source_target_pairs={{0,384},{128,0},{256,128},{384,256},{1,385},{129,1},{257,129},{385... | collective-permute-start | bytes 786440 | tf_op jit(solution)/shard_map/ppermute | solution.py:131
  35.2 3.4 %collective-permute-start.2 = (bf16[128,1024]{1,0:T(8,128)(2,1)}, bf16[128,1024]{1,0:T(8,128)(2,1)S(1)}, u32[]{:S(2)}, u32[]{:S(2)}) collective-permute-start(bf16[128,1024]{1,0:T(8,128)(2,1)} %tokens.3), channel_id=1, source_target_pairs={{0,256},{128,384},{256,0},{384,128},{1,257},{129,385},{257,1},{385... | collective-permute-start | bytes 786440 | tf_op jit(solution)/shard_map/ppermute | solution.py:131
  38.7 0.3 collective-permute-done.left
  39.0 1.7 %collective-permute-done.1.right = bf16[128,1024]{1,0:T(8,128)(2,1)S(1)} collective-permute-done((bf16[128,1024]{1,0:T(8,128)(2,1)}, bf16[128,1024]{1,0:T(8,128)(2,1)S(1)}, u32[]{:S(2)}, u32[]{:S(2)}) %collective-permute-start.1) | collective-permute-done | bytes 262176 | tf_op jit(solution)/shard_map/ppermute | solution.py:131
  40.7 4.5 %collective-permute-done.2.far = bf16[128,1024]{1,0:T(8,128)(2,1)S(1)} collective-permute-done((bf16[128,1024]{1,0:T(8,128)(2,1)}, bf16[128,1024]{1,0:T(8,128)(2,1)S(1)}, u32[]{:S(2)}, u32[]{:S(2)}) %collective-permute-start.2) | collective-permute-done | bytes 262176 | tf_op jit(solution)/shard_map/ppermute | solution.py:131
  45.2 0.7 copy-done.6
  45.9 3.7 %all-to-all-done.slots = bf16[128,2,1024]{2,1,0:T(2,128)(2,1)S(1)} async-done(((bf16[128,2,1024]{2,1,0:T(2,128)(2,1)}), bf16[128,2,1024]{2,1,0:T(2,128)(2,1)S(1)}, u32[]{:S(2)}, u32[]{:S(2)}) %all-to-all-start) | async-done | bytes 524320 | tf_op jit(solution)/shard_map/all_to_all | solution.py:135
  49.6 0.1 shard_map.83.rows
  49.7 3.1 %collective-permute-start.3 = (bf16[256,1024]{1,0:T(8,128)(2,1)S(1)}, bf16[256,1024]{1,0:T(8,128)(2,1)S(1)}, u32[]{:S(2)}, u32[]{:S(2)}) collective-permute-start(bf16[256,1024]{1,0:T(8,128)(2,1)S(1)} %shard_map.83.rows), channel_id=1, source_target_pairs={{0,128},{128,256},{256,384},{384,0},{1,129},{129,257},{257,385},{3... | collective-permute-start | bytes 1572872 | tf_op jit(solution)/shard_map/ppermute | solution.py:131
  52.8 3.4 %collective-permute-start.4 = (bf16[256,1024]{1,0:T(8,128)(2,1)S(1)}, bf16[256,1024]{1,0:T(8,128)(2,1)S(1)}, u32[]{:S(2)}, u32[]{:S(2)}) collective-permute-start(bf16[256,1024]{1,0:T(8,128)(2,1)S(1)} %shard_map.83.rows), channel_id=1, source_target_pairs={{0,384},{128,0},{256,128},{384,256},{1,385},{129,1},{257,129},{385... | collective-permute-start | bytes 1572872 | tf_op jit(solution)/shard_map/ppermute | solution.py:131
  56.2 0.0 copy-start.7
  56.2 0.9 copy-done.7
  57.2 0.1 shard_map.84.rows
  57.2 1.0 copy-done.4
  58.2 1.6 %copy-done.1 = bf16[1,1024,1024]{2,1,0:T(8,128)(2,1)S(1)} copy-done((bf16[1,1024,1024]{2,1,0:T(8,128)(2,1)S(1)}, bf16[1,1024,1024]{2,1,0:T(8,128)(2,1)}, u32[]{:S(2)}) %copy-start.1) | copy-done | bytes 2097176
  59.8 1.5 shard_map.85.own
  61.3 5.4 %collective-permute-done.3.left = bf16[256,1024]{1,0:T(8,128)(2,1)S(1)} collective-permute-done((bf16[256,1024]{1,0:T(8,128)(2,1)S(1)}, bf16[256,1024]{1,0:T(8,128)(2,1)S(1)}, u32[]{:S(2)}, u32[]{:S(2)}) %collective-permute-start.3) | collective-permute-done | bytes 524320 | tf_op jit(solution)/shard_map/ppermute | solution.py:131
  66.7 1.2 collective-permute-done.4.right
  68.0 3.6 %collective-permute-start.7 = (bf16[128,1024]{1,0:T(8,128)(2,1)S(1)}, bf16[128,1024]{1,0:T(8,128)(2,1)S(1)}, u32[]{:S(2)}, u32[]{:S(2)}) collective-permute-start(bf16[128,1024]{1,0:T(8,128)(2,1)S(1)} %slice.6), channel_id=1, source_target_pairs={{0,128},{128,256},{256,384},{384,0},{1,129},{129,257},{257,385},{3... | collective-permute-start | bytes 786440 | tf_op jit(solution)/shard_map/ppermute | solution.py:131
  71.6 0.0 copy-start.2
  71.6 3.5 %collective-permute-start.8 = (bf16[128,1024]{1,0:T(8,128)(2,1)S(1)}, bf16[128,1024]{1,0:T(8,128)(2,1)S(1)}, u32[]{:S(2)}, u32[]{:S(2)}) collective-permute-start(bf16[128,1024]{1,0:T(8,128)(2,1)S(1)} %slice.7), channel_id=1, source_target_pairs={{0,384},{128,0},{256,128},{384,256},{1,385},{129,1},{257,129},{385... | collective-permute-start | bytes 786440 | tf_op jit(solution)/shard_map/ppermute | solution.py:131
  75.1 5.0 %shard_map.86 = (bf16[256,1024]{1,0:T(8,128)(2,1)}, bf16[256,1024]{1,0:T(8,128)(2,1)}) custom-call(bf16[256,1024]{1,0:T(8,128)(2,1)S(1)} %collective-permute-done.3.left, bf16[256,1024]{1,0:T(8,128)(2,1)S(1)} %collective-permute-done.4.right, bf16[1,1024,1024]{2,1,0:T(8,128)(2,1)S(1)} %copy-done, bf16[1,1024,1024]{2,1,0:T(8,128)(2,1)} %weight_out.5), custom_call_target="tpu_custom_call" | custom-call | flops 2147483648 | bytes 6291456 | tf_op jit(solution)/shard_map/pallas_call | solution.py:117
  80.1 3.3 %collective-permute-start.5 = (bf16[256,1024]{1,0:T(8,128)(2,1)}, bf16[256,1024]{1,0:T(8,128)(2,1)}, u32[]{:S(2)}, u32[]{:S(2)}) collective-permute-start(bf16[256,1024]{1,0:T(8,128)(2,1)} %get-tuple-element.19), channel_id=1, source_target_pairs={{0,384},{128,0},{256,128},{384,256},{1,385},{129,1},{257,129},{385... | collective-permute-start | bytes 1572872 | tf_op jit(solution)/shard_map/ppermute | solution.py:131
  83.4 1.9 %collective-permute-start.6 = (bf16[256,1024]{1,0:T(8,128)(2,1)}, bf16[256,1024]{1,0:T(8,128)(2,1)}, u32[]{:S(2)}, u32[]{:S(2)}) collective-permute-start(bf16[256,1024]{1,0:T(8,128)(2,1)} %get-tuple-element.20), channel_id=1, source_target_pairs={{0,128},{128,256},{256,384},{384,0},{1,129},{129,257},{257,385},{3... | collective-permute-start | bytes 1572872 | tf_op jit(solution)/shard_map/ppermute | solution.py:131
  85.3 0.0 collective-permute-done.7.upper
  85.4 0.0 collective-permute-done.8.lower
  85.4 1.5 shard_map.87
  86.8 3.2 %collective-permute-start.9 = (bf16[256,1024]{1,0:T(8,128)(2,1)S(1)}, bf16[256,1024]{1,0:T(8,128)(2,1)S(1)}, u32[]{:S(2)}, u32[]{:S(2)}) collective-permute-start(bf16[256,1024]{1,0:T(8,128)(2,1)S(1)} %shard_map.87), channel_id=1, source_target_pairs={{0,256},{128,384},{256,0},{384,128},{1,257},{129,385},{257,1},{385... | collective-permute-start | bytes 1572872 | tf_op jit(solution)/shard_map/ppermute | solution.py:131
  90.0 14.8 %all-gather.2.cloned.1.call-done.pair = bf16[1024,2048]{1,0:T(8,128)(2,1)} async-done(((bf16[8,2048]{1,0:T(8,128)(2,1)}), bf16[1024,2048]{1,0:T(8,128)(2,1)}) %all-gather.2.cloned.1.call-update) | async-done | bytes 4194320 | tf_op jit(solution)/shard_map/all_gather | solution.py:151
  104.9 5.9 %shard_map.88 = bf16[512,1024]{1,0:T(8,128)(2,1)} custom-call(s32[1]{0:T(128)} %bitcast.1.me, bf16[512,1024]{1,0:T(8,128)(2,1)} %copy-done.4, bf16[1024,2048]{1,0:T(8,128)(2,1)} %all-gather.2.cloned.1.call-done.pair), custom_call_target="tpu_custom_call" | custom-call | flops 2147483648 | bytes 6291456 | tf_op jit(solution)/shard_map/pallas_call | solution.py:117
  110.8 0.0 reduce-scatter.2.cloned.1.call-update
  110.8 0.0 copy-start.10
  110.8 0.0 copy-start.9
  110.9 0.0 collective-permute-done.5.left
  110.9 0.0 collective-permute-done.9.far
  110.9 2.3 %shard_map.89 = bf16[128,2,1024]{2,1,0:T(2,128)(2,1)} custom-call(bf16[256,1024]{1,0:T(8,128)(2,1)S(1)} %shard_map.85.own, bf16[256,1024]{1,0:T(8,128)(2,1)} %collective-permute-done.5.left, bf16[256,1024]{1,0:T(8,128)(2,1)} %collective-permute-done.6.right, bf16[256,1024]{1,0:T(8,128)(2,1)S(1)} %collective-permute-done.9.far), custom_call_target="tpu_custom_call" | custom-call | flops 68719476736 | bytes 71303168 | tf_op jit(solution)/shard_map/pallas_call | solution.py:117
  113.2 10.7 %all-to-all-start.1 = ((bf16[128,2,1024]{2,1,0:T(2,128)(2,1)}), bf16[128,2,1024]{2,1,0:T(2,128)(2,1)S(1)}, u32[]{:S(2)}, u32[]{:S(2)}) async-start(bf16[128,2,1024]{2,1,0:T(2,128)(2,1)} %shard_map.89), calls=%async_computation.1 | async-start | bytes 1048576 | tf_op jit(solution)/shard_map/all_to_all | solution.py:135
  123.9 10.9 %reduce-scatter.2.cloned.1.call-done.res = bf16[128,1024]{1,0:T(8,128)(2,1)} async-done(((bf16[512,1024]{1,0:T(8,128)(2,1)}), bf16[128,1024]{1,0:T(8,128)(2,1)}) %reduce-scatter.2.cloned.1.call-update) | async-done | bytes 262160 | tf_op jit(solution)/shard_map/reduce_scatter | solution.py:189
  134.9 0.9 copy-done.5
  135.8 0.2 shard_map.90.scaled
  136.0 8.5 %all-to-all-done.1.slots = bf16[128,2,1024]{2,1,0:T(2,128)(2,1)S(1)} async-done(((bf16[128,2,1024]{2,1,0:T(2,128)(2,1)}), bf16[128,2,1024]{2,1,0:T(2,128)(2,1)S(1)}, u32[]{:S(2)}, u32[]{:S(2)}) %all-to-all-start.1) | async-done | bytes 524320 | tf_op jit(solution)/shard_map/all_to_all | solution.py:135
  144.5 1.1 shard_map.91
  (18 shorter events, 0.1 us)
Async XLA Ops:
  6.5 49.7 %copy-start.3 = (bf16[128,1024]{1,0:T(8,128)(2,1)S(1)}, bf16[128,1024]{1,0:T(8,128)(2,1)}, u32[]{:S(2)}) copy-start(bf16[128,1024]{1,0:T(8,128)(2,1)} %tokens.3) | copy-start | bytes 786436
  6.5 98.3 %all-gather.2.cloned.1.call-start = ((), (), s32[]{:S(2)}) async-start(), calls=%async_computation.3 | async-start | bytes 4227072 | tf_op jit(solution)/shard_map/all_gather | solution.py:151
  10.1 48.1 %copy-start = (bf16[1,1024,1024]{2,1,0:T(8,128)(2,1)S(1)}, bf16[1,1024,1024]{2,1,0:T(8,128)(2,1)}, u32[]{:S(2)}) copy-start(bf16[1,1024,1024]{2,1,0:T(8,128)(2,1)} %weight_in.5) | copy-start | bytes 6291460
  10.1 39.5 %all-to-all-start = ((bf16[128,2,1024]{2,1,0:T(2,128)(2,1)}), bf16[128,2,1024]{2,1,0:T(2,128)(2,1)S(1)}, u32[]{:S(2)}, u32[]{:S(2)}) async-start(bf16[128,2,1024]{2,1,0:T(2,128)(2,1)} %shard_map.82), calls=%async_computation | async-start | bytes 1048576 | tf_op jit(solution)/shard_map/all_to_all | solution.py:135
  28.7 106.2 %reduce-scatter.2.cloned.1.call-start = ((), (), s32[]{:S(2)}) async-start(), calls=%async_computation.4 | async-start | bytes 1310720 | tf_op jit(solution)/shard_map/reduce_scatter | solution.py:189
  28.7 10.2 %collective-permute-start = (bf16[128,1024]{1,0:T(8,128)(2,1)}, bf16[128,1024]{1,0:T(8,128)(2,1)S(1)}, u32[]{:S(2)}, u32[]{:S(2)}) collective-permute-start(bf16[128,1024]{1,0:T(8,128)(2,1)} %tokens.3), channel_id=1, source_target_pairs={{0,128},{128,256},{256,384},{384,0},{1,129},{129,257},{257,385},{3... | collective-permute-start | bytes 786440 | tf_op jit(solution)/shard_map/ppermute | solution.py:131
  31.8 8.8 %collective-permute-start.1 = (bf16[128,1024]{1,0:T(8,128)(2,1)}, bf16[128,1024]{1,0:T(8,128)(2,1)S(1)}, u32[]{:S(2)}, u32[]{:S(2)}) collective-permute-start(bf16[128,1024]{1,0:T(8,128)(2,1)} %tokens.3), channel_id=1, source_target_pairs={{0,384},{128,0},{256,128},{384,256},{1,385},{129,1},{257,129},{385... | collective-permute-start | bytes 786440 | tf_op jit(solution)/shard_map/ppermute | solution.py:131
  35.2 10.0 %collective-permute-start.2 = (bf16[128,1024]{1,0:T(8,128)(2,1)}, bf16[128,1024]{1,0:T(8,128)(2,1)S(1)}, u32[]{:S(2)}, u32[]{:S(2)}) collective-permute-start(bf16[128,1024]{1,0:T(8,128)(2,1)} %tokens.3), channel_id=1, source_target_pairs={{0,256},{128,384},{256,0},{384,128},{1,257},{129,385},{257,1},{385... | collective-permute-start | bytes 786440 | tf_op jit(solution)/shard_map/ppermute | solution.py:131
  45.2 0.7 copy-start.6
  49.7 17.0 %collective-permute-start.3 = (bf16[256,1024]{1,0:T(8,128)(2,1)S(1)}, bf16[256,1024]{1,0:T(8,128)(2,1)S(1)}, u32[]{:S(2)}, u32[]{:S(2)}) collective-permute-start(bf16[256,1024]{1,0:T(8,128)(2,1)S(1)} %shard_map.83.rows), channel_id=1, source_target_pairs={{0,128},{128,256},{256,384},{384,0},{1,129},{129,257},{257,385},{3... | collective-permute-start | bytes 1572872 | tf_op jit(solution)/shard_map/ppermute | solution.py:131
  52.8 15.1 %collective-permute-start.4 = (bf16[256,1024]{1,0:T(8,128)(2,1)S(1)}, bf16[256,1024]{1,0:T(8,128)(2,1)S(1)}, u32[]{:S(2)}, u32[]{:S(2)}) collective-permute-start(bf16[256,1024]{1,0:T(8,128)(2,1)S(1)} %shard_map.83.rows), channel_id=1, source_target_pairs={{0,384},{128,0},{256,128},{384,256},{1,385},{129,1},{257,129},{385... | collective-permute-start | bytes 1572872 | tf_op jit(solution)/shard_map/ppermute | solution.py:131
  56.2 1.0 copy-start.7
  57.2 1.0 copy-start.4
  58.2 1.6 %copy-start.1 = (bf16[1,1024,1024]{2,1,0:T(8,128)(2,1)S(1)}, bf16[1,1024,1024]{2,1,0:T(8,128)(2,1)}, u32[]{:S(2)}) copy-start(bf16[1,1024,1024]{2,1,0:T(8,128)(2,1)} %weight_out.5) | copy-start | bytes 6291460
  68.0 17.4 %collective-permute-start.7 = (bf16[128,1024]{1,0:T(8,128)(2,1)S(1)}, bf16[128,1024]{1,0:T(8,128)(2,1)S(1)}, u32[]{:S(2)}, u32[]{:S(2)}) collective-permute-start(bf16[128,1024]{1,0:T(8,128)(2,1)S(1)} %slice.6), channel_id=1, source_target_pairs={{0,128},{128,256},{256,384},{384,0},{1,129},{129,257},{257,385},{3... | collective-permute-start | bytes 786440 | tf_op jit(solution)/shard_map/ppermute | solution.py:131
  71.6 13.8 %copy-start.2 = (bf16[1,1024,1024]{2,1,0:T(8,128)(2,1)S(1)}, bf16[1,1024,1024]{2,1,0:T(8,128)(2,1)}, u32[]{:S(2)}) copy-start(bf16[1,1024,1024]{2,1,0:T(8,128)(2,1)} %weight_out.5) | copy-start | bytes 6291460
  71.6 13.8 %collective-permute-start.8 = (bf16[128,1024]{1,0:T(8,128)(2,1)S(1)}, bf16[128,1024]{1,0:T(8,128)(2,1)S(1)}, u32[]{:S(2)}, u32[]{:S(2)}) collective-permute-start(bf16[128,1024]{1,0:T(8,128)(2,1)S(1)} %slice.7), channel_id=1, source_target_pairs={{0,384},{128,0},{256,128},{384,256},{1,385},{129,1},{257,129},{385... | collective-permute-start | bytes 786440 | tf_op jit(solution)/shard_map/ppermute | solution.py:131
  80.1 30.8 %collective-permute-start.5 = (bf16[256,1024]{1,0:T(8,128)(2,1)}, bf16[256,1024]{1,0:T(8,128)(2,1)}, u32[]{:S(2)}, u32[]{:S(2)}) collective-permute-start(bf16[256,1024]{1,0:T(8,128)(2,1)} %get-tuple-element.19), channel_id=1, source_target_pairs={{0,384},{128,0},{256,128},{384,256},{1,385},{129,1},{257,129},{385... | collective-permute-start | bytes 1572872 | tf_op jit(solution)/shard_map/ppermute | solution.py:131
  83.4 27.4 %collective-permute-start.6 = (bf16[256,1024]{1,0:T(8,128)(2,1)}, bf16[256,1024]{1,0:T(8,128)(2,1)}, u32[]{:S(2)}, u32[]{:S(2)}) collective-permute-start(bf16[256,1024]{1,0:T(8,128)(2,1)} %get-tuple-element.20), channel_id=1, source_target_pairs={{0,128},{128,256},{256,384},{384,0},{1,129},{129,257},{257,385},{3... | collective-permute-start | bytes 1572872 | tf_op jit(solution)/shard_map/ppermute | solution.py:131
  86.8 24.0 %collective-permute-start.9 = (bf16[256,1024]{1,0:T(8,128)(2,1)S(1)}, bf16[256,1024]{1,0:T(8,128)(2,1)S(1)}, u32[]{:S(2)}, u32[]{:S(2)}) collective-permute-start(bf16[256,1024]{1,0:T(8,128)(2,1)S(1)} %shard_map.87), channel_id=1, source_target_pairs={{0,256},{128,384},{256,0},{384,128},{1,257},{129,385},{257,1},{385... | collective-permute-start | bytes 1572872 | tf_op jit(solution)/shard_map/ppermute | solution.py:131
  110.8 13.1 %copy-start.10 = (bf16[1024]{0:T(1024)(128)(2,1)S(1)}, bf16[1024]{0:T(1024)(128)(2,1)}, u32[]{:S(2)}) copy-start(bf16[1024]{0:T(1024)(128)(2,1)} %param.11) | copy-start | bytes 6148
  110.8 24.0 %copy-start.9 = (f32[128]{0:T(128)S(1)}, f32[128]{0:T(128)}, u32[]{:S(2)}) copy-start(f32[128]{0:T(128)} %param.10) | copy-start | bytes 1540
  113.2 31.3 %copy-start.8 = (s32[128,1]{0,1:T(1,128)S(1)}, s32[128,1]{0,1:T(1,128)}, u32[]{:S(2)}) copy-start(s32[128,1]{0,1:T(1,128)} %param.9) | copy-start | bytes 1540
  113.2 31.3 %all-to-all-start.1 = ((bf16[128,2,1024]{2,1,0:T(2,128)(2,1)}), bf16[128,2,1024]{2,1,0:T(2,128)(2,1)S(1)}, u32[]{:S(2)}, u32[]{:S(2)}) async-start(bf16[128,2,1024]{2,1,0:T(2,128)(2,1)} %shard_map.89), calls=%async_computation.1 | async-start | bytes 1048576 | tf_op jit(solution)/shard_map/all_to_all | solution.py:135
  134.9 1.0 copy-start.5
Sparse Core Ops, SparseCore 0:
  10.5 94.3 all-gather.1
  110.9 23.8 reduce-scatter.1

commit v6 on v5

--- a/solution.py
+++ b/solution.py
@@ -75,14 +75,45 @@
         out[place * count : (place + 1) * count, :] = rows[...]
 
 
-def residual_kernel(me, rows, pair, out):
-    hidden = pair.shape[1] // 2
-    part = products(rows[...], pair[:, :hidden], pair[:, hidden:], 1)
+def residual_kernel(me, rows, pair, out, held, weight_in, weight_out, made, sems):
     steps = (1, 3, 2, 0)
-    count = part.shape[0] // len(steps)
-    for place, step in enumerate(steps):
-        group = lax.rem(me[0] + len(steps) - step, len(steps))
-        out[pl.ds(pl.multiple_of(group * count, count), count), :] = part[place * count : (place + 1) * count, :]
+    cuts, model = 4, weight_in.shape[0]
+    count, width, hidden = held.shape[0] // len(steps), model // cuts, weight_in.shape[1]
+    blocks = [slice(k * width, (k + 1) * width) for k in range(cuts)]
+    rows_in = pltpu.make_async_copy(rows, held, sems.at[0])
+    first = [
+        pltpu.make_async_copy(pair.at[cut, :hidden], weight_in.at[cut, :], sems.at[1 + k])
+        for k, cut in enumerate(blocks)
+    ]
+    second = pltpu.make_async_copy(pair.at[:, hidden:], weight_out, sems.at[1 + cuts])
+    for copy in (rows_in, *first, second):
+        copy.start()
+    rows_in.wait()
+    product = None
+    for cut, copy in zip(blocks, first):
+        copy.wait()
+        term = jnp.dot(held[:, cut], weight_in[cut, :], preferred_element_type=jnp.float32)
+        product = term if product is None else product + term
+    units = jax.nn.gelu(product, approximate=True).astype(jnp.bfloat16)
+    second.wait()
+    sent = []
+    for side in range(2):
+        part = lax.dot_general(
+            units[side * 2 * count : (side + 1) * 2 * count, :],
+            weight_out[...],
+            (((1,), (1,)), ((), ())),
+            preferred_element_type=jnp.float32,
+        ).astype(jnp.bfloat16)
+        for place in (2 * side, 2 * side + 1):
+            own = slice(place * count, (place + 1) * count)
+            made[own, :] = part[(place - 2 * side) * count : (place - 2 * side + 1) * count, :]
+            group = lax.rem(me[0] + len(steps) - steps[place], len(steps))
+            target = out.at[pl.ds(pl.multiple_of(group * count, count), count), :]
+            copy = pltpu.make_async_copy(made.at[own, :], target, sems.at[2 + cuts + place])
+            copy.start()
+            sent.append(copy)
+    for copy in sent:
+        copy.wait()
 
 
 def sum_kernel(own, left, right, far, out):
@@ -179,20 +210,33 @@
     left, right, far_back = shifted(near_left, 3), shifted(near_right, 1), shifted(far, 2)
 
     me = lax.axis_index("grp").astype(jnp.int32).reshape(1)
-    res_part = call(
+    anywhere = pl.BlockSpec(memory_space=pl.ANY)
+    res_part = pl.pallas_call(
         residual_kernel,
-        (me, after(whole_rows, far), res_all),
-        whole_rows.shape,
-        cost(groups * row_count, model, hidden),
-        params=WHOLE,
-    )
+        in_specs=[SMEM, anywhere, anywhere],
+        out_specs=anywhere,
+        out_shape=jax.ShapeDtypeStruct(whole_rows.shape, jnp.bfloat16),
+        scratch_shapes=[
+            pltpu.VMEM(whole_rows.shape, jnp.bfloat16),
+            pltpu.VMEM((model, hidden), jnp.bfloat16),
+            pltpu.VMEM((model, hidden), jnp.bfloat16),
+            pltpu.VMEM(whole_rows.shape, jnp.bfloat16),
+            pltpu.SemaphoreType.DMA((10,)),
+        ],
+        compiler_params=WHOLE,
+        cost_estimate=cost(groups * row_count, model, hidden),
+    )(me, after(whole_rows, far), res_all)
     res_out = lax.psum_scatter(res_part, "grp", scatter_dimension=0, tiled=True)
-    total = call(
+    row_block = pl.BlockSpec((slots // 2, model), lambda i: (i, 0))
+    total = pl.pallas_call(
         sum_kernel,
-        (own, left, after(right, res_part), far_back),
-        (experts, capacity, model),
-        cost(64 * slots, model, hidden),
-    )
+        grid=(2,),
+        in_specs=[row_block] * 4,
+        out_specs=pl.BlockSpec((experts // 2, capacity, model), lambda i: (i, 0, 0)),
+        out_shape=jax.ShapeDtypeStruct((experts, capacity, model), jnp.bfloat16),
+        compiler_params=PARAMS,
+        cost_estimate=cost(64 * slots, model, hidden),
+    )(own, left, after(right, res_part), far_back)
     returned = across(total, "ep")
     scaled = call(
         scale_kernel,

time: 153 us -> 153 us (level)
    pallas_call x10 -> x8, Pallas kernels: 19.7 us -> 11.5 us  [call(): pl.pallas_call(kernel, grid=(1,), in_specs=[SMEM if value.ndim == 1 else...]
    pallas_call x0 -> x2, Pallas kernels: none -> 7.5 us  [the longest x1 5.39 us: local(): pl.pallas_call(residual_kernel, in_specs=[SMEM, anywhere, anywhere], out_...]
where the time goes in v6:
time: 153 us; the launch traced here: 152 us
  starting transfers between devices  61.7 us (40%)
  waiting for transfers between devices  51.2 us (33%)
  Pallas kernels  19 us (12%)
  between operations  13.7 us (9%)
  local copies, waits for them, and re-layouts  5.24 us (3%)
    ppermute x10, starting transfers between devices, shifted(): lax.ppermute(value, 'grp', [(i, (i + step) % size) for i in range(size)])  31.9 us
    all_to_all x2, starting transfers between devices, across(): return lax.all_to_all(value, axis, split_axis=0, concat_axis=0, tiled=True)  29.8 us
    all_gather x1, waiting for transfers between devices, local(): res_all = lax.all_gather(res_pair, 'ep', axis=0, tiled=True)  14.8 us
    ppermute x10, waiting for transfers between devices, shifted(): lax.ppermute(value, 'grp', [(i, (i + step) % size) for i in range(size)])  13.2 us
    all_to_all x2, waiting for transfers between devices, across(): return lax.all_to_all(value, axis, split_axis=0, concat_axis=0, tiled=True)  13 us
    pallas_call x8, Pallas kernels, call(): pl.pallas_call(kernel, grid=(1,), in_specs=[SMEM if value.ndim == 1 else...  11.5 us
    reduce_scatter x1, waiting for transfers between devices, local(): res_out = lax.psum_scatter(res_part, 'grp', scatter_dimension=0, tiled=True)  10.1 us
    pallas_call x1, Pallas kernels, local(): pl.pallas_call(residual_kernel, in_specs=[SMEM, anywhere, anywhere], out_...  5.39 us
  transfers between devices with their start and end apart: 14, of which 9 were waited for; matrix products, arithmetic and copies ran while one was open for 0% of the time, Pallas kernels for 12%

profile of v6, /device:TPU:1, one launch (start us, length us, event | category | flops | bytes accessed | tf_op | source)
XLA Modules:
  0.0 152.2 jit_solution(17484927851659948194)
XLA Ops:
  6.5 1.4 pad_maximum_fusion
  7.9 0.0 all-gather.2.cloned.1.call-update
  7.9 2.2 %shard_map.82 = bf16[128,2,1024]{2,1,0:T(2,128)(2,1)} custom-call(s32[1,128]{1,0:T(1,128)} %bitcast.4, bf16[128,1024]{1,0:T(8,128)(2,1)} %tokens.3), custom_call_target="tpu_custom_call" | custom-call | tf_op jit(solution)/shard_map/pallas_call | solution.py:148
  10.1 18.5 %all-to-all-start = ((bf16[128,2,1024]{2,1,0:T(2,128)(2,1)}), bf16[128,2,1024]{2,1,0:T(2,128)(2,1)S(1)}, u32[]{:S(2)}, u32[]{:S(2)}) async-start(bf16[128,2,1024]{2,1,0:T(2,128)(2,1)} %shard_map.82), calls=%async_computation | async-start | bytes 1048576 | tf_op jit(solution)/shard_map/all_to_all | solution.py:166
  28.7 0.0 reduce-scatter.2.cloned.1.call-start
  28.7 3.1 %collective-permute-start = (bf16[128,1024]{1,0:T(8,128)(2,1)}, bf16[128,1024]{1,0:T(8,128)(2,1)S(1)}, u32[]{:S(2)}, u32[]{:S(2)}) collective-permute-start(bf16[128,1024]{1,0:T(8,128)(2,1)} %tokens.3), channel_id=1, source_target_pairs={{0,128},{128,256},{256,384},{384,0},{1,129},{129,257},{257,385},{3... | collective-permute-start | bytes 786440 | tf_op jit(solution)/shard_map/ppermute | solution.py:162
  31.8 3.4 %collective-permute-start.1 = (bf16[128,1024]{1,0:T(8,128)(2,1)}, bf16[128,1024]{1,0:T(8,128)(2,1)S(1)}, u32[]{:S(2)}, u32[]{:S(2)}) collective-permute-start(bf16[128,1024]{1,0:T(8,128)(2,1)} %tokens.3), channel_id=1, source_target_pairs={{0,384},{128,0},{256,128},{384,256},{1,385},{129,1},{257,129},{385... | collective-permute-start | bytes 786440 | tf_op jit(solution)/shard_map/ppermute | solution.py:162
  35.2 3.4 %collective-permute-start.2 = (bf16[128,1024]{1,0:T(8,128)(2,1)}, bf16[128,1024]{1,0:T(8,128)(2,1)S(1)}, u32[]{:S(2)}, u32[]{:S(2)}) collective-permute-start(bf16[128,1024]{1,0:T(8,128)(2,1)} %tokens.3), channel_id=1, source_target_pairs={{0,256},{128,384},{256,0},{384,128},{1,257},{129,385},{257,1},{385... | collective-permute-start | bytes 786440 | tf_op jit(solution)/shard_map/ppermute | solution.py:162
  38.7 0.3 collective-permute-done.left
  39.0 1.7 %collective-permute-done.1.right = bf16[128,1024]{1,0:T(8,128)(2,1)S(1)} collective-permute-done((bf16[128,1024]{1,0:T(8,128)(2,1)}, bf16[128,1024]{1,0:T(8,128)(2,1)S(1)}, u32[]{:S(2)}, u32[]{:S(2)}) %collective-permute-start.1) | collective-permute-done | bytes 262176 | tf_op jit(solution)/shard_map/ppermute | solution.py:162
  40.7 4.5 %collective-permute-done.2.far = bf16[128,1024]{1,0:T(8,128)(2,1)S(1)} collective-permute-done((bf16[128,1024]{1,0:T(8,128)(2,1)}, bf16[128,1024]{1,0:T(8,128)(2,1)S(1)}, u32[]{:S(2)}, u32[]{:S(2)}) %collective-permute-start.2) | collective-permute-done | bytes 262176 | tf_op jit(solution)/shard_map/ppermute | solution.py:162
  45.2 0.7 copy-done.6
  45.9 3.7 %all-to-all-done.slots = bf16[128,2,1024]{2,1,0:T(2,128)(2,1)S(1)} async-done(((bf16[128,2,1024]{2,1,0:T(2,128)(2,1)}), bf16[128,2,1024]{2,1,0:T(2,128)(2,1)S(1)}, u32[]{:S(2)}, u32[]{:S(2)}) %all-to-all-start) | async-done | bytes 524320 | tf_op jit(solution)/shard_map/all_to_all | solution.py:166
  49.6 0.1 shard_map.83.rows
  49.7 3.1 %collective-permute-start.3 = (bf16[256,1024]{1,0:T(8,128)(2,1)S(1)}, bf16[256,1024]{1,0:T(8,128)(2,1)S(1)}, u32[]{:S(2)}, u32[]{:S(2)}) collective-permute-start(bf16[256,1024]{1,0:T(8,128)(2,1)S(1)} %shard_map.83.rows), channel_id=1, source_target_pairs={{0,128},{128,256},{256,384},{384,0},{1,129},{129,257},{257,385},{3... | collective-permute-start | bytes 1572872 | tf_op jit(solution)/shard_map/ppermute | solution.py:162
  52.8 3.4 %collective-permute-start.4 = (bf16[256,1024]{1,0:T(8,128)(2,1)S(1)}, bf16[256,1024]{1,0:T(8,128)(2,1)S(1)}, u32[]{:S(2)}, u32[]{:S(2)}) collective-permute-start(bf16[256,1024]{1,0:T(8,128)(2,1)S(1)} %shard_map.83.rows), channel_id=1, source_target_pairs={{0,384},{128,0},{256,128},{384,256},{1,385},{129,1},{257,129},{385... | collective-permute-start | bytes 1572872 | tf_op jit(solution)/shard_map/ppermute | solution.py:162
  56.2 0.0 copy-start.7
  56.2 0.9 copy-done.7
  57.2 0.1 shard_map.84.rows
  57.2 1.0 copy-done.4
  58.2 1.6 %copy-done.1 = bf16[1,1024,1024]{2,1,0:T(8,128)(2,1)S(1)} copy-done((bf16[1,1024,1024]{2,1,0:T(8,128)(2,1)S(1)}, bf16[1,1024,1024]{2,1,0:T(8,128)(2,1)}, u32[]{:S(2)}) %copy-start.1) | copy-done | bytes 2097176
  59.8 1.5 shard_map.85.own
  61.3 5.4 %collective-permute-done.3.left = bf16[256,1024]{1,0:T(8,128)(2,1)S(1)} collective-permute-done((bf16[256,1024]{1,0:T(8,128)(2,1)S(1)}, bf16[256,1024]{1,0:T(8,128)(2,1)S(1)}, u32[]{:S(2)}, u32[]{:S(2)}) %collective-permute-start.3) | collective-permute-done | bytes 524320 | tf_op jit(solution)/shard_map/ppermute | solution.py:162
  66.7 1.2 collective-permute-done.4.right
  68.0 3.6 %collective-permute-start.7 = (bf16[128,1024]{1,0:T(8,128)(2,1)S(1)}, bf16[128,1024]{1,0:T(8,128)(2,1)S(1)}, u32[]{:S(2)}, u32[]{:S(2)}) collective-permute-start(bf16[128,1024]{1,0:T(8,128)(2,1)S(1)} %slice.6), channel_id=1, source_target_pairs={{0,128},{128,256},{256,384},{384,0},{1,129},{129,257},{257,385},{3... | collective-permute-start | bytes 786440 | tf_op jit(solution)/shard_map/ppermute | solution.py:162
  71.6 0.0 copy-start.2
  71.6 3.5 %collective-permute-start.8 = (bf16[128,1024]{1,0:T(8,128)(2,1)S(1)}, bf16[128,1024]{1,0:T(8,128)(2,1)S(1)}, u32[]{:S(2)}, u32[]{:S(2)}) collective-permute-start(bf16[128,1024]{1,0:T(8,128)(2,1)S(1)} %slice.7), channel_id=1, source_target_pairs={{0,384},{128,0},{256,128},{384,256},{1,385},{129,1},{257,129},{385... | collective-permute-start | bytes 786440 | tf_op jit(solution)/shard_map/ppermute | solution.py:162
  75.1 5.0 %shard_map.86 = (bf16[256,1024]{1,0:T(8,128)(2,1)}, bf16[256,1024]{1,0:T(8,128)(2,1)}) custom-call(bf16[256,1024]{1,0:T(8,128)(2,1)S(1)} %collective-permute-done.3.left, bf16[256,1024]{1,0:T(8,128)(2,1)S(1)} %collective-permute-done.4.right, bf16[1,1024,1024]{2,1,0:T(8,128)(2,1)S(1)} %copy-done, bf16[1,1024,1024]{2,1,0:T(8,128)(2,1)} %weight_out.5), custom_call_target="tpu_custom_call" | custom-call | flops 2147483648 | bytes 6291456 | tf_op jit(solution)/shard_map/pallas_call | solution.py:148
  80.1 3.3 %collective-permute-start.5 = (bf16[256,1024]{1,0:T(8,128)(2,1)}, bf16[256,1024]{1,0:T(8,128)(2,1)}, u32[]{:S(2)}, u32[]{:S(2)}) collective-permute-start(bf16[256,1024]{1,0:T(8,128)(2,1)} %get-tuple-element.19), channel_id=1, source_target_pairs={{0,384},{128,0},{256,128},{384,256},{1,385},{129,1},{257,129},{385... | collective-permute-start | bytes 1572872 | tf_op jit(solution)/shard_map/ppermute | solution.py:162
  83.4 1.9 %collective-permute-start.6 = (bf16[256,1024]{1,0:T(8,128)(2,1)}, bf16[256,1024]{1,0:T(8,128)(2,1)}, u32[]{:S(2)}, u32[]{:S(2)}) collective-permute-start(bf16[256,1024]{1,0:T(8,128)(2,1)} %get-tuple-element.20), channel_id=1, source_target_pairs={{0,128},{128,256},{256,384},{384,0},{1,129},{129,257},{257,385},{3... | collective-permute-start | bytes 1572872 | tf_op jit(solution)/shard_map/ppermute | solution.py:162
  85.3 0.0 collective-permute-done.7.upper
  85.4 0.0 collective-permute-done.8.lower
  85.4 1.5 shard_map.87
  86.8 3.2 %collective-permute-start.9 = (bf16[256,1024]{1,0:T(8,128)(2,1)S(1)}, bf16[256,1024]{1,0:T(8,128)(2,1)S(1)}, u32[]{:S(2)}, u32[]{:S(2)}) collective-permute-start(bf16[256,1024]{1,0:T(8,128)(2,1)S(1)} %shard_map.87), channel_id=1, source_target_pairs={{0,256},{128,384},{256,0},{384,128},{1,257},{129,385},{257,1},{385... | collective-permute-start | bytes 1572872 | tf_op jit(solution)/shard_map/ppermute | solution.py:162
  90.0 14.8 %all-gather.2.cloned.1.call-done.pair = bf16[1024,2048]{1,0:T(8,128)(2,1)} async-done(((bf16[8,2048]{1,0:T(8,128)(2,1)}), bf16[1024,2048]{1,0:T(8,128)(2,1)}) %all-gather.2.cloned.1.call-update) | async-done | bytes 4194320 | tf_op jit(solution)/shard_map/all_gather | solution.py:182
  104.9 5.4 %shard_map.88 = bf16[512,1024]{1,0:T(8,128)(2,1)} custom-call(s32[1]{0:T(128)} %bitcast.1.me, bf16[512,1024]{1,0:T(8,128)(2,1)} %copy-done.4, bf16[1024,2048]{1,0:T(8,128)(2,1)} %all-gather.2.cloned.1.call-done.pair), custom_call_target="tpu_custom_call" | custom-call | flops 2147483648 | bytes 6291456 | tf_op jit(solution)/shard_map/pallas_call | solution.py:214
  110.3 0.0 reduce-scatter.2.cloned.1.call-update
  110.3 0.0 copy-start.10
  110.3 0.0 copy-start.9
  110.3 0.0 collective-permute-done.6.right
  110.3 0.0 collective-permute-done.9.far
  110.4 2.1 %shard_map.89 = bf16[128,2,1024]{2,1,0:T(2,128)(2,1)} custom-call(bf16[256,1024]{1,0:T(8,128)(2,1)S(1)} %shard_map.85.own, bf16[256,1024]{1,0:T(8,128)(2,1)} %collective-permute-done.5.left, bf16[256,1024]{1,0:T(8,128)(2,1)} %collective-permute-done.6.right, bf16[256,1024]{1,0:T(8,128)(2,1)S(1)} %collective-permute-done.9.far), custom_call_target="tpu_custom_call" | custom-call | flops 68719476736 | bytes 71303168 | tf_op jit(solution)/shard_map/pallas_call | solution.py:231
  112.5 11.2 %all-to-all-start.1 = ((bf16[128,2,1024]{2,1,0:T(2,128)(2,1)}), bf16[128,2,1024]{2,1,0:T(2,128)(2,1)S(1)}, u32[]{:S(2)}, u32[]{:S(2)}) async-start(bf16[128,2,1024]{2,1,0:T(2,128)(2,1)} %shard_map.89), calls=%async_computation.1 | async-start | bytes 1048576 | tf_op jit(solution)/shard_map/all_to_all | solution.py:166
  123.7 10.1 %reduce-scatter.2.cloned.1.call-done.res = bf16[128,1024]{1,0:T(8,128)(2,1)} async-done(((bf16[512,1024]{1,0:T(8,128)(2,1)}), bf16[128,1024]{1,0:T(8,128)(2,1)}) %reduce-scatter.2.cloned.1.call-update) | async-done | bytes 262160 | tf_op jit(solution)/shard_map/reduce_scatter | solution.py:229
  133.8 0.9 copy-done.5
  134.8 0.2 shard_map.90.scaled
  135.0 9.3 %all-to-all-done.1.slots = bf16[128,2,1024]{2,1,0:T(2,128)(2,1)S(1)} async-done(((bf16[128,2,1024]{2,1,0:T(2,128)(2,1)}), bf16[128,2,1024]{2,1,0:T(2,128)(2,1)S(1)}, u32[]{:S(2)}, u32[]{:S(2)}) %all-to-all-start.1) | async-done | bytes 524320 | tf_op jit(solution)/shard_map/all_to_all | solution.py:166
  144.3 1.1 shard_map.91
  (18 shorter events, 0.1 us)
Async XLA Ops:
  6.5 49.7 %copy-start.3 = (bf16[128,1024]{1,0:T(8,128)(2,1)S(1)}, bf16[128,1024]{1,0:T(8,128)(2,1)}, u32[]{:S(2)}) copy-start(bf16[128,1024]{1,0:T(8,128)(2,1)} %tokens.3) | copy-start | bytes 786436
  6.5 98.3 %all-gather.2.cloned.1.call-start = ((), (), s32[]{:S(2)}) async-start(), calls=%async_computation.3 | async-start | bytes 4227072 | tf_op jit(solution)/shard_map/all_gather | solution.py:182
  10.1 48.1 %copy-start = (bf16[1,1024,1024]{2,1,0:T(8,128)(2,1)S(1)}, bf16[1,1024,1024]{2,1,0:T(8,128)(2,1)}, u32[]{:S(2)}) copy-start(bf16[1,1024,1024]{2,1,0:T(8,128)(2,1)} %weight_in.5) | copy-start | bytes 6291460
  10.1 39.5 %all-to-all-start = ((bf16[128,2,1024]{2,1,0:T(2,128)(2,1)}), bf16[128,2,1024]{2,1,0:T(2,128)(2,1)S(1)}, u32[]{:S(2)}, u32[]{:S(2)}) async-start(bf16[128,2,1024]{2,1,0:T(2,128)(2,1)} %shard_map.82), calls=%async_computation | async-start | bytes 1048576 | tf_op jit(solution)/shard_map/all_to_all | solution.py:166
  28.7 105.2 %reduce-scatter.2.cloned.1.call-start = ((), (), s32[]{:S(2)}) async-start(), calls=%async_computation.4 | async-start | bytes 1310720 | tf_op jit(solution)/shard_map/reduce_scatter | solution.py:229
  28.7 10.2 %collective-permute-start = (bf16[128,1024]{1,0:T(8,128)(2,1)}, bf16[128,1024]{1,0:T(8,128)(2,1)S(1)}, u32[]{:S(2)}, u32[]{:S(2)}) collective-permute-start(bf16[128,1024]{1,0:T(8,128)(2,1)} %tokens.3), channel_id=1, source_target_pairs={{0,128},{128,256},{256,384},{384,0},{1,129},{129,257},{257,385},{3... | collective-permute-start | bytes 786440 | tf_op jit(solution)/shard_map/ppermute | solution.py:162
  31.8 8.8 %collective-permute-start.1 = (bf16[128,1024]{1,0:T(8,128)(2,1)}, bf16[128,1024]{1,0:T(8,128)(2,1)S(1)}, u32[]{:S(2)}, u32[]{:S(2)}) collective-permute-start(bf16[128,1024]{1,0:T(8,128)(2,1)} %tokens.3), channel_id=1, source_target_pairs={{0,384},{128,0},{256,128},{384,256},{1,385},{129,1},{257,129},{385... | collective-permute-start | bytes 786440 | tf_op jit(solution)/shard_map/ppermute | solution.py:162
  35.2 10.0 %collective-permute-start.2 = (bf16[128,1024]{1,0:T(8,128)(2,1)}, bf16[128,1024]{1,0:T(8,128)(2,1)S(1)}, u32[]{:S(2)}, u32[]{:S(2)}) collective-permute-start(bf16[128,1024]{1,0:T(8,128)(2,1)} %tokens.3), channel_id=1, source_target_pairs={{0,256},{128,384},{256,0},{384,128},{1,257},{129,385},{257,1},{385... | collective-permute-start | bytes 786440 | tf_op jit(solution)/shard_map/ppermute | solution.py:162
  45.2 0.7 copy-start.6
  49.7 17.0 %collective-permute-start.3 = (bf16[256,1024]{1,0:T(8,128)(2,1)S(1)}, bf16[256,1024]{1,0:T(8,128)(2,1)S(1)}, u32[]{:S(2)}, u32[]{:S(2)}) collective-permute-start(bf16[256,1024]{1,0:T(8,128)(2,1)S(1)} %shard_map.83.rows), channel_id=1, source_target_pairs={{0,128},{128,256},{256,384},{384,0},{1,129},{129,257},{257,385},{3... | collective-permute-start | bytes 1572872 | tf_op jit(solution)/shard_map/ppermute | solution.py:162
  52.8 15.1 %collective-permute-start.4 = (bf16[256,1024]{1,0:T(8,128)(2,1)S(1)}, bf16[256,1024]{1,0:T(8,128)(2,1)S(1)}, u32[]{:S(2)}, u32[]{:S(2)}) collective-permute-start(bf16[256,1024]{1,0:T(8,128)(2,1)S(1)} %shard_map.83.rows), channel_id=1, source_target_pairs={{0,384},{128,0},{256,128},{384,256},{1,385},{129,1},{257,129},{385... | collective-permute-start | bytes 1572872 | tf_op jit(solution)/shard_map/ppermute | solution.py:162
  56.2 1.0 copy-start.7
  57.2 1.0 copy-start.4
  58.2 1.6 %copy-start.1 = (bf16[1,1024,1024]{2,1,0:T(8,128)(2,1)S(1)}, bf16[1,1024,1024]{2,1,0:T(8,128)(2,1)}, u32[]{:S(2)}) copy-start(bf16[1,1024,1024]{2,1,0:T(8,128)(2,1)} %weight_out.5) | copy-start | bytes 6291460
  68.0 17.4 %collective-permute-start.7 = (bf16[128,1024]{1,0:T(8,128)(2,1)S(1)}, bf16[128,1024]{1,0:T(8,128)(2,1)S(1)}, u32[]{:S(2)}, u32[]{:S(2)}) collective-permute-start(bf16[128,1024]{1,0:T(8,128)(2,1)S(1)} %slice.6), channel_id=1, source_target_pairs={{0,128},{128,256},{256,384},{384,0},{1,129},{129,257},{257,385},{3... | collective-permute-start | bytes 786440 | tf_op jit(solution)/shard_map/ppermute | solution.py:162
  71.6 13.8 %copy-start.2 = (bf16[1,1024,1024]{2,1,0:T(8,128)(2,1)S(1)}, bf16[1,1024,1024]{2,1,0:T(8,128)(2,1)}, u32[]{:S(2)}) copy-start(bf16[1,1024,1024]{2,1,0:T(8,128)(2,1)} %weight_out.5) | copy-start | bytes 6291460
  71.6 13.8 %collective-permute-start.8 = (bf16[128,1024]{1,0:T(8,128)(2,1)S(1)}, bf16[128,1024]{1,0:T(8,128)(2,1)S(1)}, u32[]{:S(2)}, u32[]{:S(2)}) collective-permute-start(bf16[128,1024]{1,0:T(8,128)(2,1)S(1)} %slice.7), channel_id=1, source_target_pairs={{0,384},{128,0},{256,128},{384,256},{1,385},{129,1},{257,129},{385... | collective-permute-start | bytes 786440 | tf_op jit(solution)/shard_map/ppermute | solution.py:162
  80.1 30.3 %collective-permute-start.5 = (bf16[256,1024]{1,0:T(8,128)(2,1)}, bf16[256,1024]{1,0:T(8,128)(2,1)}, u32[]{:S(2)}, u32[]{:S(2)}) collective-permute-start(bf16[256,1024]{1,0:T(8,128)(2,1)} %get-tuple-element.19), channel_id=1, source_target_pairs={{0,384},{128,0},{256,128},{384,256},{1,385},{129,1},{257,129},{385... | collective-permute-start | bytes 1572872 | tf_op jit(solution)/shard_map/ppermute | solution.py:162
  83.4 26.9 %collective-permute-start.6 = (bf16[256,1024]{1,0:T(8,128)(2,1)}, bf16[256,1024]{1,0:T(8,128)(2,1)}, u32[]{:S(2)}, u32[]{:S(2)}) collective-permute-start(bf16[256,1024]{1,0:T(8,128)(2,1)} %get-tuple-element.20), channel_id=1, source_target_pairs={{0,128},{128,256},{256,384},{384,0},{1,129},{129,257},{257,385},{3... | collective-permute-start | bytes 1572872 | tf_op jit(solution)/shard_map/ppermute | solution.py:162
  86.8 23.5 %collective-permute-start.9 = (bf16[256,1024]{1,0:T(8,128)(2,1)S(1)}, bf16[256,1024]{1,0:T(8,128)(2,1)S(1)}, u32[]{:S(2)}, u32[]{:S(2)}) collective-permute-start(bf16[256,1024]{1,0:T(8,128)(2,1)S(1)} %shard_map.87), channel_id=1, source_target_pairs={{0,256},{128,384},{256,0},{384,128},{1,257},{129,385},{257,1},{385... | collective-permute-start | bytes 1572872 | tf_op jit(solution)/shard_map/ppermute | solution.py:162
  110.3 13.4 %copy-start.10 = (bf16[1024]{0:T(1024)(128)(2,1)S(1)}, bf16[1024]{0:T(1024)(128)(2,1)}, u32[]{:S(2)}) copy-start(bf16[1024]{0:T(1024)(128)(2,1)} %param.11) | copy-start | bytes 6148
  110.3 23.5 %copy-start.9 = (f32[128]{0:T(128)S(1)}, f32[128]{0:T(128)}, u32[]{:S(2)}) copy-start(f32[128]{0:T(128)} %param.10) | copy-start | bytes 1540
  112.5 31.8 %copy-start.8 = (s32[128,1]{0,1:T(1,128)S(1)}, s32[128,1]{0,1:T(1,128)}, u32[]{:S(2)}) copy-start(s32[128,1]{0,1:T(1,128)} %param.9) | copy-start | bytes 1540
  112.5 31.8 %all-to-all-start.1 = ((bf16[128,2,1024]{2,1,0:T(2,128)(2,1)}), bf16[128,2,1024]{2,1,0:T(2,128)(2,1)S(1)}, u32[]{:S(2)}, u32[]{:S(2)}) async-start(bf16[128,2,1024]{2,1,0:T(2,128)(2,1)} %shard_map.89), calls=%async_computation.1 | async-start | bytes 1048576 | tf_op jit(solution)/shard_map/all_to_all | solution.py:166
  133.8 1.0 copy-start.5
Sparse Core Ops, SparseCore 0:
  10.5 94.3 all-gather.1
  110.4 23.3 reduce-scatter.1

commit v7 on v4

--- a/solution.py
+++ b/solution.py
@@ -36,6 +36,12 @@
     out[...] = rows.reshape(experts, capacity, model)
 
 
+def join_kernel(left, right, out):
+    width = left.shape[1]
+    out[:, :width] = left[...]
+    out[:, width:] = right[...]
+
+
 def unpack_kernel(slots, out):
     out[...] = slots[...].reshape(out.shape)
 
@@ -89,7 +95,7 @@
     out[...] = total.astype(jnp.bfloat16).reshape(out.shape)
 
 
-def scale_kernel(left, right, far, own, tokens, weight, gate, out):
+def scale_kernel(far, left, right, own, tokens, weight, gate, out):
     model = own.shape[1]
     res = left[...].astype(jnp.float32) + right[...].astype(jnp.float32)
     res = res + far[...].astype(jnp.float32) + own[...].astype(jnp.float32)
@@ -147,7 +153,7 @@
     hidden = exp_up.shape[2]
     route_row = routes.reshape(1, row_count)
 
-    res_pair = jnp.concatenate([res_up, res_down.T], axis=1)
+    res_pair = call(join_kernel, (res_up, res_down.T), (res_up.shape[0], 2 * hidden), params=WHOLE)
     res_all = lax.all_gather(res_pair, "ep", axis=0, tiled=True)
 
     outgoing = call(dispatch_kernel, (route_row, tokens), (experts, capacity, model), params=WHOLE)
@@ -188,7 +194,9 @@
     )
     total = call(sum_kernel, (own, left, after(right, res_parts), far_back), (experts, capacity, model))
     res_parts = after(res_parts, total)
-    res_parts = [shifted(part, step) for part, step in zip(res_parts, (3, 1, 2))] + [res_parts[3]]
+    res_far = shifted(res_parts[2], 2)
+    res_near = [shifted(part, step) for part, step in zip(res_parts[:2], (3, 1))]
+    res_parts = [res_far] + res_near + [res_parts[3]]
     returned = across(total, "ep")
     scaled = call(
         scale_kernel,

time: 153 us -> 153 us (level)
    ppermute x13, waiting for transfers between devices: 22.3 us -> 20.3 us  [shifted(): lax.ppermute(value, 'grp', [(i, (i + step) % size) for i in range(size)])]
    all_to_all x2, waiting for transfers between devices: 6.25 us -> 8.19 us  [across(): return lax.all_to_all(value, axis, split_axis=0, concat_axis=0, tiled=True)]
    pallas_call x10 -> x11, Pallas kernels: 20.2 us -> 21.6 us  [call(): pl.pallas_call(kernel, grid=(1,), in_specs=[SMEM if value.ndim == 1 else...]
where the time goes in v7:
time: 153 us; the launch traced here: 152 us
  starting transfers between devices  69.9 us (46%)
  waiting for transfers between devices  42.7 us (28%)
  Pallas kernels  21.6 us (14%)
  between operations  13.7 us (9%)
  local copies, waits for them, and re-layouts  4.31 us (3%)
    ppermute x13, starting transfers between devices, shifted(): lax.ppermute(value, 'grp', [(i, (i + step) % size) for i in range(size)])  40.6 us
    all_to_all x2, starting transfers between devices, across(): return lax.all_to_all(value, axis, split_axis=0, concat_axis=0, tiled=True)  29.3 us
    pallas_call x11, Pallas kernels, call(): pl.pallas_call(kernel, grid=(1,), in_specs=[SMEM if value.ndim == 1 else...  21.6 us
    ppermute x13, waiting for transfers between devices, shifted(): lax.ppermute(value, 'grp', [(i, (i + step) % size) for i in range(size)])  20.3 us
    all_gather x1, waiting for transfers between devices, local(): res_all = lax.all_gather(res_pair, 'ep', axis=0, tiled=True)  14.1 us
    all_to_all x2, waiting for transfers between devices, across(): return lax.all_to_all(value, axis, split_axis=0, concat_axis=0, tiled=True)  8.19 us
    unnamed x22, local copies, waits for them, and re-layouts  4.27 us
  transfers between devices with their start and end apart: 16, of which 11 were waited for; matrix products, arithmetic and copies ran while one was open for 0% of the time, Pallas kernels for 11%

profile of v7, /device:TPU:1, one launch (start us, length us, event | category | flops | bytes accessed | tf_op | source)
XLA Modules:
  0.0 152.2 jit_solution(16320572237923934217)
XLA Ops:
  6.5 1.4 shard_map.88
  7.9 0.0 all-gather.2.cloned.1.call-update
  8.0 2.2 %shard_map.82 = bf16[128,2,1024]{2,1,0:T(2,128)(2,1)} custom-call(s32[1,128]{1,0:T(1,128)} %bitcast.3, bf16[128,1024]{1,0:T(8,128)(2,1)} %tokens.3), custom_call_target="tpu_custom_call" | custom-call | tf_op jit(solution)/shard_map/pallas_call | solution.py:123
  10.1 18.5 %all-to-all-start = ((bf16[128,2,1024]{2,1,0:T(2,128)(2,1)}), bf16[128,2,1024]{2,1,0:T(2,128)(2,1)S(1)}, u32[]{:S(2)}, u32[]{:S(2)}) async-start(bf16[128,2,1024]{2,1,0:T(2,128)(2,1)} %shard_map.82), calls=%async_computation | async-start | bytes 1048576 | tf_op jit(solution)/shard_map/all_to_all | solution.py:141
  28.7 3.1 %collective-permute-start = (bf16[128,1024]{1,0:T(8,128)(2,1)}, bf16[128,1024]{1,0:T(8,128)(2,1)S(1)}, u32[]{:S(2)}, u32[]{:S(2)}) collective-permute-start(bf16[128,1024]{1,0:T(8,128)(2,1)} %tokens.3), channel_id=1, source_target_pairs={{0,128},{128,256},{256,384},{384,0},{1,129},{129,257},{257,385},{3... | collective-permute-start | bytes 786440 | tf_op jit(solution)/shard_map/ppermute | solution.py:137
  31.8 3.4 %collective-permute-start.1 = (bf16[128,1024]{1,0:T(8,128)(2,1)}, bf16[128,1024]{1,0:T(8,128)(2,1)S(1)}, u32[]{:S(2)}, u32[]{:S(2)}) collective-permute-start(bf16[128,1024]{1,0:T(8,128)(2,1)} %tokens.3), channel_id=1, source_target_pairs={{0,384},{128,0},{256,128},{384,256},{1,385},{129,1},{257,129},{385... | collective-permute-start | bytes 786440 | tf_op jit(solution)/shard_map/ppermute | solution.py:137
  35.2 3.4 %collective-permute-start.2 = (bf16[128,1024]{1,0:T(8,128)(2,1)}, bf16[128,1024]{1,0:T(8,128)(2,1)S(1)}, u32[]{:S(2)}, u32[]{:S(2)}) collective-permute-start(bf16[128,1024]{1,0:T(8,128)(2,1)} %tokens.3), channel_id=1, source_target_pairs={{0,256},{128,384},{256,0},{384,128},{1,257},{129,385},{257,1},{385... | collective-permute-start | bytes 786440 | tf_op jit(solution)/shard_map/ppermute | solution.py:137
  38.6 0.3 collective-permute-done.left
  38.9 1.7 %collective-permute-done.1.right = bf16[128,1024]{1,0:T(8,128)(2,1)S(1)} collective-permute-done((bf16[128,1024]{1,0:T(8,128)(2,1)}, bf16[128,1024]{1,0:T(8,128)(2,1)S(1)}, u32[]{:S(2)}, u32[]{:S(2)}) %collective-permute-start.1) | collective-permute-done | bytes 262176 | tf_op jit(solution)/shard_map/ppermute | solution.py:137
  40.7 4.5 %collective-permute-done.2.far = bf16[128,1024]{1,0:T(8,128)(2,1)S(1)} collective-permute-done((bf16[128,1024]{1,0:T(8,128)(2,1)}, bf16[128,1024]{1,0:T(8,128)(2,1)S(1)}, u32[]{:S(2)}, u32[]{:S(2)}) %collective-permute-start.2) | collective-permute-done | bytes 262176 | tf_op jit(solution)/shard_map/ppermute | solution.py:137
  45.2 0.7 copy-done.6
  45.9 3.8 %all-to-all-done.slots = bf16[128,2,1024]{2,1,0:T(2,128)(2,1)S(1)} async-done(((bf16[128,2,1024]{2,1,0:T(2,128)(2,1)}), bf16[128,2,1024]{2,1,0:T(2,128)(2,1)S(1)}, u32[]{:S(2)}, u32[]{:S(2)}) %all-to-all-start) | async-done | bytes 524320 | tf_op jit(solution)/shard_map/all_to_all | solution.py:141
  49.6 0.1 shard_map.83.rows
  49.7 3.1 %collective-permute-start.3 = (bf16[256,1024]{1,0:T(8,128)(2,1)S(1)}, bf16[256,1024]{1,0:T(8,128)(2,1)S(1)}, u32[]{:S(2)}, u32[]{:S(2)}) collective-permute-start(bf16[256,1024]{1,0:T(8,128)(2,1)S(1)} %shard_map.83.rows), channel_id=1, source_target_pairs={{0,128},{128,256},{256,384},{384,0},{1,129},{129,257},{257,385},{3... | collective-permute-start | bytes 1572872 | tf_op jit(solution)/shard_map/ppermute | solution.py:137
  52.8 3.4 %collective-permute-start.4 = (bf16[256,1024]{1,0:T(8,128)(2,1)S(1)}, bf16[256,1024]{1,0:T(8,128)(2,1)S(1)}, u32[]{:S(2)}, u32[]{:S(2)}) collective-permute-start(bf16[256,1024]{1,0:T(8,128)(2,1)S(1)} %shard_map.83.rows), channel_id=1, source_target_pairs={{0,384},{128,0},{256,128},{384,256},{1,385},{129,1},{257,129},{385... | collective-permute-start | bytes 1572872 | tf_op jit(solution)/shard_map/ppermute | solution.py:137
  56.2 0.0 copy-start.7
  56.2 0.9 copy-done.7
  57.2 0.1 shard_map.84.rows
  57.3 1.0 copy-done.4
  58.3 1.6 %copy-done.1 = bf16[1,1024,1024]{2,1,0:T(8,128)(2,1)S(1)} copy-done((bf16[1,1024,1024]{2,1,0:T(8,128)(2,1)S(1)}, bf16[1,1024,1024]{2,1,0:T(8,128)(2,1)}, u32[]{:S(2)}) %copy-start.1) | copy-done | bytes 2097176
  59.9 1.5 shard_map.85.own
  61.3 5.4 %collective-permute-done.3.left = bf16[256,1024]{1,0:T(8,128)(2,1)S(1)} collective-permute-done((bf16[256,1024]{1,0:T(8,128)(2,1)S(1)}, bf16[256,1024]{1,0:T(8,128)(2,1)S(1)}, u32[]{:S(2)}, u32[]{:S(2)}) %collective-permute-start.3) | collective-permute-done | bytes 524320 | tf_op jit(solution)/shard_map/ppermute | solution.py:137
  66.7 1.3 collective-permute-done.4.right
  68.0 3.5 %collective-permute-start.7 = (bf16[128,1024]{1,0:T(8,128)(2,1)S(1)}, bf16[128,1024]{1,0:T(8,128)(2,1)S(1)}, u32[]{:S(2)}, u32[]{:S(2)}) collective-permute-start(bf16[128,1024]{1,0:T(8,128)(2,1)S(1)} %slice.6), channel_id=1, source_target_pairs={{0,128},{128,256},{256,384},{384,0},{1,129},{129,257},{257,385},{3... | collective-permute-start | bytes 786440 | tf_op jit(solution)/shard_map/ppermute | solution.py:137
  71.6 0.0 copy-start.2
  71.6 3.5 %collective-permute-start.8 = (bf16[128,1024]{1,0:T(8,128)(2,1)S(1)}, bf16[128,1024]{1,0:T(8,128)(2,1)S(1)}, u32[]{:S(2)}, u32[]{:S(2)}) collective-permute-start(bf16[128,1024]{1,0:T(8,128)(2,1)S(1)} %slice.7), channel_id=1, source_target_pairs={{0,384},{128,0},{256,128},{384,256},{1,385},{129,1},{257,129},{385... | collective-permute-start | bytes 786440 | tf_op jit(solution)/shard_map/ppermute | solution.py:137
  75.1 4.9 %shard_map.86 = (bf16[256,1024]{1,0:T(8,128)(2,1)}, bf16[256,1024]{1,0:T(8,128)(2,1)}) custom-call(bf16[256,1024]{1,0:T(8,128)(2,1)S(1)} %collective-permute-done.3.left, bf16[256,1024]{1,0:T(8,128)(2,1)S(1)} %collective-permute-done.4.right, bf16[1,1024,1024]{2,1,0:T(8,128)(2,1)S(1)} %copy-done, bf16[1,1024,1024]{2,1,0:T(8,128)(2,1)} %weight_out.5), custom_call_target="tpu_custom_call" | custom-call | flops 2147483648 | bytes 6291456 | tf_op jit(solution)/shard_map/pallas_call | solution.py:123
  80.0 3.4 %collective-permute-start.5 = (bf16[256,1024]{1,0:T(8,128)(2,1)}, bf16[256,1024]{1,0:T(8,128)(2,1)S(1)}, u32[]{:S(2)}, u32[]{:S(2)}) collective-permute-start(bf16[256,1024]{1,0:T(8,128)(2,1)} %get-tuple-element.27), channel_id=1, source_target_pairs={{0,384},{128,0},{256,128},{384,256},{1,385},{129,1},{257,129},{385... | collective-permute-start | bytes 1572872 | tf_op jit(solution)/shard_map/ppermute | solution.py:137
  83.3 1.9 %collective-permute-start.6 = (bf16[256,1024]{1,0:T(8,128)(2,1)}, bf16[256,1024]{1,0:T(8,128)(2,1)}, u32[]{:S(2)}, u32[]{:S(2)}) collective-permute-start(bf16[256,1024]{1,0:T(8,128)(2,1)} %get-tuple-element.28), channel_id=1, source_target_pairs={{0,128},{128,256},{256,384},{384,0},{1,129},{129,257},{257,385},{3... | collective-permute-start | bytes 1572872 | tf_op jit(solution)/shard_map/ppermute | solution.py:137
  85.3 0.0 collective-permute-done.7.upper
  85.3 0.0 collective-permute-done.8.lower
  85.3 2.3 %shard_map.87 = bf16[256,1024]{1,0:T(8,128)(2,1)} custom-call(bf16[128,1024]{1,0:T(8,128)(2,1)S(1)} %collective-permute-done.7.upper, bf16[128,1024]{1,0:T(8,128)(2,1)S(1)} %collective-permute-done.8.lower, bf16[1,1024,1024]{2,1,0:T(8,128)(2,1)S(1)} %copy-done, bf16[1,1024,1024]{2,1,0:T(8,128)(2,1)S(1)} %copy-done.2), custom_call_target="tpu_custom_call" | custom-call | flops 1073741824 | bytes 5242880 | tf_op jit(solution)/shard_map/pallas_call | solution.py:123
  87.6 3.2 %collective-permute-start.9 = (bf16[256,1024]{1,0:T(8,128)(2,1)}, bf16[256,1024]{1,0:T(8,128)(2,1)S(1)}, u32[]{:S(2)}, u32[]{:S(2)}) collective-permute-start(bf16[256,1024]{1,0:T(8,128)(2,1)} %shard_map.87), channel_id=1, source_target_pairs={{0,256},{128,384},{256,0},{384,128},{1,257},{129,385},{257,1},{385... | collective-permute-start | bytes 1572872 | tf_op jit(solution)/shard_map/ppermute | solution.py:137
  90.7 14.1 %all-gather.2.cloned.1.call-done.pair = bf16[1024,2048]{1,0:T(8,128)(2,1)} async-done(((bf16[8,2048]{1,0:T(8,128)(2,1)}), bf16[1024,2048]{1,0:T(8,128)(2,1)}) %all-gather.2.cloned.1.call-update) | async-done | bytes 4194320 | tf_op jit(solution)/shard_map/all_gather | solution.py:157
  104.9 5.8 %shard_map.89 = (bf16[128,1024]{1,0:T(8,128)(2,1)}, bf16[128,1024]{1,0:T(8,128)(2,1)}, bf16[128,1024]{1,0:T(8,128)(2,1)}, bf16[128,1024]{1,0:T(8,128)(2,1)}) custom-call(bf16[512,1024]{1,0:T(8,128)(2,1)} %copy-done.4, bf16[1024,2048]{1,0:T(8,128)(2,1)} %all-gather.2.cloned.1.call-done.pair), custom_call_target="tpu_custom_call" | custom-call | flops 2147483648 | bytes 6291456 | tf_op jit(solution)/shard_map/pallas_call | solution.py:123
  110.7 0.0 collective-permute-done.6.right
  110.7 0.0 collective-permute-done.9.far
  110.7 2.2 %shard_map.90 = bf16[128,2,1024]{2,1,0:T(2,128)(2,1)} custom-call(bf16[256,1024]{1,0:T(8,128)(2,1)S(1)} %shard_map.85.own, bf16[256,1024]{1,0:T(8,128)(2,1)S(1)} %collective-permute-done.5.left, bf16[256,1024]{1,0:T(8,128)(2,1)} %collective-permute-done.6.right, bf16[256,1024]{1,0:T(8,128)(2,1)S(1)} %collective-permute-done.9.far), custom_call_target="tpu_custom_call" | custom-call | tf_op jit(solution)/shard_map/pallas_call | solution.py:123
  112.9 10.7 %all-to-all-start.1 = ((bf16[128,2,1024]{2,1,0:T(2,128)(2,1)}), bf16[128,2,1024]{2,1,0:T(2,128)(2,1)S(1)}, u32[]{:S(2)}, u32[]{:S(2)}) async-start(bf16[128,2,1024]{2,1,0:T(2,128)(2,1)} %shard_map.90), calls=%async_computation.1 | async-start | bytes 1048576 | tf_op jit(solution)/shard_map/all_to_all | solution.py:141
  123.6 3.5 %collective-permute-start.10 = (bf16[128,1024]{1,0:T(8,128)(2,1)}, bf16[128,1024]{1,0:T(8,128)(2,1)S(1)}, u32[]{:S(2)}, u32[]{:S(2)}) collective-permute-start(bf16[128,1024]{1,0:T(8,128)(2,1)} %get-tuple-element.36), channel_id=1, source_target_pairs={{0,256},{128,384},{256,0},{384,128},{1,257},{129,385},{257,1},{385... | collective-permute-start | bytes 786440 | tf_op jit(solution)/shard_map/ppermute | solution.py:137
  127.1 2.8 %collective-permute-start.11 = (bf16[128,1024]{1,0:T(8,128)(2,1)}, bf16[128,1024]{1,0:T(8,128)(2,1)S(1)}, u32[]{:S(2)}, u32[]{:S(2)}) collective-permute-start(bf16[128,1024]{1,0:T(8,128)(2,1)} %get-tuple-element.37), channel_id=1, source_target_pairs={{0,384},{128,0},{256,128},{384,256},{1,385},{129,1},{257,129},{385... | collective-permute-start | bytes 786440 | tf_op jit(solution)/shard_map/ppermute | solution.py:137
  129.9 2.5 %collective-permute-start.12 = (bf16[128,1024]{1,0:T(8,128)(2,1)}, bf16[128,1024]{1,0:T(8,128)(2,1)S(1)}, u32[]{:S(2)}, u32[]{:S(2)}) collective-permute-start(bf16[128,1024]{1,0:T(8,128)(2,1)} %get-tuple-element.38), channel_id=1, source_target_pairs={{0,128},{128,256},{256,384},{384,0},{1,129},{129,257},{257,385},{3... | collective-permute-start | bytes 786440 | tf_op jit(solution)/shard_map/ppermute | solution.py:137
  132.5 1.7 %collective-permute-done.10.far = bf16[128,1024]{1,0:T(8,128)(2,1)S(1)} collective-permute-done((bf16[128,1024]{1,0:T(8,128)(2,1)}, bf16[128,1024]{1,0:T(8,128)(2,1)S(1)}, u32[]{:S(2)}, u32[]{:S(2)}) %collective-permute-start.10) | collective-permute-done | bytes 262176 | tf_op jit(solution)/shard_map/ppermute | solution.py:137
  134.2 4.7 %collective-permute-done.11.left = bf16[128,1024]{1,0:T(8,128)(2,1)S(1)} collective-permute-done((bf16[128,1024]{1,0:T(8,128)(2,1)}, bf16[128,1024]{1,0:T(8,128)(2,1)S(1)}, u32[]{:S(2)}, u32[]{:S(2)}) %collective-permute-start.11) | collective-permute-done | bytes 262176 | tf_op jit(solution)/shard_map/ppermute | solution.py:137
  138.8 0.8 collective-permute-done.12.right
  139.6 0.2 shard_map.91.scaled
  139.8 4.4 %all-to-all-done.1.slots = bf16[128,2,1024]{2,1,0:T(2,128)(2,1)S(1)} async-done(((bf16[128,2,1024]{2,1,0:T(2,128)(2,1)}), bf16[128,2,1024]{2,1,0:T(2,128)(2,1)S(1)}, u32[]{:S(2)}, u32[]{:S(2)}) %all-to-all-start.1) | async-done | bytes 524320 | tf_op jit(solution)/shard_map/all_to_all | solution.py:141
  144.2 1.1 shard_map.92
  (21 shorter events, 0.1 us)
Async XLA Ops:
  6.5 49.7 %copy-start.3 = (bf16[128,1024]{1,0:T(8,128)(2,1)S(1)}, bf16[128,1024]{1,0:T(8,128)(2,1)}, u32[]{:S(2)}) copy-start(bf16[128,1024]{1,0:T(8,128)(2,1)} %tokens.3) | copy-start | bytes 786436
  6.5 98.3 %all-gather.2.cloned.1.call-start = ((), (), s32[]{:S(2)}) async-start(), calls=%async_computation.2 | async-start | bytes 4227072 | tf_op jit(solution)/shard_map/all_gather | solution.py:157
  10.1 48.1 %copy-start = (bf16[1,1024,1024]{2,1,0:T(8,128)(2,1)S(1)}, bf16[1,1024,1024]{2,1,0:T(8,128)(2,1)}, u32[]{:S(2)}) copy-start(bf16[1,1024,1024]{2,1,0:T(8,128)(2,1)} %weight_in.5) | copy-start | bytes 6291460
  10.1 39.5 %all-to-all-start = ((bf16[128,2,1024]{2,1,0:T(2,128)(2,1)}), bf16[128,2,1024]{2,1,0:T(2,128)(2,1)S(1)}, u32[]{:S(2)}, u32[]{:S(2)}) async-start(bf16[128,2,1024]{2,1,0:T(2,128)(2,1)} %shard_map.82), calls=%async_computation | async-start | bytes 1048576 | tf_op jit(solution)/shard_map/all_to_all | solution.py:141
  28.7 10.2 %collective-permute-start = (bf16[128,1024]{1,0:T(8,128)(2,1)}, bf16[128,1024]{1,0:T(8,128)(2,1)S(1)}, u32[]{:S(2)}, u32[]{:S(2)}) collective-permute-start(bf16[128,1024]{1,0:T(8,128)(2,1)} %tokens.3), channel_id=1, source_target_pairs={{0,128},{128,256},{256,384},{384,0},{1,129},{129,257},{257,385},{3... | collective-permute-start | bytes 786440 | tf_op jit(solution)/shard_map/ppermute | solution.py:137
  31.8 8.8 %collective-permute-start.1 = (bf16[128,1024]{1,0:T(8,128)(2,1)}, bf16[128,1024]{1,0:T(8,128)(2,1)S(1)}, u32[]{:S(2)}, u32[]{:S(2)}) collective-permute-start(bf16[128,1024]{1,0:T(8,128)(2,1)} %tokens.3), channel_id=1, source_target_pairs={{0,384},{128,0},{256,128},{384,256},{1,385},{129,1},{257,129},{385... | collective-permute-start | bytes 786440 | tf_op jit(solution)/shard_map/ppermute | solution.py:137
  35.2 10.0 %collective-permute-start.2 = (bf16[128,1024]{1,0:T(8,128)(2,1)}, bf16[128,1024]{1,0:T(8,128)(2,1)S(1)}, u32[]{:S(2)}, u32[]{:S(2)}) collective-permute-start(bf16[128,1024]{1,0:T(8,128)(2,1)} %tokens.3), channel_id=1, source_target_pairs={{0,256},{128,384},{256,0},{384,128},{1,257},{129,385},{257,1},{385... | collective-permute-start | bytes 786440 | tf_op jit(solution)/shard_map/ppermute | solution.py:137
  45.2 0.7 copy-start.6
  49.7 17.0 %collective-permute-start.3 = (bf16[256,1024]{1,0:T(8,128)(2,1)S(1)}, bf16[256,1024]{1,0:T(8,128)(2,1)S(1)}, u32[]{:S(2)}, u32[]{:S(2)}) collective-permute-start(bf16[256,1024]{1,0:T(8,128)(2,1)S(1)} %shard_map.83.rows), channel_id=1, source_target_pairs={{0,128},{128,256},{256,384},{384,0},{1,129},{129,257},{257,385},{3... | collective-permute-start | bytes 1572872 | tf_op jit(solution)/shard_map/ppermute | solution.py:137
  52.8 15.2 %collective-permute-start.4 = (bf16[256,1024]{1,0:T(8,128)(2,1)S(1)}, bf16[256,1024]{1,0:T(8,128)(2,1)S(1)}, u32[]{:S(2)}, u32[]{:S(2)}) collective-permute-start(bf16[256,1024]{1,0:T(8,128)(2,1)S(1)} %shard_map.83.rows), channel_id=1, source_target_pairs={{0,384},{128,0},{256,128},{384,256},{1,385},{129,1},{257,129},{385... | collective-permute-start | bytes 1572872 | tf_op jit(solution)/shard_map/ppermute | solution.py:137
  56.2 1.0 copy-start.7
  57.2 1.0 copy-start.4
  58.3 1.6 %copy-start.1 = (bf16[1,1024,1024]{2,1,0:T(8,128)(2,1)S(1)}, bf16[1,1024,1024]{2,1,0:T(8,128)(2,1)}, u32[]{:S(2)}) copy-start(bf16[1,1024,1024]{2,1,0:T(8,128)(2,1)} %weight_out.5) | copy-start | bytes 6291460
  68.0 17.2 %collective-permute-start.7 = (bf16[128,1024]{1,0:T(8,128)(2,1)S(1)}, bf16[128,1024]{1,0:T(8,128)(2,1)S(1)}, u32[]{:S(2)}, u32[]{:S(2)}) collective-permute-start(bf16[128,1024]{1,0:T(8,128)(2,1)S(1)} %slice.6), channel_id=1, source_target_pairs={{0,128},{128,256},{256,384},{384,0},{1,129},{129,257},{257,385},{3... | collective-permute-start | bytes 786440 | tf_op jit(solution)/shard_map/ppermute | solution.py:137
  71.6 13.7 %copy-start.2 = (bf16[1,1024,1024]{2,1,0:T(8,128)(2,1)S(1)}, bf16[1,1024,1024]{2,1,0:T(8,128)(2,1)}, u32[]{:S(2)}) copy-start(bf16[1,1024,1024]{2,1,0:T(8,128)(2,1)} %weight_out.5) | copy-start | bytes 6291460
  71.6 13.7 %collective-permute-start.8 = (bf16[128,1024]{1,0:T(8,128)(2,1)S(1)}, bf16[128,1024]{1,0:T(8,128)(2,1)S(1)}, u32[]{:S(2)}, u32[]{:S(2)}) collective-permute-start(bf16[128,1024]{1,0:T(8,128)(2,1)S(1)} %slice.7), channel_id=1, source_target_pairs={{0,384},{128,0},{256,128},{384,256},{1,385},{129,1},{257,129},{385... | collective-permute-start | bytes 786440 | tf_op jit(solution)/shard_map/ppermute | solution.py:137
  80.0 30.7 %collective-permute-start.5 = (bf16[256,1024]{1,0:T(8,128)(2,1)}, bf16[256,1024]{1,0:T(8,128)(2,1)S(1)}, u32[]{:S(2)}, u32[]{:S(2)}) collective-permute-start(bf16[256,1024]{1,0:T(8,128)(2,1)} %get-tuple-element.27), channel_id=1, source_target_pairs={{0,384},{128,0},{256,128},{384,256},{1,385},{129,1},{257,129},{385... | collective-permute-start | bytes 1572872 | tf_op jit(solution)/shard_map/ppermute | solution.py:137
  83.3 27.3 %collective-permute-start.6 = (bf16[256,1024]{1,0:T(8,128)(2,1)}, bf16[256,1024]{1,0:T(8,128)(2,1)}, u32[]{:S(2)}, u32[]{:S(2)}) collective-permute-start(bf16[256,1024]{1,0:T(8,128)(2,1)} %get-tuple-element.28), channel_id=1, source_target_pairs={{0,128},{128,256},{256,384},{384,0},{1,129},{129,257},{257,385},{3... | collective-permute-start | bytes 1572872 | tf_op jit(solution)/shard_map/ppermute | solution.py:137
  87.6 23.1 %collective-permute-start.9 = (bf16[256,1024]{1,0:T(8,128)(2,1)}, bf16[256,1024]{1,0:T(8,128)(2,1)S(1)}, u32[]{:S(2)}, u32[]{:S(2)}) collective-permute-start(bf16[256,1024]{1,0:T(8,128)(2,1)} %shard_map.87), channel_id=1, source_target_pairs={{0,256},{128,384},{256,0},{384,128},{1,257},{129,385},{257,1},{385... | collective-permute-start | bytes 1572872 | tf_op jit(solution)/shard_map/ppermute | solution.py:137
  110.7 21.8 %copy-start.10 = (bf16[1024]{0:T(1024)(128)(2,1)S(1)}, bf16[1024]{0:T(1024)(128)(2,1)}, u32[]{:S(2)}) copy-start(bf16[1024]{0:T(1024)(128)(2,1)} %param.11) | copy-start | bytes 6148
  110.7 28.9 %copy-start.5 = (bf16[128,1024]{1,0:T(8,128)(2,1)S(1)}, bf16[128,1024]{1,0:T(8,128)(2,1)}, u32[]{:S(2)}) copy-start(bf16[128,1024]{1,0:T(8,128)(2,1)} %get-tuple-element.39.own) | copy-start | bytes 786436
  110.7 28.9 %copy-start.9 = (f32[128]{0:T(128)S(1)}, f32[128]{0:T(128)}, u32[]{:S(2)}) copy-start(f32[128]{0:T(128)} %param.10) | copy-start | bytes 1540
  112.9 31.3 %copy-start.8 = (s32[128,1]{0,1:T(1,128)S(1)}, s32[128,1]{0,1:T(1,128)}, u32[]{:S(2)}) copy-start(s32[128,1]{0,1:T(1,128)} %param.9) | copy-start | bytes 1540
  112.9 31.3 %all-to-all-start.1 = ((bf16[128,2,1024]{2,1,0:T(2,128)(2,1)}), bf16[128,2,1024]{2,1,0:T(2,128)(2,1)S(1)}, u32[]{:S(2)}, u32[]{:S(2)}) async-start(bf16[128,2,1024]{2,1,0:T(2,128)(2,1)} %shard_map.90), calls=%async_computation.1 | async-start | bytes 1048576 | tf_op jit(solution)/shard_map/all_to_all | solution.py:141
  123.6 10.5 %collective-permute-start.10 = (bf16[128,1024]{1,0:T(8,128)(2,1)}, bf16[128,1024]{1,0:T(8,128)(2,1)S(1)}, u32[]{:S(2)}, u32[]{:S(2)}) collective-permute-start(bf16[128,1024]{1,0:T(8,128)(2,1)} %get-tuple-element.36), channel_id=1, source_target_pairs={{0,256},{128,384},{256,0},{384,128},{1,257},{129,385},{257,1},{385... | collective-permute-start | bytes 786440 | tf_op jit(solution)/shard_map/ppermute | solution.py:137
  127.1 11.7 %collective-permute-start.11 = (bf16[128,1024]{1,0:T(8,128)(2,1)}, bf16[128,1024]{1,0:T(8,128)(2,1)S(1)}, u32[]{:S(2)}, u32[]{:S(2)}) collective-permute-start(bf16[128,1024]{1,0:T(8,128)(2,1)} %get-tuple-element.37), channel_id=1, source_target_pairs={{0,384},{128,0},{256,128},{384,256},{1,385},{129,1},{257,129},{385... | collective-permute-start | bytes 786440 | tf_op jit(solution)/shard_map/ppermute | solution.py:137
  129.9 9.7 %collective-permute-start.12 = (bf16[128,1024]{1,0:T(8,128)(2,1)}, bf16[128,1024]{1,0:T(8,128)(2,1)S(1)}, u32[]{:S(2)}, u32[]{:S(2)}) collective-permute-start(bf16[128,1024]{1,0:T(8,128)(2,1)} %get-tuple-element.38), channel_id=1, source_target_pairs={{0,128},{128,256},{256,384},{384,0},{1,129},{129,257},{257,385},{3... | collective-permute-start | bytes 786440 | tf_op jit(solution)/shard_map/ppermute | solution.py:137
Sparse Core Ops, SparseCore 0:
  10.5 94.3 all-gather.1

commit v8 on v7

--- a/solution.py
+++ b/solution.py
@@ -34,12 +34,6 @@
     table = slot_table(routes[...], capacity, experts * capacity)
     rows = jnp.dot(table, tokens[...], preferred_element_type=jnp.float32).astype(jnp.bfloat16)
     out[...] = rows.reshape(experts, capacity, model)
-
-
-def join_kernel(left, right, out):
-    width = left.shape[1]
-    out[:, :width] = left[...]
-    out[:, width:] = right[...]
 
 
 def unpack_kernel(slots, out):
@@ -153,7 +147,7 @@
     hidden = exp_up.shape[2]
     route_row = routes.reshape(1, row_count)
 
-    res_pair = call(join_kernel, (res_up, res_down.T), (res_up.shape[0], 2 * hidden), params=WHOLE)
+    res_pair = jnp.concatenate([res_up, res_down.T], axis=1)
     res_all = lax.all_gather(res_pair, "ep", axis=0, tiled=True)
 
     outgoing = call(dispatch_kernel, (route_row, tokens), (experts, capacity, model), params=WHOLE)
@@ -192,7 +186,15 @@
         count=groups,
         params=WHOLE,
     )
-    total = call(sum_kernel, (own, left, after(right, res_parts), far_back), (experts, capacity, model))
+    row_block = pl.BlockSpec((slots // 2, model), lambda i: (i, 0))
+    total = pl.pallas_call(
+        sum_kernel,
+        grid=(2,),
+        in_specs=[row_block] * 4,
+        out_specs=pl.BlockSpec((experts // 2, capacity, model), lambda i: (i, 0, 0)),
+        out_shape=jax.ShapeDtypeStruct((experts, capacity, model), jnp.bfloat16),
+        compiler_params=PARAMS,
+    )(own, left, after(right, res_parts), far_back)
     res_parts = after(res_parts, total)
     res_far = shifted(res_parts[2], 2)
     res_near = [shifted(part, step) for part, step in zip(res_parts[:2], (3, 1))]

time: 153 us -> 153 us (level)
    pallas_call x11 -> x9, Pallas kernels: 21.6 us -> 18 us  [call(): pl.pallas_call(kernel, grid=(1,), in_specs=[SMEM if value.ndim == 1 else...]
    pallas_call x0 -> x1, Pallas kernels: none -> 2.06 us  [local(): pl.pallas_call(sum_kernel, grid=(2,), in_specs=[row_block] * 4, out_specs...]
where the time goes in v8:
time: 153 us; the launch traced here: 152 us
  starting transfers between devices  69.9 us (46%)
  waiting for transfers between devices  42.7 us (28%)
  Pallas kernels  20.1 us (13%)
  between operations  13.7 us (9%)
  local copies, waits for them, and re-layouts  4.31 us (3%)
    ppermute x13, starting transfers between devices, shifted(): lax.ppermute(value, 'grp', [(i, (i + step) % size) for i in range(size)])  40.6 us
    all_to_all x2, starting transfers between devices, across(): return lax.all_to_all(value, axis, split_axis=0, concat_axis=0, tiled=True)  29.3 us
    ppermute x13, waiting for transfers between devices, shifted(): lax.ppermute(value, 'grp', [(i, (i + step) % size) for i in range(size)])  20.3 us
    pallas_call x9, Pallas kernels, call(): pl.pallas_call(kernel, grid=(1,), in_specs=[SMEM if value.ndim == 1 else...  18 us
    all_gather x1, waiting for transfers between devices, local(): res_all = lax.all_gather(res_pair, 'ep', axis=0, tiled=True)  14.1 us
    all_to_all x2, waiting for transfers between devices, across(): return lax.all_to_all(value, axis, split_axis=0, concat_axis=0, tiled=True)  8.18 us
    unnamed x22, local copies, waits for them, and re-layouts  4.27 us
  transfers between devices with their start and end apart: 16, of which 11 were waited for; matrix products, arithmetic and copies ran while one was open for 0% of the time, Pallas kernels for 11%

profile of v8, /device:TPU:1, one launch (start us, length us, event | category | flops | bytes accessed | tf_op | source)
XLA Modules:
  0.0 152.0 jit_solution(12398716684882316897)
XLA Ops:
  6.5 1.4 pad_maximum_fusion
  7.9 0.0 all-gather.2.cloned.1.call-update
  8.0 2.2 %shard_map.82 = bf16[128,2,1024]{2,1,0:T(2,128)(2,1)} custom-call(s32[1,128]{1,0:T(1,128)} %bitcast.3, bf16[128,1024]{1,0:T(8,128)(2,1)} %tokens.3), custom_call_target="tpu_custom_call" | custom-call | tf_op jit(solution)/shard_map/pallas_call | solution.py:117
  10.1 18.6 %all-to-all-start = ((bf16[128,2,1024]{2,1,0:T(2,128)(2,1)}), bf16[128,2,1024]{2,1,0:T(2,128)(2,1)S(1)}, u32[]{:S(2)}, u32[]{:S(2)}) async-start(bf16[128,2,1024]{2,1,0:T(2,128)(2,1)} %shard_map.82), calls=%async_computation | async-start | bytes 1048576 | tf_op jit(solution)/shard_map/all_to_all | solution.py:135
  28.7 3.1 %collective-permute-start = (bf16[128,1024]{1,0:T(8,128)(2,1)}, bf16[128,1024]{1,0:T(8,128)(2,1)S(1)}, u32[]{:S(2)}, u32[]{:S(2)}) collective-permute-start(bf16[128,1024]{1,0:T(8,128)(2,1)} %tokens.3), channel_id=1, source_target_pairs={{0,128},{128,256},{256,384},{384,0},{1,129},{129,257},{257,385},{3... | collective-permute-start | bytes 786440 | tf_op jit(solution)/shard_map/ppermute | solution.py:131
  31.8 3.4 %collective-permute-start.1 = (bf16[128,1024]{1,0:T(8,128)(2,1)}, bf16[128,1024]{1,0:T(8,128)(2,1)S(1)}, u32[]{:S(2)}, u32[]{:S(2)}) collective-permute-start(bf16[128,1024]{1,0:T(8,128)(2,1)} %tokens.3), channel_id=1, source_target_pairs={{0,384},{128,0},{256,128},{384,256},{1,385},{129,1},{257,129},{385... | collective-permute-start | bytes 786440 | tf_op jit(solution)/shard_map/ppermute | solution.py:131
  35.2 3.4 %collective-permute-start.2 = (bf16[128,1024]{1,0:T(8,128)(2,1)}, bf16[128,1024]{1,0:T(8,128)(2,1)S(1)}, u32[]{:S(2)}, u32[]{:S(2)}) collective-permute-start(bf16[128,1024]{1,0:T(8,128)(2,1)} %tokens.3), channel_id=1, source_target_pairs={{0,256},{128,384},{256,0},{384,128},{1,257},{129,385},{257,1},{385... | collective-permute-start | bytes 786440 | tf_op jit(solution)/shard_map/ppermute | solution.py:131
  38.6 0.3 collective-permute-done.left
  38.9 1.7 %collective-permute-done.1.right = bf16[128,1024]{1,0:T(8,128)(2,1)S(1)} collective-permute-done((bf16[128,1024]{1,0:T(8,128)(2,1)}, bf16[128,1024]{1,0:T(8,128)(2,1)S(1)}, u32[]{:S(2)}, u32[]{:S(2)}) %collective-permute-start.1) | collective-permute-done | bytes 262176 | tf_op jit(solution)/shard_map/ppermute | solution.py:131
  40.7 4.5 %collective-permute-done.2.far = bf16[128,1024]{1,0:T(8,128)(2,1)S(1)} collective-permute-done((bf16[128,1024]{1,0:T(8,128)(2,1)}, bf16[128,1024]{1,0:T(8,128)(2,1)S(1)}, u32[]{:S(2)}, u32[]{:S(2)}) %collective-permute-start.2) | collective-permute-done | bytes 262176 | tf_op jit(solution)/shard_map/ppermute | solution.py:131
  45.2 0.7 copy-done.6
  45.9 3.8 %all-to-all-done.slots = bf16[128,2,1024]{2,1,0:T(2,128)(2,1)S(1)} async-done(((bf16[128,2,1024]{2,1,0:T(2,128)(2,1)}), bf16[128,2,1024]{2,1,0:T(2,128)(2,1)S(1)}, u32[]{:S(2)}, u32[]{:S(2)}) %all-to-all-start) | async-done | bytes 524320 | tf_op jit(solution)/shard_map/all_to_all | solution.py:135
  49.6 0.1 shard_map.83.rows
  49.7 3.1 %collective-permute-start.3 = (bf16[256,1024]{1,0:T(8,128)(2,1)S(1)}, bf16[256,1024]{1,0:T(8,128)(2,1)S(1)}, u32[]{:S(2)}, u32[]{:S(2)}) collective-permute-start(bf16[256,1024]{1,0:T(8,128)(2,1)S(1)} %shard_map.83.rows), channel_id=1, source_target_pairs={{0,128},{128,256},{256,384},{384,0},{1,129},{129,257},{257,385},{3... | collective-permute-start | bytes 1572872 | tf_op jit(solution)/shard_map/ppermute | solution.py:131
  52.8 3.4 %collective-permute-start.4 = (bf16[256,1024]{1,0:T(8,128)(2,1)S(1)}, bf16[256,1024]{1,0:T(8,128)(2,1)S(1)}, u32[]{:S(2)}, u32[]{:S(2)}) collective-permute-start(bf16[256,1024]{1,0:T(8,128)(2,1)S(1)} %shard_map.83.rows), channel_id=1, source_target_pairs={{0,384},{128,0},{256,128},{384,256},{1,385},{129,1},{257,129},{385... | collective-permute-start | bytes 1572872 | tf_op jit(solution)/shard_map/ppermute | solution.py:131
  56.2 0.0 copy-start.7
  56.2 0.9 copy-done.7
  57.2 0.1 shard_map.84.rows
  57.3 1.0 copy-done.4
  58.3 1.6 %copy-done.1 = bf16[1,1024,1024]{2,1,0:T(8,128)(2,1)S(1)} copy-done((bf16[1,1024,1024]{2,1,0:T(8,128)(2,1)S(1)}, bf16[1,1024,1024]{2,1,0:T(8,128)(2,1)}, u32[]{:S(2)}) %copy-start.1) | copy-done | bytes 2097176
  59.9 1.5 shard_map.85.own
  61.3 5.4 %collective-permute-done.3.left = bf16[256,1024]{1,0:T(8,128)(2,1)S(1)} collective-permute-done((bf16[256,1024]{1,0:T(8,128)(2,1)S(1)}, bf16[256,1024]{1,0:T(8,128)(2,1)S(1)}, u32[]{:S(2)}, u32[]{:S(2)}) %collective-permute-start.3) | collective-permute-done | bytes 524320 | tf_op jit(solution)/shard_map/ppermute | solution.py:131
  66.7 1.3 collective-permute-done.4.right
  68.0 3.5 %collective-permute-start.7 = (bf16[128,1024]{1,0:T(8,128)(2,1)S(1)}, bf16[128,1024]{1,0:T(8,128)(2,1)S(1)}, u32[]{:S(2)}, u32[]{:S(2)}) collective-permute-start(bf16[128,1024]{1,0:T(8,128)(2,1)S(1)} %slice.6), channel_id=1, source_target_pairs={{0,128},{128,256},{256,384},{384,0},{1,129},{129,257},{257,385},{3... | collective-permute-start | bytes 786440 | tf_op jit(solution)/shard_map/ppermute | solution.py:131
  71.6 0.0 copy-start.2
  71.6 3.5 %collective-permute-start.8 = (bf16[128,1024]{1,0:T(8,128)(2,1)S(1)}, bf16[128,1024]{1,0:T(8,128)(2,1)S(1)}, u32[]{:S(2)}, u32[]{:S(2)}) collective-permute-start(bf16[128,1024]{1,0:T(8,128)(2,1)S(1)} %slice.7), channel_id=1, source_target_pairs={{0,384},{128,0},{256,128},{384,256},{1,385},{129,1},{257,129},{385... | collective-permute-start | bytes 786440 | tf_op jit(solution)/shard_map/ppermute | solution.py:131
  75.1 4.9 %shard_map.86 = (bf16[256,1024]{1,0:T(8,128)(2,1)}, bf16[256,1024]{1,0:T(8,128)(2,1)}) custom-call(bf16[256,1024]{1,0:T(8,128)(2,1)S(1)} %collective-permute-done.3.left, bf16[256,1024]{1,0:T(8,128)(2,1)S(1)} %collective-permute-done.4.right, bf16[1,1024,1024]{2,1,0:T(8,128)(2,1)S(1)} %copy-done, bf16[1,1024,1024]{2,1,0:T(8,128)(2,1)} %weight_out.5), custom_call_target="tpu_custom_call" | custom-call | flops 2147483648 | bytes 6291456 | tf_op jit(solution)/shard_map/pallas_call | solution.py:117
  80.0 3.4 %collective-permute-start.5 = (bf16[256,1024]{1,0:T(8,128)(2,1)}, bf16[256,1024]{1,0:T(8,128)(2,1)S(1)}, u32[]{:S(2)}, u32[]{:S(2)}) collective-permute-start(bf16[256,1024]{1,0:T(8,128)(2,1)} %get-tuple-element.27), channel_id=1, source_target_pairs={{0,384},{128,0},{256,128},{384,256},{1,385},{129,1},{257,129},{385... | collective-permute-start | bytes 1572872 | tf_op jit(solution)/shard_map/ppermute | solution.py:131
  83.3 1.9 %collective-permute-start.6 = (bf16[256,1024]{1,0:T(8,128)(2,1)}, bf16[256,1024]{1,0:T(8,128)(2,1)}, u32[]{:S(2)}, u32[]{:S(2)}) collective-permute-start(bf16[256,1024]{1,0:T(8,128)(2,1)} %get-tuple-element.28), channel_id=1, source_target_pairs={{0,128},{128,256},{256,384},{384,0},{1,129},{129,257},{257,385},{3... | collective-permute-start | bytes 1572872 | tf_op jit(solution)/shard_map/ppermute | solution.py:131
  85.3 0.0 collective-permute-done.7.upper
  85.3 0.0 collective-permute-done.8.lower
  85.3 2.3 %shard_map.87 = bf16[256,1024]{1,0:T(8,128)(2,1)} custom-call(bf16[128,1024]{1,0:T(8,128)(2,1)S(1)} %collective-permute-done.7.upper, bf16[128,1024]{1,0:T(8,128)(2,1)S(1)} %collective-permute-done.8.lower, bf16[1,1024,1024]{2,1,0:T(8,128)(2,1)S(1)} %copy-done, bf16[1,1024,1024]{2,1,0:T(8,128)(2,1)S(1)} %copy-done.2), custom_call_target="tpu_custom_call" | custom-call | flops 1073741824 | bytes 5242880 | tf_op jit(solution)/shard_map/pallas_call | solution.py:117
  87.6 3.2 %collective-permute-start.9 = (bf16[256,1024]{1,0:T(8,128)(2,1)}, bf16[256,1024]{1,0:T(8,128)(2,1)S(1)}, u32[]{:S(2)}, u32[]{:S(2)}) collective-permute-start(bf16[256,1024]{1,0:T(8,128)(2,1)} %shard_map.87), channel_id=1, source_target_pairs={{0,256},{128,384},{256,0},{384,128},{1,257},{129,385},{257,1},{385... | collective-permute-start | bytes 1572872 | tf_op jit(solution)/shard_map/ppermute | solution.py:131
  90.7 14.1 %all-gather.2.cloned.1.call-done.pair = bf16[1024,2048]{1,0:T(8,128)(2,1)} async-done(((bf16[8,2048]{1,0:T(8,128)(2,1)}), bf16[1024,2048]{1,0:T(8,128)(2,1)}) %all-gather.2.cloned.1.call-update) | async-done | bytes 4194320 | tf_op jit(solution)/shard_map/all_gather | solution.py:151
  104.9 5.8 %shard_map.88 = (bf16[128,1024]{1,0:T(8,128)(2,1)}, bf16[128,1024]{1,0:T(8,128)(2,1)}, bf16[128,1024]{1,0:T(8,128)(2,1)}, bf16[128,1024]{1,0:T(8,128)(2,1)}) custom-call(bf16[512,1024]{1,0:T(8,128)(2,1)} %copy-done.4, bf16[1024,2048]{1,0:T(8,128)(2,1)} %all-gather.2.cloned.1.call-done.pair), custom_call_target="tpu_custom_call" | custom-call | flops 2147483648 | bytes 6291456 | tf_op jit(solution)/shard_map/pallas_call | solution.py:117
  110.7 0.0 collective-permute-done.5.left
  110.7 0.0 collective-permute-done.9.far
  110.7 2.1 %shard_map.89 = bf16[128,2,1024]{2,1,0:T(2,128)(2,1)} custom-call(bf16[256,1024]{1,0:T(8,128)(2,1)S(1)} %shard_map.85.own, bf16[256,1024]{1,0:T(8,128)(2,1)S(1)} %collective-permute-done.5.left, bf16[256,1024]{1,0:T(8,128)(2,1)} %collective-permute-done.6.right, bf16[256,1024]{1,0:T(8,128)(2,1)S(1)} %collective-permute-done.9.far), custom_call_target="tpu_custom_call" | custom-call | tf_op jit(solution)/shard_map/pallas_call | solution.py:190
  112.8 10.7 %all-to-all-start.1 = ((bf16[128,2,1024]{2,1,0:T(2,128)(2,1)}), bf16[128,2,1024]{2,1,0:T(2,128)(2,1)S(1)}, u32[]{:S(2)}, u32[]{:S(2)}) async-start(bf16[128,2,1024]{2,1,0:T(2,128)(2,1)} %shard_map.89), calls=%async_computation.1 | async-start | bytes 1048576 | tf_op jit(solution)/shard_map/all_to_all | solution.py:135
  123.5 3.5 %collective-permute-start.10 = (bf16[128,1024]{1,0:T(8,128)(2,1)}, bf16[128,1024]{1,0:T(8,128)(2,1)S(1)}, u32[]{:S(2)}, u32[]{:S(2)}) collective-permute-start(bf16[128,1024]{1,0:T(8,128)(2,1)} %get-tuple-element.36), channel_id=1, source_target_pairs={{0,256},{128,384},{256,0},{384,128},{1,257},{129,385},{257,1},{385... | collective-permute-start | bytes 786440 | tf_op jit(solution)/shard_map/ppermute | solution.py:131
  127.0 2.8 %collective-permute-start.11 = (bf16[128,1024]{1,0:T(8,128)(2,1)}, bf16[128,1024]{1,0:T(8,128)(2,1)S(1)}, u32[]{:S(2)}, u32[]{:S(2)}) collective-permute-start(bf16[128,1024]{1,0:T(8,128)(2,1)} %get-tuple-element.37), channel_id=1, source_target_pairs={{0,384},{128,0},{256,128},{384,256},{1,385},{129,1},{257,129},{385... | collective-permute-start | bytes 786440 | tf_op jit(solution)/shard_map/ppermute | solution.py:131
  129.8 2.5 %collective-permute-start.12 = (bf16[128,1024]{1,0:T(8,128)(2,1)}, bf16[128,1024]{1,0:T(8,128)(2,1)S(1)}, u32[]{:S(2)}, u32[]{:S(2)}) collective-permute-start(bf16[128,1024]{1,0:T(8,128)(2,1)} %get-tuple-element.38), channel_id=1, source_target_pairs={{0,128},{128,256},{256,384},{384,0},{1,129},{129,257},{257,385},{3... | collective-permute-start | bytes 786440 | tf_op jit(solution)/shard_map/ppermute | solution.py:131
  132.3 1.7 %collective-permute-done.10.far = bf16[128,1024]{1,0:T(8,128)(2,1)S(1)} collective-permute-done((bf16[128,1024]{1,0:T(8,128)(2,1)}, bf16[128,1024]{1,0:T(8,128)(2,1)S(1)}, u32[]{:S(2)}, u32[]{:S(2)}) %collective-permute-start.10) | collective-permute-done | bytes 262176 | tf_op jit(solution)/shard_map/ppermute | solution.py:131
  134.0 4.7 %collective-permute-done.11.left = bf16[128,1024]{1,0:T(8,128)(2,1)S(1)} collective-permute-done((bf16[128,1024]{1,0:T(8,128)(2,1)}, bf16[128,1024]{1,0:T(8,128)(2,1)S(1)}, u32[]{:S(2)}, u32[]{:S(2)}) %collective-permute-start.11) | collective-permute-done | bytes 262176 | tf_op jit(solution)/shard_map/ppermute | solution.py:131
  138.7 0.8 collective-permute-done.12.right
  139.4 0.2 shard_map.90.scaled
  139.7 4.4 %all-to-all-done.1.slots = bf16[128,2,1024]{2,1,0:T(2,128)(2,1)S(1)} async-done(((bf16[128,2,1024]{2,1,0:T(2,128)(2,1)}), bf16[128,2,1024]{2,1,0:T(2,128)(2,1)S(1)}, u32[]{:S(2)}, u32[]{:S(2)}) %all-to-all-start.1) | async-done | bytes 524320 | tf_op jit(solution)/shard_map/all_to_all | solution.py:135
  144.1 1.1 shard_map.91
  (21 shorter events, 0.1 us)
Async XLA Ops:
  6.5 49.7 %copy-start.3 = (bf16[128,1024]{1,0:T(8,128)(2,1)S(1)}, bf16[128,1024]{1,0:T(8,128)(2,1)}, u32[]{:S(2)}) copy-start(bf16[128,1024]{1,0:T(8,128)(2,1)} %tokens.3) | copy-start | bytes 786436
  6.5 98.3 %all-gather.2.cloned.1.call-start = ((), (), s32[]{:S(2)}) async-start(), calls=%async_computation.2 | async-start | bytes 4227072 | tf_op jit(solution)/shard_map/all_gather | solution.py:151
  10.1 48.1 %copy-start = (bf16[1,1024,1024]{2,1,0:T(8,128)(2,1)S(1)}, bf16[1,1024,1024]{2,1,0:T(8,128)(2,1)}, u32[]{:S(2)}) copy-start(bf16[1,1024,1024]{2,1,0:T(8,128)(2,1)} %weight_in.5) | copy-start | bytes 6291460
  10.1 39.5 %all-to-all-start = ((bf16[128,2,1024]{2,1,0:T(2,128)(2,1)}), bf16[128,2,1024]{2,1,0:T(2,128)(2,1)S(1)}, u32[]{:S(2)}, u32[]{:S(2)}) async-start(bf16[128,2,1024]{2,1,0:T(2,128)(2,1)} %shard_map.82), calls=%async_computation | async-start | bytes 1048576 | tf_op jit(solution)/shard_map/all_to_all | solution.py:135
  28.7 10.2 %collective-permute-start = (bf16[128,1024]{1,0:T(8,128)(2,1)}, bf16[128,1024]{1,0:T(8,128)(2,1)S(1)}, u32[]{:S(2)}, u32[]{:S(2)}) collective-permute-start(bf16[128,1024]{1,0:T(8,128)(2,1)} %tokens.3), channel_id=1, source_target_pairs={{0,128},{128,256},{256,384},{384,0},{1,129},{129,257},{257,385},{3... | collective-permute-start | bytes 786440 | tf_op jit(solution)/shard_map/ppermute | solution.py:131
  31.8 8.8 %collective-permute-start.1 = (bf16[128,1024]{1,0:T(8,128)(2,1)}, bf16[128,1024]{1,0:T(8,128)(2,1)S(1)}, u32[]{:S(2)}, u32[]{:S(2)}) collective-permute-start(bf16[128,1024]{1,0:T(8,128)(2,1)} %tokens.3), channel_id=1, source_target_pairs={{0,384},{128,0},{256,128},{384,256},{1,385},{129,1},{257,129},{385... | collective-permute-start | bytes 786440 | tf_op jit(solution)/shard_map/ppermute | solution.py:131
  35.2 10.0 %collective-permute-start.2 = (bf16[128,1024]{1,0:T(8,128)(2,1)}, bf16[128,1024]{1,0:T(8,128)(2,1)S(1)}, u32[]{:S(2)}, u32[]{:S(2)}) collective-permute-start(bf16[128,1024]{1,0:T(8,128)(2,1)} %tokens.3), channel_id=1, source_target_pairs={{0,256},{128,384},{256,0},{384,128},{1,257},{129,385},{257,1},{385... | collective-permute-start | bytes 786440 | tf_op jit(solution)/shard_map/ppermute | solution.py:131
  45.2 0.7 copy-start.6
  49.7 17.0 %collective-permute-start.3 = (bf16[256,1024]{1,0:T(8,128)(2,1)S(1)}, bf16[256,1024]{1,0:T(8,128)(2,1)S(1)}, u32[]{:S(2)}, u32[]{:S(2)}) collective-permute-start(bf16[256,1024]{1,0:T(8,128)(2,1)S(1)} %shard_map.83.rows), channel_id=1, source_target_pairs={{0,128},{128,256},{256,384},{384,0},{1,129},{129,257},{257,385},{3... | collective-permute-start | bytes 1572872 | tf_op jit(solution)/shard_map/ppermute | solution.py:131
  52.8 15.2 %collective-permute-start.4 = (bf16[256,1024]{1,0:T(8,128)(2,1)S(1)}, bf16[256,1024]{1,0:T(8,128)(2,1)S(1)}, u32[]{:S(2)}, u32[]{:S(2)}) collective-permute-start(bf16[256,1024]{1,0:T(8,128)(2,1)S(1)} %shard_map.83.rows), channel_id=1, source_target_pairs={{0,384},{128,0},{256,128},{384,256},{1,385},{129,1},{257,129},{385... | collective-permute-start | bytes 1572872 | tf_op jit(solution)/shard_map/ppermute | solution.py:131
  56.2 1.0 copy-start.7
  57.2 1.0 copy-start.4
  58.3 1.6 %copy-start.1 = (bf16[1,1024,1024]{2,1,0:T(8,128)(2,1)S(1)}, bf16[1,1024,1024]{2,1,0:T(8,128)(2,1)}, u32[]{:S(2)}) copy-start(bf16[1,1024,1024]{2,1,0:T(8,128)(2,1)} %weight_out.5) | copy-start | bytes 6291460
  68.0 17.2 %collective-permute-start.7 = (bf16[128,1024]{1,0:T(8,128)(2,1)S(1)}, bf16[128,1024]{1,0:T(8,128)(2,1)S(1)}, u32[]{:S(2)}, u32[]{:S(2)}) collective-permute-start(bf16[128,1024]{1,0:T(8,128)(2,1)S(1)} %slice.6), channel_id=1, source_target_pairs={{0,128},{128,256},{256,384},{384,0},{1,129},{129,257},{257,385},{3... | collective-permute-start | bytes 786440 | tf_op jit(solution)/shard_map/ppermute | solution.py:131
  71.6 13.7 %copy-start.2 = (bf16[1,1024,1024]{2,1,0:T(8,128)(2,1)S(1)}, bf16[1,1024,1024]{2,1,0:T(8,128)(2,1)}, u32[]{:S(2)}) copy-start(bf16[1,1024,1024]{2,1,0:T(8,128)(2,1)} %weight_out.5) | copy-start | bytes 6291460
  71.6 13.7 %collective-permute-start.8 = (bf16[128,1024]{1,0:T(8,128)(2,1)S(1)}, bf16[128,1024]{1,0:T(8,128)(2,1)S(1)}, u32[]{:S(2)}, u32[]{:S(2)}) collective-permute-start(bf16[128,1024]{1,0:T(8,128)(2,1)S(1)} %slice.7), channel_id=1, source_target_pairs={{0,384},{128,0},{256,128},{384,256},{1,385},{129,1},{257,129},{385... | collective-permute-start | bytes 786440 | tf_op jit(solution)/shard_map/ppermute | solution.py:131
  80.0 30.7 %collective-permute-start.5 = (bf16[256,1024]{1,0:T(8,128)(2,1)}, bf16[256,1024]{1,0:T(8,128)(2,1)S(1)}, u32[]{:S(2)}, u32[]{:S(2)}) collective-permute-start(bf16[256,1024]{1,0:T(8,128)(2,1)} %get-tuple-element.27), channel_id=1, source_target_pairs={{0,384},{128,0},{256,128},{384,256},{1,385},{129,1},{257,129},{385... | collective-permute-start | bytes 1572872 | tf_op jit(solution)/shard_map/ppermute | solution.py:131
  83.3 27.3 %collective-permute-start.6 = (bf16[256,1024]{1,0:T(8,128)(2,1)}, bf16[256,1024]{1,0:T(8,128)(2,1)}, u32[]{:S(2)}, u32[]{:S(2)}) collective-permute-start(bf16[256,1024]{1,0:T(8,128)(2,1)} %get-tuple-element.28), channel_id=1, source_target_pairs={{0,128},{128,256},{256,384},{384,0},{1,129},{129,257},{257,385},{3... | collective-permute-start | bytes 1572872 | tf_op jit(solution)/shard_map/ppermute | solution.py:131
  87.6 23.1 %collective-permute-start.9 = (bf16[256,1024]{1,0:T(8,128)(2,1)}, bf16[256,1024]{1,0:T(8,128)(2,1)S(1)}, u32[]{:S(2)}, u32[]{:S(2)}) collective-permute-start(bf16[256,1024]{1,0:T(8,128)(2,1)} %shard_map.87), channel_id=1, source_target_pairs={{0,256},{128,384},{256,0},{384,128},{1,257},{129,385},{257,1},{385... | collective-permute-start | bytes 1572872 | tf_op jit(solution)/shard_map/ppermute | solution.py:131
  110.7 21.6 %copy-start.10 = (bf16[1024]{0:T(1024)(128)(2,1)S(1)}, bf16[1024]{0:T(1024)(128)(2,1)}, u32[]{:S(2)}) copy-start(bf16[1024]{0:T(1024)(128)(2,1)} %param.11) | copy-start | bytes 6148
  110.7 28.8 %copy-start.5 = (bf16[128,1024]{1,0:T(8,128)(2,1)S(1)}, bf16[128,1024]{1,0:T(8,128)(2,1)}, u32[]{:S(2)}) copy-start(bf16[128,1024]{1,0:T(8,128)(2,1)} %get-tuple-element.39.own) | copy-start | bytes 786436
  110.7 28.8 %copy-start.9 = (f32[128]{0:T(128)S(1)}, f32[128]{0:T(128)}, u32[]{:S(2)}) copy-start(f32[128]{0:T(128)} %param.10) | copy-start | bytes 1540
  112.8 31.3 %copy-start.8 = (s32[128,1]{0,1:T(1,128)S(1)}, s32[128,1]{0,1:T(1,128)}, u32[]{:S(2)}) copy-start(s32[128,1]{0,1:T(1,128)} %param.9) | copy-start | bytes 1540
  112.8 31.3 %all-to-all-start.1 = ((bf16[128,2,1024]{2,1,0:T(2,128)(2,1)}), bf16[128,2,1024]{2,1,0:T(2,128)(2,1)S(1)}, u32[]{:S(2)}, u32[]{:S(2)}) async-start(bf16[128,2,1024]{2,1,0:T(2,128)(2,1)} %shard_map.89), calls=%async_computation.1 | async-start | bytes 1048576 | tf_op jit(solution)/shard_map/all_to_all | solution.py:135
  123.5 10.5 %collective-permute-start.10 = (bf16[128,1024]{1,0:T(8,128)(2,1)}, bf16[128,1024]{1,0:T(8,128)(2,1)S(1)}, u32[]{:S(2)}, u32[]{:S(2)}) collective-permute-start(bf16[128,1024]{1,0:T(8,128)(2,1)} %get-tuple-element.36), channel_id=1, source_target_pairs={{0,256},{128,384},{256,0},{384,128},{1,257},{129,385},{257,1},{385... | collective-permute-start | bytes 786440 | tf_op jit(solution)/shard_map/ppermute | solution.py:131
  127.0 11.7 %collective-permute-start.11 = (bf16[128,1024]{1,0:T(8,128)(2,1)}, bf16[128,1024]{1,0:T(8,128)(2,1)S(1)}, u32[]{:S(2)}, u32[]{:S(2)}) collective-permute-start(bf16[128,1024]{1,0:T(8,128)(2,1)} %get-tuple-element.37), channel_id=1, source_target_pairs={{0,384},{128,0},{256,128},{384,256},{1,385},{129,1},{257,129},{385... | collective-permute-start | bytes 786440 | tf_op jit(solution)/shard_map/ppermute | solution.py:131
  129.8 9.7 %collective-permute-start.12 = (bf16[128,1024]{1,0:T(8,128)(2,1)}, bf16[128,1024]{1,0:T(8,128)(2,1)S(1)}, u32[]{:S(2)}, u32[]{:S(2)}) collective-permute-start(bf16[128,1024]{1,0:T(8,128)(2,1)} %get-tuple-element.38), channel_id=1, source_target_pairs={{0,128},{128,256},{256,384},{384,0},{1,129},{129,257},{257,385},{3... | collective-permute-start | bytes 786440 | tf_op jit(solution)/shard_map/ppermute | solution.py:131
Sparse Core Ops, SparseCore 0:
  10.5 94.3 all-gather.1
